TPU v7x, 32 devices: a whole 2x2x4 slice. The times are simulated.
32 devices in a mesh: req: 8 (over z, x), kv: 4 (over y, core).
Axes of the slice: x: 2, y: 2, z: 4, core: 2. Of those that a mesh axis runs over, the one named last changes fastest.
Arguments:
- residual_in: bfloat16 [256, 4096], P(None, 'req'), may hold values from -6 to 6
- attn_gain: float32 [4096], replicated, may hold values from 0.1 to 1.9
- query_weight: bfloat16 [4096, 4096], P(None, 'kv'), may hold values from -0.09375 to 0.09375
- key_matrix: bfloat16 [4096, 1024], P(None, 'kv'), may hold values from -0.09375 to 0.09375
- value_matrix: bfloat16 [4096, 1024], P(None, 'kv'), may hold values from -0.09375 to 0.09375
- key_cache: bfloat16 [256, 8, 640, 128], P('req', 'kv'), may hold values from -400 to 400
- cached_values: bfloat16 [256, 8, 640, 128], P('req', 'kv'), may hold values from -6 to 6
- cache_lengths: int32 [256], P('req'), may hold values from 1 to 640, as said below
- positions: int32 [256], P('req'), may hold values from 640 to 16383
- output_weight: bfloat16 [4096, 4096], P(None, 'req'), may hold values from -0.09375 to 0.09375
- mlp_gain: float32 [4096], P('req'), may hold values from 0.1 to 1.9
- gate_weight: bfloat16 [4096, 14336], P('req', 'kv'), may hold values from -0.09375 to 0.09375
- up_weight: bfloat16 [4096, 14336], P('req', 'kv'), may hold values from -0.09375 to 0.09375
- down_weight: bfloat16 [14336, 4096], P('kv', 'req'), may hold values from -0.046875 to 0.046875
Outputs:
- output: bfloat16 [256, 4096], P('kv', 'req')
Inputs may be any that keep to these rules, and one draw needn't show every extreme that they name: `cache_lengths`: each request's filled slots; some request has exactly 640 and some exactly 1.
All inputs are finite; a program needn't handle non-finite values.
Results may differ from a plain program's by a relative error of at most 0.025.
Values may be sent and summed in bfloat16 or wider, within the bound.
No kernel may reach another device: no remote copies, remote signals or barrier semaphores. Data moves between devices by JAX's collectives and lax.ppermute only.
A program may use at most 128 MiB of HBM per device.

v0:
```python
import math

import jax
import jax.numpy as jnp
from jax import lax
from jax.sharding import PartitionSpec as P

MODEL_WIDTH = 4096
WINDOW = 512
SINKS = 4


EPS = 1e-05
THETA = 10000.0


def apply_rotary(vectors, places):
    half = vectors.shape[-1] // 2
    freqs = jnp.exp(
        jnp.arange(half, dtype=jnp.float32) * (-2.0 * math.log(THETA) / vectors.shape[-1])
    )
    angles = places.astype(jnp.float32)[:, None] * freqs[None, :]
    cosine = jnp.cos(angles)[:, None, :]
    sine = jnp.sin(angles)[:, None, :]
    first = vectors[..., :half]
    second = vectors[..., half:]
    return jnp.concatenate(
        [first * cosine - second * sine, second * cosine + first * sine], axis=-1
    )


def attend(query_rows, keys, values, new_key, new_value, allowed):
    factor = 1.0 / math.sqrt(query_rows.shape[-1])
    scores = (
        jnp.einsum("bgd,bjd->bgj", query_rows, keys, preferred_element_type=jnp.float32) * factor
    )
    scores = jnp.where(allowed[:, None, :], scores, -1e30)
    own = jnp.einsum("bgd,bd->bg", query_rows, new_key, preferred_element_type=jnp.float32) * factor
    peak = jnp.maximum(jnp.max(scores, axis=-1), own)
    expo = jnp.where(allowed[:, None, :], jnp.exp(scores - peak[..., None]), 0.0)
    own_expo = jnp.exp(own - peak)
    denom = jnp.sum(expo, axis=-1) + own_expo
    weights = (expo / denom[..., None]).astype(jnp.bfloat16)
    own_weight = (own_expo / denom).astype(jnp.bfloat16)
    mixed = jnp.einsum("bgj,bjd->bgd", weights, values, preferred_element_type=jnp.float32)
    mixed = (
        mixed
        + own_weight.astype(jnp.float32)[..., None] * new_value.astype(jnp.float32)[:, None, :]
    )
    return mixed.astype(jnp.bfloat16)


def shards(
    residual_in,
    attn_gain,
    query_weight,
    key_matrix,
    value_matrix,
    key_cache,
    cached_values,
    cache_lengths,
    positions,
    output_weight,
    mlp_gain,
    gate_weight,
    up_weight,
    down_weight,
):
    tokens = lax.all_to_all(residual_in, "req", split_axis=0, concat_axis=1, tiled=True)
    local_rows = tokens.shape[0]
    heads_here = key_cache.shape[1]
    head_size = key_cache.shape[3]
    query_group = query_weight.shape[1] // (heads_here * head_size)
    stream = tokens.astype(jnp.float32)
    normed_input = (
        stream
        / jnp.sqrt(jnp.sum(stream * stream, axis=-1, keepdims=True) / MODEL_WIDTH + EPS)
        * attn_gain
    ).astype(jnp.bfloat16)
    query_rows = jnp.dot(normed_input, query_weight, preferred_element_type=jnp.float32).reshape(
        local_rows, heads_here * query_group, head_size
    )
    query_rows = (
        apply_rotary(query_rows, positions)
        .astype(jnp.bfloat16)
        .reshape(local_rows, heads_here, query_group, head_size)
    )
    fresh_keys = jnp.dot(normed_input, key_matrix, preferred_element_type=jnp.float32).reshape(
        local_rows, heads_here, head_size
    )
    fresh_keys = apply_rotary(fresh_keys, positions).astype(jnp.bfloat16)
    fresh_values = (
        jnp.dot(normed_input, value_matrix, preferred_element_type=jnp.float32)
        .reshape(local_rows, heads_here, head_size)
        .astype(jnp.bfloat16)
    )
    slots = jnp.arange(key_cache.shape[2], dtype=jnp.int32)[None, :]
    limit = cache_lengths[:, None]
    allowed = (slots < limit) & ((slots < SINKS) | (slots > limit - WINDOW))
    results = []
    for head in range(heads_here):
        results.append(
            attend(
                query_rows[:, head],
                key_cache[:, head],
                cached_values[:, head],
                fresh_keys[:, head],
                fresh_values[:, head],
                allowed,
            )
        )
    attended_rows = jnp.stack(results, axis=1).reshape(
        local_rows, heads_here * query_group * head_size
    )
    features = attended_rows.shape[1]
    kv_place = lax.axis_index("kv")
    weight_rows = lax.dynamic_slice_in_dim(output_weight, kv_place * features, features, 0)
    partial_mix = jnp.dot(
        lax.all_gather(attended_rows, "req", axis=0, tiled=True),
        weight_rows,
        preferred_element_type=jnp.float32,
    )
    mixed = lax.psum(partial_mix.astype(jnp.bfloat16), "kv").astype(jnp.float32)
    middle = residual_in.astype(jnp.float32) + mixed
    scaled = (middle * mlp_gain).astype(jnp.bfloat16)
    squares = jnp.sum(middle * middle, axis=-1)
    gate_part = jnp.dot(scaled, gate_weight, preferred_element_type=jnp.float32)
    upper_part = jnp.dot(scaled, up_weight, preferred_element_type=jnp.float32)
    gate_total, upper_total, square_total = (
        lax.psum(gate_part.astype(jnp.bfloat16), "req").astype(jnp.float32),
        lax.psum(upper_part.astype(jnp.bfloat16), "req").astype(jnp.float32),
        lax.psum(squares.astype(jnp.bfloat16), "req").astype(jnp.float32),
    )
    inverse = (1.0 / jnp.sqrt(square_total / MODEL_WIDTH + EPS))[:, None]
    hidden = (jax.nn.silu(gate_total * inverse) * (upper_total * inverse)).astype(jnp.bfloat16)
    partial_out = jnp.dot(hidden, down_weight, preferred_element_type=jnp.float32)
    summed = lax.psum_scatter(
        partial_out.astype(jnp.bfloat16), "kv", scatter_dimension=0, tiled=True
    ).astype(jnp.float32)
    share = summed.shape[0]
    base_rows = lax.dynamic_slice_in_dim(middle, kv_place * share, share, 0)
    return (base_rows + summed).astype(jnp.bfloat16)


def solution(mesh):
    return jax.shard_map(
        shards,
        mesh=mesh,
        in_specs=(
            P(None, "req"),
            P(),
            P(None, "kv"),
            P(None, "kv"),
            P(None, "kv"),
            P("req", "kv", None, None),
            P("req", "kv", None, None),
            P("req"),
            P("req"),
            P(None, "req"),
            P("req"),
            P("req", "kv"),
            P("req", "kv"),
            P("kv", "req"),
        ),
        out_specs=P("kv", "req"),
        check_vma=False,
    )
```

profile of v0, /device:TPU:0, one launch (start us, length us, event | category | flops | bytes accessed | tf_op | source)
XLA Modules:
  0.0 304.8 jit_solution(17425931877830689585)
XLA Ops:
  6.5 7.3 %all-to-all-start = ((bf16[8,32,512]{2,1,0:T(8,128)(2,1)}), bf16[8,32,512]{2,1,0:T(8,128)(2,1)S(1)}, u32[]{:S(2)}, u32[]{:S(2)}) async-start(bf16[8,32,512]{2,1,0:T(8,128)(2,1)} %bitcast.101), calls=%async_computation | async-start | bytes 524288 | tf_op jit(solution)/shard_map/all_to_all | solution.py:69
  13.8 0.0 all-reduce.4.cloned.1.call-start
  13.8 0.7 broadcast_add_fusion
  14.5 0.7 mul.197
  15.2 11.9 %copy.40 = bf16[1024,4096]{1,0:T(8,128)(2,1)} copy(bf16[1024,4096]{0,1:T(8,128)(2,1)} %bitcast.98) | data formatting | bytes 16777216 | tf_op jit(solution)/shard_map/dot_general | solution.py:80
  27.2 0.0 copy-start.6
  27.2 3.0 copy.41
  30.2 2.9 copy.42
  33.1 0.1 fusion.59
  33.2 0.1 multiply_cosine_fusion
  33.3 0.0 all-to-all-done
  33.4 0.2 fusion.45
  33.5 0.1 fusion.48
  33.7 0.2 copy.25
  33.8 0.1 reshape.171
  34.0 0.0 slice-start
  34.0 6.1 %fusion.83 = f32[32,8,128]{2,0,1:T(8,128)S(1)} fusion(bf16[32,4096,1]{1,0,2:T(8,128)(2,1)S(1)} %reshape.171, bf16[8,128,4096]{2,1,0:T(8,128)(2,1)} %bitcast.97), kind=kOutput, calls=%fused_computation.106 | convolution fusion | flops 268435456 | bytes 8781824 | tf_op jit(solution)/shard_map/dot_general | solution.py:80
  40.1 0.0 slice-start.1
  40.1 0.1 subtract_convert_fusion
  40.3 0.7 fusion.84
  41.1 0.1 add_convert_fusion.2
  41.2 0.1 fusion.62
  41.3 0.1 fusion.73
  41.4 0.1 fusion.64
  41.5 4.3 %fusion.82 = (f32[32,4]{1,0:T(8,128)S(1)}, f32[32,4,640]{2,1,0:T(4,128)S(1)}) fusion(bf16[32,4,128]{2,1,0:T(4,128)(2,1)S(1)} %get-tuple-element.14, bf16[32,2,640,128]{3,2,1,0:T(8,128)(2,1)} %param.19, pred[32,640]{1,0:T(8,128)(4,1)S(1)} %fusion.59), kind=kOutput, calls=%fused_computation.105 | convolution fusion | flops 21217152 | bytes 5624320 | tf_op jit(solution)/shard_map/bgd,bjd->bgj/dot_general | solution.py:35
  45.8 4.5 %fusion.81 = (f32[32,4]{1,0:T(8,128)S(1)}, f32[32,4,640]{2,1,0:T(4,128)S(1)}) fusion(bf16[32,4,128]{2,1,0:T(4,128)(2,1)S(1)} %get-tuple-element.13, bf16[32,2,640,128]{3,2,1,0:T(8,128)(2,1)} %param.19, pred[32,640]{1,0:T(8,128)(4,1)S(1)} %fusion.59), kind=kOutput, calls=%fused_computation.104 | convolution fusion | flops 21217152 | bytes 5624320 | tf_op jit(solution)/shard_map/bgd,bjd->bgj/dot_general | solution.py:35
  50.3 0.2 fusion.66
  50.4 0.7 convolution_convert_fusion.3
  51.2 0.5 fusion.49
  51.9 1.0 fusion.32
  52.9 1.0 fusion.35
  53.9 0.1 pad_maximum_fusion
  54.0 31.9 %all_gather.3 = bf16[256,1024]{1,0:T(8,128)(2,1)S(1)} all-gather(bf16[32,1024]{1,0:T(8,128)(2,1)S(1)} %reshape.168), channel_id=1, replica_groups=mesh['req'=8,'kv'=4] {'req'}, dimensions={0}, use_global_device_ids=true | all-gather | bytes 589824 | tf_op jit(solution)/shard_map/all_gather | solution.py:119
  85.9 2.4 convolution_convert_fusion.2
  88.3 0.0 all-reduce.4.cloned.1.call-update
  88.3 0.2 all-reduce.6.cloned.1.call-start
  88.6 32.7 %all-reduce.4.cloned.1.call-done = bf16[256,512]{1,0:T(8,128)(2,1)} async-done(((bf16[256,512]{1,0:T(8,128)(2,1)}), bf16[256,512]{1,0:T(8,128)(2,1)}) %all-reduce.4.cloned.1.call-update) | async-done | bytes 262160 | tf_op jit(solution)/shard_map/psum | solution.py:123
  121.3 4.7 %convolution_convert_fusion = bf16[256,3584]{1,0:T(8,128)(2,1)} fusion(bf16[512,3584]{1,0:T(8,128)(2,1)} %param.26, f32[512]{0:T(512)S(1)} %copy-done.5, bf16[256,512]{1,0:T(8,128)(2,1)} %all-reduce.4.cloned.1.call-done, bf16[256,512]{1,0:T(8,128)(2,1)S(1)} %copy-done.1), kind=kOutput, calls=%fused_computation.12 | convolution fusion | flops 941096960 | bytes 6031360 | tf_op jit(solution)/shard_map/dot_general | solution.py:128
  126.0 2.4 convolution_convert_fusion.1
  128.3 0.0 all-reduce.6.cloned.1.call-update
  128.4 0.0 reduce-scatter.2.cloned.1.call-start
  128.4 0.2 convert_add_fusion
  128.6 22.1 %psum.30 = bf16[256]{0:T(256)(128)(2,1)S(1)} all-reduce(bf16[256]{0:T(256)(128)(2,1)S(1)} %get-tuple-element.10), channel_id=1, replica_groups=mesh['req'=8,'kv'=4] {'req'}, use_global_device_ids=true, to_apply=%region_8.9 | all-reduce | flops 256 | bytes 1024 | tf_op jit(solution)/shard_map/psum | solution.py:132
  150.7 121.5 %all-reduce.6.cloned.1.call-done = (bf16[256,3584]{1,0:T(8,128)(2,1)}, bf16[256,3584]{1,0:T(8,128)(2,1)}) async-done(((bf16[256,3584]{1,0:T(8,128)(2,1)}, bf16[256,3584]{1,0:T(8,128)(2,1)}), (bf16[256,3584]{1,0:T(8,128)(2,1)}, bf16[256,3584]{1,0:T(8,128)(2,1)})) %all-reduce.6.cloned.1.call-update) | async-done | bytes 3670032 | tf_op jit(solution)/shard_map/psum | solution.py:131
  272.2 5.3 %fusion.13 = bf16[256,512]{1,0:T(8,128)(2,1)} fusion(bf16[3584,512]{1,0:T(8,128)(2,1)} %param.27, bf16[256,3584]{1,0:T(8,128)(2,1)} %get-tuple-element.7, bf16[256,3584]{1,0:T(8,128)(2,1)} %get-tuple-element.8, f32[256]{0:T(256)S(1)} %add_rsqrt_fusion), kind=kOutput, calls=%fused_computation.17 | convolution fusion | flops 948830208 | bytes 7603200 | tf_op jit(solution)/shard_map/dot_general | solution.py:136
  277.5 0.0 reduce-scatter.2.cloned.1.call-update
  277.6 19.2 %reduce-scatter.2.cloned.1.call-done = bf16[64,512]{1,0:T(8,128)(2,1)} async-done(((bf16[256,512]{1,0:T(8,128)(2,1)}), bf16[64,512]{1,0:T(8,128)(2,1)}) %reduce-scatter.2.cloned.1.call-update) | async-done | bytes 65552 | tf_op jit(solution)/shard_map/reduce_scatter | solution.py:137
  296.8 1.5 add_convert_fusion
  (33 shorter events, 0.3 us)
Async XLA Ops:
  6.5 26.8 %all-to-all-start = ((bf16[8,32,512]{2,1,0:T(8,128)(2,1)}), bf16[8,32,512]{2,1,0:T(8,128)(2,1)S(1)}, u32[]{:S(2)}, u32[]{:S(2)}) async-start(bf16[8,32,512]{2,1,0:T(8,128)(2,1)} %bitcast.101), calls=%async_computation | async-start | bytes 524288 | tf_op jit(solution)/shard_map/all_to_all | solution.py:69
  13.8 107.5 %all-reduce.4.cloned.1.call-start = ((), (), s32[]{:S(2)}) async-start(), calls=%async_computation.2 | async-start | bytes 524288 | tf_op jit(solution)/shard_map/psum | solution.py:123
  15.2 12.0 %copy-start.7 = (s32[32]{0:T(128)S(1)}, s32[32]{0:T(128)}, u32[]{:S(2)}) copy-start(s32[32]{0:T(128)} %param.22) | copy-start | bytes 388
  15.2 12.0 %copy-start.4 = (bf16[4096,256]{1,0:T(8,128)(2,1)S(1)}, bf16[4096,256]{1,0:T(8,128)(2,1)}, u32[]{:S(2)}) copy-start(bf16[4096,256]{1,0:T(8,128)(2,1)} %param.17) | copy-start | bytes 6291460
  27.2 5.9 %copy-start.6 = (s32[32]{0:T(128)S(1)}, s32[32]{0:T(128)}, u32[]{:S(2)}) copy-start(s32[32]{0:T(128)} %param.21) | copy-start | bytes 388
  34.0 6.3 %copy-start = (bf16[256,4096]{1,0:T(8,128)(2,1)S(1)}, bf16[256,4096]{1,0:T(8,128)(2,1)}, u32[]{:S(2)}) copy-start(bf16[256,4096]{1,0:T(8,128)(2,1)} %copy.41) | copy-start | bytes 6291460
  34.0 17.8 %slice-start = ((s8[10485760]{0:T(1024)(128)(4,1)}), s8[2097152]{0:T(1024)(128)(4,1)S(1)}, s32[]{:S(2)}) async-start(s8[10485760]{0:T(1024)(128)(4,1)} %bitcast.110), calls=%async_computation.5 | async-start | bytes 4194304
  40.1 11.7 %slice-start.1 = ((s8[10485760]{0:T(1024)(128)(4,1)}), s8[4194304]{0:T(1024)(128)(4,1)S(1)}, s32[]{:S(2)}) async-start(s8[10485760]{0:T(1024)(128)(4,1)} %bitcast.110), calls=%async_computation.6 | async-start | bytes 8388608
  45.8 6.0 %slice-start.2 = ((s8[10485760]{0:T(1024)(128)(4,1)}), s8[4194304]{0:T(1024)(128)(4,1)S(1)}, s32[]{:S(2)}) async-start(s8[10485760]{0:T(1024)(128)(4,1)} %bitcast.110), calls=%async_computation.7 | async-start | bytes 8388608
  52.9 68.4 %copy-start.1 = (bf16[256,512]{1,0:T(8,128)(2,1)S(1)}, bf16[256,512]{1,0:T(8,128)(2,1)}, u32[]{:S(2)}) copy-start(bf16[256,512]{1,0:T(8,128)(2,1)} %param.14) | copy-start | bytes 786436
  52.9 68.4 %copy-start.5 = (f32[512]{0:T(512)S(1)}, f32[512]{0:T(512)}, u32[]{:S(2)}) copy-start(f32[512]{0:T(512)} %param.24) | copy-start | bytes 6148
  88.3 183.9 %all-reduce.6.cloned.1.call-start = ((), (), s32[]{:S(2)}) async-start(), calls=%async_computation.4 | async-start | bytes 7340032 | tf_op jit(solution)/shard_map/psum | solution.py:131
  121.3 4.7 %copy-start.2 = (bf16[512,3584]{1,0:T(8,128)(2,1)S(1)}, bf16[512,3584]{1,0:T(8,128)(2,1)}, u32[]{:S(2)}) copy-start(bf16[512,3584]{1,0:T(8,128)(2,1)} %param.25) | copy-start | bytes 11010052
  121.3 4.7 %copy-start.3 = (bf16[256,512]{1,0:T(8,128)(2,1)S(1)}, bf16[256,512]{1,0:T(8,128)(2,1)}, u32[]{:S(2)}) copy-start(bf16[256,512]{1,0:T(8,128)(2,1)} %all-reduce.4.cloned.1.call-done) | copy-start | bytes 786436
  128.4 168.4 %reduce-scatter.2.cloned.1.call-start = ((), (), s32[]{:S(2)}) async-start(), calls=%async_computation.3 | async-start | bytes 327680 | tf_op jit(solution)/shard_map/reduce_scatter | solution.py:137
Sparse Core Ops, SparseCore 0:
  88.4 32.7 all-reduce.3
  128.5 143.6 all-reduce.5
  277.7 19.0 reduce-scatter.1
where the time goes:
time: 305 us
  waiting for transfers between devices  173 us (57%)
  blocking collectives  54 us (18%)
  matrix products  33.4 us (11%)
  local copies, waits for them, and re-layouts  19 us (6%)
  between operations  13.4 us (4%)
  starting transfers between devices  7.55 us (2%)
  other arithmetic  3.94 us (1%)
    psum x1, waiting for transfers between devices, shards(): lax.psum(upper_part.astype(jnp.bfloat16), 'req').astype(jnp.float32)  122 us
    psum x1, waiting for transfers between devices, shards(): mixed = lax.psum(partial_mix.astype(jnp.bfloat16), 'kv').astype(jnp.float32)  32.7 us
    all_gather x1, blocking collectives, shards(): lax.all_gather(attended_rows, 'req', axis=0, tiled=True)  31.9 us
    psum x1, blocking collectives, shards(): lax.psum(squares.astype(jnp.bfloat16), 'req').astype(jnp.float32)  22.1 us
    reduce_scatter x1, waiting for transfers between devices, shards(): lax.psum_scatter(partial_out.astype(jnp.bfloat16), 'kv', scatter_dimensio...  19.2 us
    dot_general x1, local copies, waits for them, and re-layouts, shards(): jnp.dot(normed_input, query_weight, preferred_element_type=jnp.float32)  11.9 us
    dot_general x2, matrix products, attend(): jnp.einsum('bgd,bjd->bgj', query_rows, keys, preferred_element_type=jnp.f...  8.77 us
    all_to_all x1, starting transfers between devices, shards(): lax.all_to_all(residual_in, 'req', split_axis=0, concat_axis=1, tiled=True)  7.25 us
  transfers between devices with their start and end apart: 4, of which 3 were waited for; matrix products, arithmetic and copies ran while one was open for 6% of the time, Pallas kernels for 0%

commit v1 on v0

v1 whole, which is shorter than its diff:
```python
import math

import jax
import jax.numpy as jnp
from jax import lax
from jax.sharding import PartitionSpec as P

MODEL_WIDTH = 4096
WINDOW = 512
SINKS = 4


EPS = 1e-05
THETA = 10000.0


def rotary_tables(places, head_size):
    half = head_size // 2
    freqs = jnp.exp(jnp.arange(half, dtype=jnp.float32) * (-2.0 * math.log(THETA) / head_size))
    angles = places.astype(jnp.float32)[:, None] * freqs[None, :]
    return jnp.cos(angles), jnp.sin(angles)


def rotate(flat, cosine, sine, head_size):
    half = head_size // 2
    heads = []
    for start in range(0, flat.shape[1], head_size):
        first = flat[:, start : start + half]
        second = flat[:, start + half : start + head_size]
        heads.append(first * cosine - second * sine)
        heads.append(second * cosine + first * sine)
    return jnp.concatenate(heads, axis=1).astype(jnp.bfloat16)


def attend(query_rows, keys, values, new_key, new_value, allowed):
    factor = 1.0 / math.sqrt(query_rows.shape[-1])
    scores = (
        jnp.einsum("bgd,bjd->bgj", query_rows, keys, preferred_element_type=jnp.float32) * factor
    )
    scores = jnp.where(allowed[:, None, :], scores, -1e30)
    own = jnp.einsum("bgd,bd->bg", query_rows, new_key, preferred_element_type=jnp.float32) * factor
    peak = jnp.maximum(jnp.max(scores, axis=-1), own)
    expo = jnp.where(allowed[:, None, :], jnp.exp(scores - peak[..., None]), 0.0)
    own_expo = jnp.exp(own - peak)
    denom = jnp.sum(expo, axis=-1) + own_expo
    weights = (expo / denom[..., None]).astype(jnp.bfloat16)
    own_weight = (own_expo / denom).astype(jnp.bfloat16)
    mixed = jnp.einsum("bgj,bjd->bgd", weights, values, preferred_element_type=jnp.float32)
    mixed = (
        mixed
        + own_weight.astype(jnp.float32)[..., None] * new_value.astype(jnp.float32)[:, None, :]
    )
    return mixed.astype(jnp.bfloat16)


def bit_reverse(value, bits):
    result = 0
    for bit in range(bits):
        result |= ((value >> bit) & 1) << (bits - 1 - bit)
    return result


def exchange(value, size, bit):
    return lax.ppermute(value, "req", [(i, i ^ (1 << bit)) for i in range(size)])


def local_order(value, place, size):
    bits = size.bit_length() - 1
    rows = value.shape[0] // size
    return jnp.concatenate(
        [
            lax.dynamic_slice_in_dim(value, (place ^ bit_reverse(i, bits)) * rows, rows, 0)
            for i in range(size)
        ],
        axis=0,
    )


def natural_order(value, place, size):
    bits = size.bit_length() - 1
    rows = value.shape[0] // size
    pieces = []
    for block in range(size):
        other = place ^ block
        spot = jnp.int32(0)
        for bit in range(bits):
            spot = spot | (((other >> bit) & 1) << (bits - 1 - bit))
        pieces.append(lax.dynamic_slice_in_dim(value, spot * rows, rows, 0))
    return jnp.concatenate(pieces, axis=0)


def gather_rows(value, size):
    for bit in reversed(range(size.bit_length() - 1)):
        value = jnp.concatenate([value, exchange(value, size, bit)], axis=0)
    return value


def scatter_sum(value, size):
    for bit in range(size.bit_length() - 1):
        half = value.shape[0] // 2
        other = exchange(value[half:], size, bit)
        value = (value[:half].astype(jnp.float32) + other.astype(jnp.float32)).astype(jnp.bfloat16)
    return value


def chunks_of(columns):
    tiles = columns // 128
    for count in (4, 2, 1):
        if tiles % count == 0:
            return count
    return 1


def shards(
    residual_in,
    attn_gain,
    query_weight,
    key_matrix,
    value_matrix,
    key_cache,
    cached_values,
    cache_lengths,
    positions,
    output_weight,
    mlp_gain,
    gate_weight,
    up_weight,
    down_weight,
):
    req_size = lax.axis_size("req")
    kv_size = lax.axis_size("kv")
    req_place = lax.axis_index("req")
    kv_place = lax.axis_index("kv")
    tokens = lax.all_to_all(residual_in, "req", split_axis=0, concat_axis=1, tiled=True)
    local_rows = tokens.shape[0]
    heads_here = key_cache.shape[1]
    head_size = key_cache.shape[3]
    query_group = query_weight.shape[1] // (heads_here * head_size)
    stream = tokens.astype(jnp.float32)
    normed_input = (
        stream
        / jnp.sqrt(jnp.sum(stream * stream, axis=-1, keepdims=True) / MODEL_WIDTH + EPS)
        * attn_gain
    ).astype(jnp.bfloat16)
    cosine, sine = rotary_tables(positions, head_size)
    query_rows, fresh_keys, fresh_values = lax.optimization_barrier(
        (
            jnp.dot(normed_input, query_weight, preferred_element_type=jnp.float32),
            jnp.dot(normed_input, key_matrix, preferred_element_type=jnp.float32),
            jnp.dot(normed_input, value_matrix, preferred_element_type=jnp.float32),
        )
    )
    query_rows = rotate(query_rows, cosine, sine, head_size).reshape(
        local_rows, heads_here, query_group, head_size
    )
    fresh_keys = rotate(fresh_keys, cosine, sine, head_size).reshape(
        local_rows, heads_here, head_size
    )
    fresh_values = fresh_values.astype(jnp.bfloat16).reshape(local_rows, heads_here, head_size)
    slots = jnp.arange(key_cache.shape[2], dtype=jnp.int32)[None, :]
    limit = cache_lengths[:, None]
    allowed = (slots < limit) & ((slots < SINKS) | (slots > limit - WINDOW))
    results = []
    for head in range(heads_here):
        results.append(
            attend(
                query_rows[:, head],
                key_cache[:, head],
                cached_values[:, head],
                fresh_keys[:, head],
                fresh_values[:, head],
                allowed,
            )
        )
    attended_rows = jnp.stack(results, axis=1).reshape(
        local_rows, heads_here * query_group * head_size
    )
    features = attended_rows.shape[1]
    weight_rows = lax.dynamic_slice_in_dim(output_weight, kv_place * features, features, 0)
    residual_rows = local_order(residual_in, req_place, req_size).astype(jnp.float32)
    partial_mix = jnp.dot(
        gather_rows(attended_rows, req_size),
        weight_rows,
        preferred_element_type=jnp.float32,
    ).astype(jnp.bfloat16)
    total_rows = partial_mix.shape[0]
    pieces = lax.all_to_all(
        partial_mix.reshape(kv_size, total_rows // kv_size, -1), "kv", split_axis=0, concat_axis=0
    )
    mixed_share = jnp.sum(pieces.astype(jnp.float32), axis=0).astype(jnp.bfloat16)
    mixed = lax.all_gather(mixed_share, "kv", axis=0, tiled=True)
    middle = residual_rows + mixed.astype(jnp.float32)
    scaled = (middle * mlp_gain).astype(jnp.bfloat16)
    squares = jnp.sum(middle * middle, axis=-1, keepdims=True)
    count = chunks_of(gate_weight.shape[1])
    width = gate_weight.shape[1] // count
    inverse = None
    partial_out = None
    sums = []
    for chunk in range(count):
        columns = slice(chunk * width, (chunk + 1) * width)
        parts = [
            jnp.dot(scaled, gate_weight[:, columns], preferred_element_type=jnp.float32),
            jnp.dot(scaled, up_weight[:, columns], preferred_element_type=jnp.float32),
        ]
        if chunk == 0:
            parts.append(jnp.broadcast_to(squares, (total_rows, 128)))
        sums.append(scatter_sum(jnp.concatenate(parts, axis=1).astype(jnp.bfloat16), req_size))
    for chunk in range(count):
        total = sums[chunk].astype(jnp.float32)
        if chunk == 0:
            inverse = 1.0 / jnp.sqrt(total[:, 2 * width : 2 * width + 1] / MODEL_WIDTH + EPS)
        hidden = (
            jax.nn.silu(total[:, :width] * inverse) * (total[:, width : 2 * width] * inverse)
        ).astype(jnp.bfloat16)
        product = jnp.dot(
            gather_rows(hidden, req_size),
            down_weight[chunk * width : (chunk + 1) * width],
            preferred_element_type=jnp.float32,
        )
        partial_out = product if partial_out is None else partial_out + product
    ordered = natural_order(partial_out.astype(jnp.bfloat16), req_place, req_size)
    pieces = lax.all_to_all(
        ordered.reshape(kv_size, total_rows // kv_size, -1), "kv", split_axis=0, concat_axis=0
    )
    share = total_rows // kv_size
    base_rows = lax.dynamic_slice_in_dim(
        natural_order(middle, req_place, req_size), kv_place * share, share, 0
    )
    return (base_rows + jnp.sum(pieces.astype(jnp.float32), axis=0)).astype(jnp.bfloat16)


def solution(mesh):
    return jax.shard_map(
        shards,
        mesh=mesh,
        in_specs=(
            P(None, "req"),
            P(),
            P(None, "kv"),
            P(None, "kv"),
            P(None, "kv"),
            P("req", "kv", None, None),
            P("req", "kv", None, None),
            P("req"),
            P("req"),
            P(None, "req"),
            P("req"),
            P("req", "kv"),
            P("req", "kv"),
            P("kv", "req"),
        ),
        out_specs=P("kv", "req"),
        check_vma=False,
    )
```

time: 305 us -> 206 us (0.68)
  waiting for transfers between devices: 173 us -> 114 us
  blocking collectives: 54 us -> 6.1 us
  starting transfers between devices: 7.55 us -> 40.4 us
  local copies, waits for them, and re-layouts: 19 us -> 5.64 us
  between operations: 13.4 us -> 0.71 us
    psum x2 -> x0, waiting for transfers between devices: 154 us -> none  [the longest x1 122 us: shards(): lax.psum(upper_part.astype(jnp.bfloat16), 'req').astype(jnp.float32)]
    ppermute x0 -> x27, waiting for transfers between devices: none -> 95.3 us  [exchange(): return lax.ppermute(value, 'req', [(i, i ^ 1 << bit) for i in range(size)])]
    ppermute x0 -> x27, starting transfers between devices: none -> 26.2 us  [exchange(): return lax.ppermute(value, 'req', [(i, i ^ 1 << bit) for i in range(size)])]
    all_gather x1, blocking collectives: 31.9 us -> 6.1 us  [shards(): mixed = lax.all_gather(mixed_share, 'kv', axis=0, tiled=True)]
    psum x1 -> x0, blocking collectives: 22.1 us -> none  [shards(): lax.psum(squares.astype(jnp.bfloat16), 'req').astype(jnp.float32)]
    reduce_scatter x1 -> x0, waiting for transfers between devices: 19.2 us -> none  [shards(): lax.psum_scatter(partial_out.astype(jnp.bfloat16), 'kv', scatter_dimensio...]
    dot_general x3 -> x0, local copies, waits for them, and re-layouts: 17.8 us -> none  [the longest x1 11.9 us: shards(): jnp.dot(normed_input, query_weight, preferred_element_type=jnp.float32)]
    all_to_all x0 -> x2, waiting for transfers between devices: none -> 11.9 us  [the longest x1 5.96 us: shards(): lax.all_to_all(partial_mix.reshape(kv_size, total_rows // kv_size, -1), '...]
  transfers between devices with their start and end apart: 4 -> 30, of which waited for: 3 -> 24; matrix products, arithmetic and copies ran while one was open for 6% -> 2% of each run, Pallas kernels for 0% -> 0%
where the time goes in v1:
time: 206 us; the launch traced here: 205 us
  waiting for transfers between devices  114 us (55%)
  starting transfers between devices  40.4 us (20%)
  matrix products  32.3 us (16%)
  blocking collectives  6.1 us (3%)
  other arithmetic  5.9 us (3%)
  local copies, waits for them, and re-layouts  5.64 us (3%)
    ppermute x27, waiting for transfers between devices, exchange(): return lax.ppermute(value, 'req', [(i, i ^ 1 << bit) for i in range(size)])  95.3 us
    ppermute x27, starting transfers between devices, exchange(): return lax.ppermute(value, 'req', [(i, i ^ 1 << bit) for i in range(size)])  26.2 us
    dot_general x2, matrix products, attend(): jnp.einsum('bgd,bjd->bgj', query_rows, keys, preferred_element_type=jnp.f...  8.61 us
    all_to_all x1, starting transfers between devices, shards(): lax.all_to_all(residual_in, 'req', split_axis=0, concat_axis=1, tiled=True)  7.38 us
    dot_general x2, matrix products, attend(): jnp.einsum('bgj,bjd->bgd', weights, values, preferred_element_type=jnp.fl...  7.03 us
    all_to_all x1, waiting for transfers between devices, shards(): lax.all_to_all(residual_in, 'req', split_axis=0, concat_axis=1, tiled=True)  6.82 us
    all_gather x1, blocking collectives, shards(): mixed = lax.all_gather(mixed_share, 'kv', axis=0, tiled=True)  6.1 us
    all_to_all x1, waiting for transfers between devices, shards(): lax.all_to_all(partial_mix.reshape(kv_size, total_rows // kv_size, -1), '...  5.96 us
  transfers between devices with their start and end apart: 30, of which 24 were waited for; matrix products, arithmetic and copies ran while one was open for 2% of the time, Pallas kernels for 0%

profile of v1, /device:TPU:0, one launch (start us, length us, event | category | flops | bytes accessed | tf_op | source)
XLA Modules:
  0.0 205.0 jit_solution(10614848120679569710)
XLA Ops:
  0.0 7.4 %all-to-all-start = ((bf16[8,32,512]{2,1,0:T(8,128)(2,1)}), bf16[8,32,512]{2,1,0:T(8,128)(2,1)S(1)}, u32[]{:S(2)}, u32[]{:S(2)}) async-start(bf16[8,32,512]{2,1,0:T(8,128)(2,1)} %bitcast.97), calls=%async_computation | async-start | bytes 524288 | tf_op jit(solution)/shard_map/all_to_all | solution.py:134
  9.5 6.8 %all-to-all-done = bf16[8,32,512]{2,1,0:T(8,128)(2,1)S(1)} async-done(((bf16[8,32,512]{2,1,0:T(8,128)(2,1)}), bf16[8,32,512]{2,1,0:T(8,128)(2,1)S(1)}, u32[]{:S(2)}, u32[]{:S(2)}) %all-to-all-start) | async-done | bytes 262176 | tf_op jit(solution)/shard_map/all_to_all | solution.py:134
  16.6 5.2 %fusion.225 = f32[32,1024]{1,0:T(8,128)S(1)} fusion(bf16[4096,1024]{1,0:T(8,128)(2,1)} %param.16, f32[32,4096]{1,0:T(8,128)S(1)} %bitcast.94, f32[4096]{0:T(1024)} %param.15, f32[32]{0:T(128)S(1)} %add_sqrt_fusion), kind=kOutput, calls=%fused_computation.314 | convolution fusion | flops 268828672 | bytes 9060480 | tf_op jit(solution)/shard_map/dot_general | solution.py:148
  23.3 4.3 %fusion.228 = (f32[32,4]{1,0:T(8,128)S(1)}, f32[32,4,640]{2,1,0:T(4,128)S(1)}) fusion(bf16[32,2,640,128]{3,2,1,0:T(8,128)(2,1)} %param.19, bf16[32,2,4,128]{3,2,1,0:T(4,128)(2,1)S(1)} %convert_element_type.226, pred[32,640]{1,0:T(8,128)(4,1)S(1)} %fusion.122), kind=kOutput, calls=%fused_computation.317 | convolution fusion | flops 21217152 | bytes 5624320 | tf_op jit(solution)/shard_map/bgd,bjd->bgj/dot_general | solution.py:38
  27.6 4.3 %fusion.227 = (f32[32,4]{1,0:T(8,128)S(1)}, f32[32,4,640]{2,1,0:T(4,128)S(1)}) fusion(bf16[32,2,640,128]{3,2,1,0:T(8,128)(2,1)} %param.19, bf16[32,2,4,128]{3,2,1,0:T(4,128)(2,1)S(1)} %convert_element_type.226, pred[32,640]{1,0:T(8,128)(4,1)S(1)} %fusion.122), kind=kOutput, calls=%fused_computation.316 | convolution fusion | flops 21217152 | bytes 5624320 | tf_op jit(solution)/shard_map/bgd,bjd->bgj/dot_general | solution.py:38
  33.3 3.5 %fusion.36 = bf16[32,1,4,128]{3,2,0,1:T(4,128)(2,1)S(1)} fusion(bf16[32,2,640,128]{3,2,1,0:T(8,128)(2,1)} %param.20, f32[32,4,640]{2,1,0:T(4,128)S(1)} %get-tuple-element.51, f32[32,4]{1,0:T(8,128)S(1)} %get-tuple-element.35, f32[32,4]{1,0:T(8,128)S(1)} %multiply_maximum_fusion, pred[32,640]{1,0:T(8,128)(4,1)S(1)} %fusion.122, f32[32,128]{1,0:T(8,128)S(1)} %bitcast.103, ...), kind=kOutput, calls=%fused_computation.32 | convolution fusion | flops 21348352 | bytes 5641728 | tf_op jit(solution)/shard_map/bgj,bjd->bgd/dot_general | solution.py:48
  36.8 3.5 %fusion.33 = bf16[32,1,4,128]{3,2,0,1:T(4,128)(2,1)S(1)} fusion(bf16[32,2,640,128]{3,2,1,0:T(8,128)(2,1)} %param.20, f32[32,4,640]{2,1,0:T(4,128)S(1)} %get-tuple-element.49, f32[32,4]{1,0:T(8,128)S(1)} %get-tuple-element.33, f32[32,4]{1,0:T(8,128)S(1)} %multiply_maximum_fusion.1, pred[32,640]{1,0:T(8,128)(4,1)S(1)} %fusion.122, ...), kind=kOutput, calls=%fused_computation.31 | convolution fusion | flops 21348352 | bytes 5641728 | tf_op jit(solution)/shard_map/bgj,bjd->bgd/dot_general | solution.py:48
  40.4 1.1 collective-permute-start
  41.6 4.9 %collective-permute-done = bf16[32,1024]{1,0:T(8,128)(2,1)S(1)} collective-permute-done((bf16[32,1024]{1,0:T(8,128)(2,1)S(1)}, bf16[32,1024]{1,0:T(8,128)(2,1)S(1)}, u32[]{:S(2)}, u32[]{:S(2)}) %collective-permute-start) | collective-permute-done | bytes 65568 | tf_op jit(solution)/shard_map/ppermute | solution.py:64
  46.9 4.6 %collective-permute-done.1 = bf16[64,1024]{1,0:T(8,128)(2,1)S(1)} collective-permute-done((bf16[64,1024]{1,0:T(8,128)(2,1)S(1)}, bf16[64,1024]{1,0:T(8,128)(2,1)S(1)}, u32[]{:S(2)}, u32[]{:S(2)}) %collective-permute-start.1) | collective-permute-done | bytes 131104 | tf_op jit(solution)/shard_map/ppermute | solution.py:64
  52.5 5.5 %collective-permute-done.2 = bf16[128,1024]{1,0:T(8,128)(2,1)S(1)} collective-permute-done((bf16[128,1024]{1,0:T(8,128)(2,1)S(1)}, bf16[128,1024]{1,0:T(8,128)(2,1)S(1)}, u32[]{:S(2)}, u32[]{:S(2)}) %collective-permute-start.2) | collective-permute-done | bytes 262176 | tf_op jit(solution)/shard_map/ppermute | solution.py:64
  58.0 2.4 %convolution_convert_fusion.8 = bf16[256,512]{1,0:T(8,128)(2,1)} fusion(bf16[4096,512]{1,0:T(8,128)(2,1)} %param.23, s32[]{:T(128)S(6)} %select_n.87, bf16[128,1024]{1,0:T(8,128)(2,1)S(1)} %collective-permute-done.2, bf16[64,1024]{1,0:T(8,128)(2,1)S(1)} %collective-permute-done.1, bf16[32,1024]{1,0:T(8,128)(2,1)S(1)} %collective-permute-done, ...), kind=kOutput, calls=%fused_computation.23 | convolution fusion | flops 270663680 | bytes 1835012 | tf_op jit(solution)/shard_map/dot_general | solution.py:181
  60.4 3.4 %all-to-all-start.1 = ((bf16[4,64,512]{2,1,0:T(8,128)(2,1)}), bf16[4,64,512]{2,1,0:T(8,128)(2,1)S(1)}, u32[]{:S(2)}, u32[]{:S(2)}) async-start(bf16[4,64,512]{2,1,0:T(8,128)(2,1)} %bitcast.20), calls=%async_computation.1 | async-start | bytes 524288 | tf_op jit(solution)/shard_map/all_to_all | solution.py:187
  63.8 6.0 %all-to-all-done.1 = bf16[4,64,512]{2,1,0:T(8,128)(2,1)S(1)} async-done(((bf16[4,64,512]{2,1,0:T(8,128)(2,1)}), bf16[4,64,512]{2,1,0:T(8,128)(2,1)S(1)}, u32[]{:S(2)}, u32[]{:S(2)}) %all-to-all-start.1) | async-done | bytes 262176 | tf_op jit(solution)/shard_map/all_to_all | solution.py:187
  69.8 6.1 %all_gather.3 = bf16[256,512]{1,0:T(8,128)(2,1)S(1)} all-gather(bf16[64,512]{1,0:T(8,128)(2,1)S(1)} %reduce_sum.60), channel_id=1, replica_groups=mesh['req'=8,'kv'=4] {'kv'}, dimensions={0}, use_global_device_ids=true | all-gather | bytes 327680 | tf_op jit(solution)/shard_map/all_gather | solution.py:191
  76.1 1.8 convolution_convert_fusion.6
  77.9 1.6 convolution_convert_fusion.2
  82.5 0.9 collective-permute-start.3
  83.4 1.3 collective-permute-start.15
  85.6 1.3 collective-permute-start.21
  87.0 19.4 %collective-permute-done.15 = bf16[128,1792]{1,0:T(8,128)(2,1)S(1)} collective-permute-done((bf16[128,1792]{1,0:T(8,128)(2,1)S(1)}, bf16[128,1792]{1,0:T(8,128)(2,1)S(1)}, u32[]{:S(2)}, u32[]{:S(2)}) %collective-permute-start.15) | collective-permute-done | bytes 458784 | tf_op jit(solution)/shard_map/ppermute | solution.py:64
  107.0 9.3 %collective-permute-done.9 = bf16[128,1792]{1,0:T(8,128)(2,1)S(1)} collective-permute-done((bf16[128,1792]{1,0:T(8,128)(2,1)S(1)}, bf16[128,1792]{1,0:T(8,128)(2,1)S(1)}, u32[]{:S(2)}, u32[]{:S(2)}) %collective-permute-start.9) | collective-permute-done | bytes 458784 | tf_op jit(solution)/shard_map/ppermute | solution.py:64
  116.8 8.7 %collective-permute-done.21 = bf16[128,1792]{1,0:T(8,128)(2,1)S(1)} collective-permute-done((bf16[128,1792]{1,0:T(8,128)(2,1)S(1)}, bf16[128,1792]{1,0:T(8,128)(2,1)S(1)}, u32[]{:S(2)}, u32[]{:S(2)}) %collective-permute-start.21) | collective-permute-done | bytes 458784 | tf_op jit(solution)/shard_map/ppermute | solution.py:64
  126.2 1.7 collective-permute-start.4
  128.4 2.7 %collective-permute-start.11 = (bf16[32,1792]{1,0:T(8,128)(2,1)S(1)}, bf16[32,1792]{1,0:T(8,128)(2,1)S(1)}, u32[]{:S(2)}, u32[]{:S(2)}) collective-permute-start(bf16[32,1792]{1,0:T(8,128)(2,1)S(1)} %slice.320), channel_id=1, source_target_pairs={{0,16},{4,20},{8,24},{12,28},{16,0},{20,4},{24,8},{28,12},{1,17},{... | collective-permute-start | bytes 344072 | tf_op jit(solution)/shard_map/ppermute | solution.py:64
  131.2 8.0 %collective-permute-done.22 = bf16[64,1792]{1,0:T(8,128)(2,1)S(1)} collective-permute-done((bf16[64,1792]{1,0:T(8,128)(2,1)S(1)}, bf16[64,1792]{1,0:T(8,128)(2,1)S(1)}, u32[]{:S(2)}, u32[]{:S(2)}) %collective-permute-start.22) | collective-permute-done | bytes 229408 | tf_op jit(solution)/shard_map/ppermute | solution.py:64
  139.3 3.7 %collective-permute-done.4 = bf16[64,1920]{1,0:T(8,128)(2,1)S(1)} collective-permute-done((bf16[64,1920]{1,0:T(8,128)(2,1)S(1)}, bf16[64,1920]{1,0:T(8,128)(2,1)S(1)}, u32[]{:S(2)}, u32[]{:S(2)}) %collective-permute-start.4) | collective-permute-done | bytes 245792 | tf_op jit(solution)/shard_map/ppermute | solution.py:64
  143.3 7.0 %collective-permute-done.23 = bf16[32,1792]{1,0:T(8,128)(2,1)S(1)} collective-permute-done((bf16[32,1792]{1,0:T(8,128)(2,1)S(1)}, bf16[32,1792]{1,0:T(8,128)(2,1)S(1)}, u32[]{:S(2)}, u32[]{:S(2)}) %collective-permute-start.23) | collective-permute-done | bytes 114720 | tf_op jit(solution)/shard_map/ppermute | solution.py:64
  150.3 2.5 %collective-permute-done.5 = bf16[32,1920]{1,0:T(8,128)(2,1)S(1)} collective-permute-done((bf16[32,1920]{1,0:T(8,128)(2,1)S(1)}, bf16[32,1920]{1,0:T(8,128)(2,1)S(1)}, u32[]{:S(2)}, u32[]{:S(2)}) %collective-permute-start.5) | collective-permute-done | bytes 122912 | tf_op jit(solution)/shard_map/ppermute | solution.py:64
  153.3 2.9 %collective-permute-start.18 = (bf16[32,896]{1,0:T(8,128)(2,1)S(1)}, bf16[32,896]{1,0:T(8,128)(2,1)S(1)}, u32[]{:S(2)}, u32[]{:S(2)}) collective-permute-start(bf16[32,896]{1,0:T(8,128)(2,1)S(1)} %get-tuple-element.45), channel_id=1, source_target_pairs={{0,16},{4,20},{8,24},{12,28},{16,0},{20,4},{24,8},{28,12},{1,17},{... | collective-permute-start | bytes 172040 | tf_op jit(solution)/shard_map/ppermute | solution.py:64
  156.3 2.8 %collective-permute-start.6 = (bf16[32,896]{1,0:T(8,128)(2,1)S(1)}, bf16[32,896]{1,0:T(8,128)(2,1)S(1)}, u32[]{:S(2)}, u32[]{:S(2)}) collective-permute-start(bf16[32,896]{1,0:T(8,128)(2,1)S(1)} %get-tuple-element.44), channel_id=1, source_target_pairs={{0,16},{4,20},{8,24},{12,28},{16,0},{20,4},{24,8},{28,12},{1,17},{... | collective-permute-start | bytes 172040 | tf_op jit(solution)/shard_map/ppermute | solution.py:64
  159.1 2.9 %collective-permute-done.24 = bf16[32,896]{1,0:T(8,128)(2,1)S(1)} collective-permute-done((bf16[32,896]{1,0:T(8,128)(2,1)S(1)}, bf16[32,896]{1,0:T(8,128)(2,1)S(1)}, u32[]{:S(2)}, u32[]{:S(2)}) %collective-permute-start.24) | collective-permute-done | bytes 57376 | tf_op jit(solution)/shard_map/ppermute | solution.py:64
  162.1 1.8 collective-permute-done.18
  164.2 1.0 collective-permute-done.12
  165.2 0.9 collective-permute-start.13
  166.2 1.2 collective-permute-start.7
  167.4 1.2 collective-permute-done.25
  168.6 1.3 collective-permute-start.26
  169.9 1.1 collective-permute-done.19
  171.1 1.3 collective-permute-start.20
  172.4 1.1 collective-permute-done.13
  173.5 1.3 collective-permute-start.14
  176.1 1.1 collective-permute-done.26
  177.6 4.5 %collective-permute-done.20 = bf16[128,896]{1,0:T(8,128)(2,1)S(1)} collective-permute-done((bf16[128,896]{1,0:T(8,128)(2,1)S(1)}, bf16[128,896]{1,0:T(8,128)(2,1)S(1)}, u32[]{:S(2)}, u32[]{:S(2)}) %collective-permute-start.20) | collective-permute-done | bytes 229408 | tf_op jit(solution)/shard_map/ppermute | solution.py:64
  182.6 4.5 %collective-permute-done.14 = bf16[128,896]{1,0:T(8,128)(2,1)S(1)} collective-permute-done((bf16[128,896]{1,0:T(8,128)(2,1)S(1)}, bf16[128,896]{1,0:T(8,128)(2,1)S(1)}, u32[]{:S(2)}, u32[]{:S(2)}) %collective-permute-start.14) | collective-permute-done | bytes 229408 | tf_op jit(solution)/shard_map/ppermute | solution.py:64
  187.5 2.0 collective-permute-done.8
  194.9 3.4 %all-to-all-start.2 = ((bf16[4,64,512]{2,1,0:T(8,128)(2,1)}), bf16[4,64,512]{2,1,0:T(8,128)(2,1)S(1)}, u32[]{:S(2)}, u32[]{:S(2)}) async-start(bf16[4,64,512]{2,1,0:T(8,128)(2,1)} %bitcast.21), calls=%async_computation.2 | async-start | bytes 524288 | tf_op jit(solution)/shard_map/all_to_all | solution.py:223
  198.3 6.0 %all-to-all-done.2 = bf16[4,64,512]{2,1,0:T(8,128)(2,1)S(1)} async-done(((bf16[4,64,512]{2,1,0:T(8,128)(2,1)}), bf16[4,64,512]{2,1,0:T(8,128)(2,1)S(1)}, u32[]{:S(2)}, u32[]{:S(2)}) %all-to-all-start.2) | async-done | bytes 262176 | tf_op jit(solution)/shard_map/all_to_all | solution.py:223
  (147 shorter events, 22.9 us)
Async XLA Ops:
  0.0 21.8 %copy-start = (bf16[4096,256]{1,0:T(8,128)(2,1)S(1)}, bf16[4096,256]{1,0:T(8,128)(2,1)}, u32[]{:S(2)}) copy-start(bf16[4096,256]{1,0:T(8,128)(2,1)} %param.17) | copy-start | bytes 6291460
  0.0 16.3 %all-to-all-start = ((bf16[8,32,512]{2,1,0:T(8,128)(2,1)}), bf16[8,32,512]{2,1,0:T(8,128)(2,1)S(1)}, u32[]{:S(2)}, u32[]{:S(2)}) async-start(bf16[8,32,512]{2,1,0:T(8,128)(2,1)} %bitcast.97), calls=%async_computation | async-start | bytes 524288 | tf_op jit(solution)/shard_map/all_to_all | solution.py:134
  16.6 5.2 %copy-start.3 = (f32[4096]{0:T(1024)S(1)}, f32[4096]{0:T(1024)}, u32[]{:S(2)}) copy-start(f32[4096]{0:T(1024)} %param.15) | copy-start | bytes 49156
  16.6 5.7 %copy-start.8 = (bf16[4096,256]{1,0:T(8,128)(2,1)S(1)}, bf16[4096,256]{1,0:T(8,128)(2,1)}, u32[]{:S(2)}) copy-start(bf16[4096,256]{1,0:T(8,128)(2,1)} %param.18) | copy-start | bytes 6291460
  36.7 4.8 %copy-start.2 = (bf16[256,512]{1,0:T(8,128)(2,1)S(1)}, bf16[256,512]{1,0:T(8,128)(2,1)}, u32[]{:S(2)}) copy-start(bf16[256,512]{1,0:T(8,128)(2,1)} %param.14) | copy-start | bytes 786436
  40.3 35.6 %copy-start.4 = (f32[512]{0:T(512)S(1)}, f32[512]{0:T(512)}, u32[]{:S(2)}) copy-start(f32[512]{0:T(512)} %param.24) | copy-start | bytes 6148
  40.4 6.0 %collective-permute-start = (bf16[32,1024]{1,0:T(8,128)(2,1)S(1)}, bf16[32,1024]{1,0:T(8,128)(2,1)S(1)}, u32[]{:S(2)}, u32[]{:S(2)}) collective-permute-start(bf16[32,1024]{1,0:T(8,128)(2,1)S(1)} %reshape.100), channel_id=1, source_target_pairs={{0,16},{4,20},{8,24},{12,28},{16,0},{20,4},{24,8},{28,12},{1,17},{... | collective-permute-start | bytes 196616 | tf_op jit(solution)/shard_map/ppermute | solution.py:64
  46.5 5.0 %collective-permute-start.1 = (bf16[64,1024]{1,0:T(8,128)(2,1)S(1)}, bf16[64,1024]{1,0:T(8,128)(2,1)S(1)}, u32[]{:S(2)}, u32[]{:S(2)}) collective-permute-start(bf16[64,1024]{1,0:T(8,128)(2,1)S(1)} %pad_maximum_fusion.9), channel_id=1, source_target_pairs={{0,8},{4,12},{8,0},{12,4},{16,24},{20,28},{24,16},{28,20},{1,9},{5... | collective-permute-start | bytes 393224 | tf_op jit(solution)/shard_map/ppermute | solution.py:64
  51.5 6.4 %collective-permute-start.2 = (bf16[128,1024]{1,0:T(8,128)(2,1)S(1)}, bf16[128,1024]{1,0:T(8,128)(2,1)S(1)}, u32[]{:S(2)}, u32[]{:S(2)}) collective-permute-start(bf16[128,1024]{1,0:T(8,128)(2,1)S(1)} %pad_maximum_fusion.4), channel_id=1, source_target_pairs={{0,4},{4,0},{8,12},{12,8},{16,20},{20,16},{24,28},{28,24},{1,5},{5... | collective-permute-start | bytes 786440 | tf_op jit(solution)/shard_map/ppermute | solution.py:64
  60.4 9.4 %all-to-all-start.1 = ((bf16[4,64,512]{2,1,0:T(8,128)(2,1)}), bf16[4,64,512]{2,1,0:T(8,128)(2,1)S(1)}, u32[]{:S(2)}, u32[]{:S(2)}) async-start(bf16[4,64,512]{2,1,0:T(8,128)(2,1)} %bitcast.20), calls=%async_computation.1 | async-start | bytes 524288 | tf_op jit(solution)/shard_map/all_to_all | solution.py:187
  69.8 9.7 %copy-start.6 = (bf16[512,3584]{1,0:T(8,128)(2,1)S(1)}, bf16[512,3584]{1,0:T(8,128)(2,1)}, u32[]{:S(2)}) copy-start(bf16[512,3584]{1,0:T(8,128)(2,1)} %param.25) | copy-start | bytes 11010052
  76.1 4.3 %copy-start.5 = (bf16[512,3584]{1,0:T(8,128)(2,1)S(1)}, bf16[512,3584]{1,0:T(8,128)(2,1)}, u32[]{:S(2)}) copy-start(bf16[512,3584]{1,0:T(8,128)(2,1)} %param.26) | copy-start | bytes 11010052
  82.5 43.6 %collective-permute-start.3 = (bf16[128,1920]{1,0:T(8,128)(2,1)S(1)}, bf16[128,1920]{1,0:T(8,128)(2,1)S(1)}, u32[]{:S(2)}, u32[]{:S(2)}) collective-permute-start(bf16[128,1920]{1,0:T(8,128)(2,1)S(1)} %slice.307), channel_id=1, source_target_pairs={{0,4},{4,0},{8,12},{12,8},{16,20},{20,16},{24,28},{28,24},{1,5},{5... | collective-permute-start | bytes 1474568 | tf_op jit(solution)/shard_map/ppermute | solution.py:64
  83.4 23.0 %collective-permute-start.15 = (bf16[128,1792]{1,0:T(8,128)(2,1)S(1)}, bf16[128,1792]{1,0:T(8,128)(2,1)S(1)}, u32[]{:S(2)}, u32[]{:S(2)}) collective-permute-start(bf16[128,1792]{1,0:T(8,128)(2,1)S(1)} %pad_maximum_fusion.2), channel_id=1, source_target_pairs={{0,4},{4,0},{8,12},{12,8},{16,20},{20,16},{24,28},{28,24},{1,5},{5... | collective-permute-start | bytes 1376264 | tf_op jit(solution)/shard_map/ppermute | solution.py:64
  84.7 31.5 %collective-permute-start.9 = (bf16[128,1792]{1,0:T(8,128)(2,1)S(1)}, bf16[128,1792]{1,0:T(8,128)(2,1)S(1)}, u32[]{:S(2)}, u32[]{:S(2)}) collective-permute-start(bf16[128,1792]{1,0:T(8,128)(2,1)S(1)} %pad_maximum_fusion.3), channel_id=1, source_target_pairs={{0,4},{4,0},{8,12},{12,8},{16,20},{20,16},{24,28},{28,24},{1,5},{5... | collective-permute-start | bytes 1376264 | tf_op jit(solution)/shard_map/ppermute | solution.py:64
  85.6 39.9 %collective-permute-start.21 = (bf16[128,1792]{1,0:T(8,128)(2,1)S(1)}, bf16[128,1792]{1,0:T(8,128)(2,1)S(1)}, u32[]{:S(2)}, u32[]{:S(2)}) collective-permute-start(bf16[128,1792]{1,0:T(8,128)(2,1)S(1)} %pad_maximum_fusion.1), channel_id=1, source_target_pairs={{0,4},{4,0},{8,12},{12,8},{16,20},{20,16},{24,28},{28,24},{1,5},{5... | collective-permute-start | bytes 1376264 | tf_op jit(solution)/shard_map/ppermute | solution.py:64
  106.5 21.4 %collective-permute-start.16 = (bf16[64,1792]{1,0:T(8,128)(2,1)S(1)}, bf16[64,1792]{1,0:T(8,128)(2,1)S(1)}, u32[]{:S(2)}, u32[]{:S(2)}) collective-permute-start(bf16[64,1792]{1,0:T(8,128)(2,1)S(1)} %slice.326), channel_id=1, source_target_pairs={{0,8},{4,12},{8,0},{12,4},{16,24},{20,28},{24,16},{28,20},{1,9},{5... | collective-permute-start | bytes 688136 | tf_op jit(solution)/shard_map/ppermute | solution.py:64
  116.4 12.0 %collective-permute-start.10 = (bf16[64,1792]{1,0:T(8,128)(2,1)S(1)}, bf16[64,1792]{1,0:T(8,128)(2,1)S(1)}, u32[]{:S(2)}, u32[]{:S(2)}) collective-permute-start(bf16[64,1792]{1,0:T(8,128)(2,1)S(1)} %slice.318), channel_id=1, source_target_pairs={{0,8},{4,12},{8,0},{12,4},{16,24},{20,28},{24,16},{28,20},{1,9},{5... | collective-permute-start | bytes 688136 | tf_op jit(solution)/shard_map/ppermute | solution.py:64
  125.6 13.5 %collective-permute-start.22 = (bf16[64,1792]{1,0:T(8,128)(2,1)S(1)}, bf16[64,1792]{1,0:T(8,128)(2,1)S(1)}, u32[]{:S(2)}, u32[]{:S(2)}) collective-permute-start(bf16[64,1792]{1,0:T(8,128)(2,1)S(1)} %slice.334), channel_id=1, source_target_pairs={{0,8},{4,12},{8,0},{12,4},{16,24},{20,28},{24,16},{28,20},{1,9},{5... | collective-permute-start | bytes 688136 | tf_op jit(solution)/shard_map/ppermute | solution.py:64
  126.2 16.8 %collective-permute-start.4 = (bf16[64,1920]{1,0:T(8,128)(2,1)S(1)}, bf16[64,1920]{1,0:T(8,128)(2,1)S(1)}, u32[]{:S(2)}, u32[]{:S(2)}) collective-permute-start(bf16[64,1920]{1,0:T(8,128)(2,1)S(1)} %slice.309), channel_id=1, source_target_pairs={{0,8},{4,12},{8,0},{12,4},{16,24},{20,28},{24,16},{28,20},{1,9},{5... | collective-permute-start | bytes 737288 | tf_op jit(solution)/shard_map/ppermute | solution.py:64
  128.0 15.2 %collective-permute-start.17 = (bf16[32,1792]{1,0:T(8,128)(2,1)S(1)}, bf16[32,1792]{1,0:T(8,128)(2,1)S(1)}, u32[]{:S(2)}, u32[]{:S(2)}) collective-permute-start(bf16[32,1792]{1,0:T(8,128)(2,1)S(1)} %slice.328), channel_id=1, source_target_pairs={{0,16},{4,20},{8,24},{12,28},{16,0},{20,4},{24,8},{28,12},{1,17},{... | collective-permute-start | bytes 344072 | tf_op jit(solution)/shard_map/ppermute | solution.py:64
  128.4 14.8 %collective-permute-start.11 = (bf16[32,1792]{1,0:T(8,128)(2,1)S(1)}, bf16[32,1792]{1,0:T(8,128)(2,1)S(1)}, u32[]{:S(2)}, u32[]{:S(2)}) collective-permute-start(bf16[32,1792]{1,0:T(8,128)(2,1)S(1)} %slice.320), channel_id=1, source_target_pairs={{0,16},{4,20},{8,24},{12,28},{16,0},{20,4},{24,8},{28,12},{1,17},{... | collective-permute-start | bytes 344072 | tf_op jit(solution)/shard_map/ppermute | solution.py:64
  139.2 38.0 %copy-start.7 = (bf16[3584,512]{1,0:T(8,128)(2,1)S(1)}, bf16[3584,512]{1,0:T(8,128)(2,1)}, u32[]{:S(2)}) copy-start(bf16[3584,512]{1,0:T(8,128)(2,1)} %param.27) | copy-start | bytes 11010052
  139.2 11.0 %collective-permute-start.23 = (bf16[32,1792]{1,0:T(8,128)(2,1)S(1)}, bf16[32,1792]{1,0:T(8,128)(2,1)S(1)}, u32[]{:S(2)}, u32[]{:S(2)}) collective-permute-start(bf16[32,1792]{1,0:T(8,128)(2,1)S(1)} %slice.336), channel_id=1, source_target_pairs={{0,16},{4,20},{8,24},{12,28},{16,0},{20,4},{24,8},{28,12},{1,17},{... | collective-permute-start | bytes 344072 | tf_op jit(solution)/shard_map/ppermute | solution.py:64
  143.1 9.7 %collective-permute-start.5 = (bf16[32,1920]{1,0:T(8,128)(2,1)S(1)}, bf16[32,1920]{1,0:T(8,128)(2,1)S(1)}, u32[]{:S(2)}, u32[]{:S(2)}) collective-permute-start(bf16[32,1920]{1,0:T(8,128)(2,1)S(1)} %slice.311), channel_id=1, source_target_pairs={{0,16},{4,20},{8,24},{12,28},{16,0},{20,4},{24,8},{28,12},{1,17},{... | collective-permute-start | bytes 368648 | tf_op jit(solution)/shard_map/ppermute | solution.py:64
  153.2 8.8 %collective-permute-start.24 = (bf16[32,896]{1,0:T(8,128)(2,1)S(1)}, bf16[32,896]{1,0:T(8,128)(2,1)S(1)}, u32[]{:S(2)}, u32[]{:S(2)}) collective-permute-start(bf16[32,896]{1,0:T(8,128)(2,1)S(1)} %get-tuple-element.47), channel_id=1, source_target_pairs={{0,16},{4,20},{8,24},{12,28},{16,0},{20,4},{24,8},{28,12},{1,17},{... | collective-permute-start | bytes 172040 | tf_op jit(solution)/shard_map/ppermute | solution.py:64
  153.3 10.7 %collective-permute-start.18 = (bf16[32,896]{1,0:T(8,128)(2,1)S(1)}, bf16[32,896]{1,0:T(8,128)(2,1)S(1)}, u32[]{:S(2)}, u32[]{:S(2)}) collective-permute-start(bf16[32,896]{1,0:T(8,128)(2,1)S(1)} %get-tuple-element.45), channel_id=1, source_target_pairs={{0,16},{4,20},{8,24},{12,28},{16,0},{20,4},{24,8},{28,12},{1,17},{... | collective-permute-start | bytes 172040 | tf_op jit(solution)/shard_map/ppermute | solution.py:64
  156.2 9.0 %collective-permute-start.12 = (bf16[32,896]{1,0:T(8,128)(2,1)S(1)}, bf16[32,896]{1,0:T(8,128)(2,1)S(1)}, u32[]{:S(2)}, u32[]{:S(2)}) collective-permute-start(bf16[32,896]{1,0:T(8,128)(2,1)S(1)} %get-tuple-element.46), channel_id=1, source_target_pairs={{0,16},{4,20},{8,24},{12,28},{16,0},{20,4},{24,8},{28,12},{1,17},{... | collective-permute-start | bytes 172040 | tf_op jit(solution)/shard_map/ppermute | solution.py:64
  156.3 9.9 %collective-permute-start.6 = (bf16[32,896]{1,0:T(8,128)(2,1)S(1)}, bf16[32,896]{1,0:T(8,128)(2,1)S(1)}, u32[]{:S(2)}, u32[]{:S(2)}) collective-permute-start(bf16[32,896]{1,0:T(8,128)(2,1)S(1)} %get-tuple-element.44), channel_id=1, source_target_pairs={{0,16},{4,20},{8,24},{12,28},{16,0},{20,4},{24,8},{28,12},{1,17},{... | collective-permute-start | bytes 172040 | tf_op jit(solution)/shard_map/ppermute | solution.py:64
  162.0 6.6 %collective-permute-start.25 = (bf16[64,896]{1,0:T(8,128)(2,1)S(1)}, bf16[64,896]{1,0:T(8,128)(2,1)S(1)}, u32[]{:S(2)}, u32[]{:S(2)}) collective-permute-start(bf16[64,896]{1,0:T(8,128)(2,1)S(1)} %pad_maximum_fusion.13), channel_id=1, source_target_pairs={{0,8},{4,12},{8,0},{12,4},{16,24},{20,28},{24,16},{28,20},{1,9},{5... | collective-permute-start | bytes 344072 | tf_op jit(solution)/shard_map/ppermute | solution.py:64
  164.0 7.1 %collective-permute-start.19 = (bf16[64,896]{1,0:T(8,128)(2,1)S(1)}, bf16[64,896]{1,0:T(8,128)(2,1)S(1)}, u32[]{:S(2)}, u32[]{:S(2)}) collective-permute-start(bf16[64,896]{1,0:T(8,128)(2,1)S(1)} %pad_maximum_fusion.12), channel_id=1, source_target_pairs={{0,8},{4,12},{8,0},{12,4},{16,24},{20,28},{24,16},{28,20},{1,9},{5... | collective-permute-start | bytes 344072 | tf_op jit(solution)/shard_map/ppermute | solution.py:64
  165.2 8.3 %collective-permute-start.13 = (bf16[64,896]{1,0:T(8,128)(2,1)S(1)}, bf16[64,896]{1,0:T(8,128)(2,1)S(1)}, u32[]{:S(2)}, u32[]{:S(2)}) collective-permute-start(bf16[64,896]{1,0:T(8,128)(2,1)S(1)} %pad_maximum_fusion.11), channel_id=1, source_target_pairs={{0,8},{4,12},{8,0},{12,4},{16,24},{20,28},{24,16},{28,20},{1,9},{5... | collective-permute-start | bytes 344072 | tf_op jit(solution)/shard_map/ppermute | solution.py:64
  166.2 9.0 %collective-permute-start.7 = (bf16[64,896]{1,0:T(8,128)(2,1)S(1)}, bf16[64,896]{1,0:T(8,128)(2,1)S(1)}, u32[]{:S(2)}, u32[]{:S(2)}) collective-permute-start(bf16[64,896]{1,0:T(8,128)(2,1)S(1)} %pad_maximum_fusion.10), channel_id=1, source_target_pairs={{0,8},{4,12},{8,0},{12,4},{16,24},{20,28},{24,16},{28,20},{1,9},{5... | collective-permute-start | bytes 344072 | tf_op jit(solution)/shard_map/ppermute | solution.py:64
  168.6 8.6 %collective-permute-start.26 = (bf16[128,896]{1,0:T(8,128)(2,1)S(1)}, bf16[128,896]{1,0:T(8,128)(2,1)S(1)}, u32[]{:S(2)}, u32[]{:S(2)}) collective-permute-start(bf16[128,896]{1,0:T(8,128)(2,1)S(1)} %pad_maximum_fusion.8), channel_id=1, source_target_pairs={{0,4},{4,0},{8,12},{12,8},{16,20},{20,16},{24,28},{28,24},{1,5},{5... | collective-permute-start | bytes 688136 | tf_op jit(solution)/shard_map/ppermute | solution.py:64
  171.1 11.0 %collective-permute-start.20 = (bf16[128,896]{1,0:T(8,128)(2,1)S(1)}, bf16[128,896]{1,0:T(8,128)(2,1)S(1)}, u32[]{:S(2)}, u32[]{:S(2)}) collective-permute-start(bf16[128,896]{1,0:T(8,128)(2,1)S(1)} %pad_maximum_fusion.7), channel_id=1, source_target_pairs={{0,4},{4,0},{8,12},{12,8},{16,20},{20,16},{24,28},{28,24},{1,5},{5... | collective-permute-start | bytes 688136 | tf_op jit(solution)/shard_map/ppermute | solution.py:64
  173.5 13.5 %collective-permute-start.14 = (bf16[128,896]{1,0:T(8,128)(2,1)S(1)}, bf16[128,896]{1,0:T(8,128)(2,1)S(1)}, u32[]{:S(2)}, u32[]{:S(2)}) collective-permute-start(bf16[128,896]{1,0:T(8,128)(2,1)S(1)} %pad_maximum_fusion.6), channel_id=1, source_target_pairs={{0,4},{4,0},{8,12},{12,8},{16,20},{20,16},{24,28},{28,24},{1,5},{5... | collective-permute-start | bytes 688136 | tf_op jit(solution)/shard_map/ppermute | solution.py:64
  175.2 14.3 %collective-permute-start.8 = (bf16[128,896]{1,0:T(8,128)(2,1)S(1)}, bf16[128,896]{1,0:T(8,128)(2,1)S(1)}, u32[]{:S(2)}, u32[]{:S(2)}) collective-permute-start(bf16[128,896]{1,0:T(8,128)(2,1)S(1)} %pad_maximum_fusion.5), channel_id=1, source_target_pairs={{0,4},{4,0},{8,12},{12,8},{16,20},{20,16},{24,28},{28,24},{1,5},{5... | collective-permute-start | bytes 688136 | tf_op jit(solution)/shard_map/ppermute | solution.py:64
  182.1 22.8 %copy-start.1 = (bf16[4096,256]{1,0:T(8,128)(2,1)S(1)}, bf16[4096,256]{1,0:T(8,128)(2,1)}, u32[]{:S(2)}) copy-start(bf16[4096,256]{1,0:T(8,128)(2,1)} %param.17) | copy-start | bytes 6291460
  194.9 9.4 %all-to-all-start.2 = ((bf16[4,64,512]{2,1,0:T(8,128)(2,1)}), bf16[4,64,512]{2,1,0:T(8,128)(2,1)S(1)}, u32[]{:S(2)}, u32[]{:S(2)}) async-start(bf16[4,64,512]{2,1,0:T(8,128)(2,1)} %bitcast.21), calls=%async_computation.2 | async-start | bytes 524288 | tf_op jit(solution)/shard_map/all_to_all | solution.py:223

commit v2 on v1

--- a/solution.py
+++ b/solution.py
@@ -3,6 +3,8 @@
 import jax
 import jax.numpy as jnp
 from jax import lax
+from jax.experimental import pallas as pl
+from jax.experimental.pallas import tpu as pltpu
 from jax.sharding import PartitionSpec as P
 
 MODEL_WIDTH = 4096
@@ -76,17 +78,13 @@
     )
 
 
-def natural_order(value, place, size):
+def local_spot(place, block, size):
     bits = size.bit_length() - 1
-    rows = value.shape[0] // size
-    pieces = []
-    for block in range(size):
-        other = place ^ block
-        spot = jnp.int32(0)
-        for bit in range(bits):
-            spot = spot | (((other >> bit) & 1) << (bits - 1 - bit))
-        pieces.append(lax.dynamic_slice_in_dim(value, spot * rows, rows, 0))
-    return jnp.concatenate(pieces, axis=0)
+    other = place ^ block
+    spot = jnp.int32(0)
+    for bit in range(bits):
+        spot = spot | (((other >> bit) & 1) << (bits - 1 - bit))
+    return spot
 
 
 def gather_rows(value, size):
@@ -95,12 +93,22 @@
     return value
 
 
-def scatter_sum(value, size):
-    for bit in range(size.bit_length() - 1):
-        half = value.shape[0] // 2
-        other = exchange(value[half:], size, bit)
-        value = (value[:half].astype(jnp.float32) + other.astype(jnp.float32)).astype(jnp.bfloat16)
-    return value
+def kv_exchange(value, size, bit):
+    return lax.ppermute(value, "kv", [(i, i ^ (1 << bit)) for i in range(size)])
+
+
+def kv_sum(value, place, size):
+    half = value.shape[0] // 2
+    mine = lax.rem(place, 2)
+    pair = value.astype(jnp.float32) + kv_exchange(value, size, 0).astype(jnp.float32)
+    part = lax.dynamic_slice_in_dim(pair, mine * half, half, 0)
+    for bit in range(1, size.bit_length() - 1):
+        part = part + kv_exchange(part.astype(jnp.bfloat16), size, bit).astype(jnp.float32)
+    part = part.astype(jnp.bfloat16)
+    other = kv_exchange(part, size, 0)
+    return jnp.where(
+        mine == 0, jnp.concatenate([part, other], axis=0), jnp.concatenate([other, part], axis=0)
+    )
 
 
 def chunks_of(columns):
@@ -109,6 +117,224 @@
         if tiles % count == 0:
             return count
     return 1
+
+
+class Chain:
+    def __init__(self, token):
+        self.token = token
+
+    def run(self, body, outs, ins, in_specs=None, flops=0):
+        specs = list(in_specs or [None] * len(ins))
+        specs = [
+            pl.BlockSpec(memory_space=pltpu.VMEM) if spec is None else spec for spec in specs
+        ]
+        count = len(ins)
+
+        def kernel(*refs):
+            body(*refs[:count], *refs[count + 1 :])
+
+        results = pl.pallas_call(
+            kernel,
+            out_shape=outs,
+            grid=(1,),
+            in_specs=[*specs, pl.BlockSpec(memory_space=pl.ANY)],
+            out_specs=[pl.BlockSpec(memory_space=pltpu.VMEM)] * len(outs),
+            compiler_params=pltpu.CompilerParams(vmem_limit_bytes=32 * 1024 * 1024),
+            cost_estimate=pl.CostEstimate(flops=0, bytes_accessed=0, transcendentals=0),
+        )(*ins, self.token)
+        self.token = results[0]
+        return results
+
+
+def array(shape, dtype):
+    return jax.ShapeDtypeStruct(shape, dtype)
+
+
+def project(chain, scaled, squares, gate, up, chunk, width):
+    rows, depth = scaled.shape
+    half = rows // 2
+    total = 2 * width + (128 if squares is not None else 0)
+
+    def body(scaled_ref, gate_ref, up_ref, *refs):
+        send_ref, keep_ref = refs[-2:]
+        for start, out_ref in ((half, send_ref), (0, keep_ref)):
+            left = scaled_ref[start : start + half]
+            out_ref[:, :width] = jnp.dot(
+                left, gate_ref[...], preferred_element_type=jnp.float32
+            ).astype(jnp.bfloat16)
+            out_ref[:, width : 2 * width] = jnp.dot(
+                left, up_ref[...], preferred_element_type=jnp.float32
+            ).astype(jnp.bfloat16)
+            if squares is not None:
+                out_ref[:, 2 * width :] = jnp.broadcast_to(
+                    refs[0][start : start + half], (half, 128)
+                ).astype(jnp.bfloat16)
+
+    ins, specs = [scaled, gate, up], [None]
+    specs += [pl.BlockSpec((depth, width), lambda i: (0, chunk))] * 2
+    if squares is not None:
+        ins.append(squares)
+        specs.append(None)
+    out = array((half, total), jnp.bfloat16)
+    return chain.run(body, [out, out], ins, specs, flops=4 * rows * depth * width)
+
+
+def add_halve(chain, other, kept):
+    half = kept.shape[0] // 2
+
+    def body(other_ref, kept_ref, send_ref, keep_ref):
+        for start, out_ref in ((half, send_ref), (0, keep_ref)):
+            rows = slice(start, start + half)
+            out_ref[...] = (
+                other_ref[rows].astype(jnp.float32) + kept_ref[rows].astype(jnp.float32)
+            ).astype(jnp.bfloat16)
+
+    out = array((half, kept.shape[1]), jnp.bfloat16)
+    return chain.run(body, [out, out], [other, kept])
+
+
+def activate(chain, other, kept, inverse, width):
+    rows = kept.shape[0]
+    first = inverse is None
+
+    def body(other_ref, kept_ref, *refs):
+        def total(columns):
+            return other_ref[:, columns].astype(jnp.float32) + kept_ref[:, columns].astype(
+                jnp.float32
+            )
+
+        if first:
+            hidden_ref, inverse_ref = refs
+            scale = 1.0 / jnp.sqrt(total(slice(2 * width, 2 * width + 128)) / MODEL_WIDTH + EPS)
+            inverse_ref[...] = scale
+        else:
+            scale_ref, hidden_ref = refs
+            scale = scale_ref[...]
+        scale = scale[:, :1]
+        gate = total(slice(0, width)) * scale
+        up = total(slice(width, 2 * width)) * scale
+        hidden_ref[...] = (gate / (1.0 + jnp.exp(-gate)) * up).astype(jnp.bfloat16)
+
+    outs = [array((rows, width), jnp.bfloat16)]
+    ins = [other, kept]
+    if first:
+        outs.append(array((rows, 128), jnp.float32))
+    else:
+        ins.append(inverse)
+    results = chain.run(body, outs, ins)
+    return results if first else (results[0], inverse)
+
+
+def join(chain, kept, other):
+    rows = kept.shape[0]
+
+    def body(kept_ref, other_ref, out_ref):
+        out_ref[:rows] = kept_ref[...]
+        out_ref[rows:] = other_ref[...]
+
+    return chain.run(body, [array((2 * rows, kept.shape[1]), kept.dtype)], [kept, other])[0]
+
+
+def lower(chain, kept, other, down, chunk, width, carried):
+    half = kept.shape[0]
+    columns = down.shape[1]
+
+    def body(kept_ref, other_ref, down_ref, *refs):
+        out_ref = refs[-1]
+        for start, hidden_ref in ((0, kept_ref), (half, other_ref)):
+            rows = slice(start, start + half)
+            product = jnp.dot(
+                hidden_ref[...], down_ref[...], preferred_element_type=jnp.float32
+            )
+            out_ref[rows] = product if carried is None else refs[0][rows] + product
+
+    ins = [kept, other, down]
+    specs = [None, None, pl.BlockSpec((width, columns), lambda i: (chunk, 0))]
+    if carried is not None:
+        ins.append(carried)
+        specs.append(None)
+    return chain.run(
+        body,
+        [array((2 * half, columns), jnp.float32)],
+        ins,
+        specs,
+        flops=4 * half * width * columns,
+    )[0]
+
+
+def split_for_kv(chain, total, places, req_size, kv_size):
+    rows, columns = total.shape
+    bits = req_size.bit_length() - 1
+    block = rows // req_size
+    per = req_size // kv_size
+
+    def body(places_ref, total_ref, send_ref, keep_ref):
+        req_place, mine = places_ref[0], places_ref[1]
+        for spot in range(req_size):
+            actual = req_place ^ bit_reverse(spot, bits)
+            owner = actual // per
+            start = pl.multiple_of(((owner // 2) * per + actual % per) * block, block)
+            value = total_ref[spot * block : (spot + 1) * block].astype(jnp.bfloat16)
+
+            @pl.when(owner % 2 == mine)
+            def _():
+                keep_ref[pl.ds(start, block)] = value
+
+            @pl.when(owner % 2 != mine)
+            def _():
+                send_ref[pl.ds(start, block)] = value
+
+    out = array((rows // 2, columns), jnp.bfloat16)
+    return chain.run(
+        body,
+        [out, out],
+        [places, total],
+        [pl.BlockSpec(memory_space=pltpu.SMEM), None],
+    )
+
+
+def feed_forward(scaled, squares, gate_weight, up_weight, down_weight, req_size):
+    bits = req_size.bit_length() - 1
+    count = chunks_of(gate_weight.shape[1])
+    width = gate_weight.shape[1] // count
+    chain = Chain(scaled)
+    kept, moving = {}, {}
+    state = {"inverse": None, "total": None}
+
+    def step(chunk, stage):
+        if stage == 0:
+            send, kept[chunk] = project(
+                chain, scaled, squares if chunk == 0 else None, gate_weight, up_weight, chunk, width
+            )
+            moving[chunk] = exchange(send, req_size, 0)
+        elif stage < bits:
+            send, kept[chunk] = add_halve(chain, moving[chunk], kept[chunk])
+            moving[chunk] = exchange(send, req_size, stage)
+        elif stage == bits:
+            kept[chunk], state["inverse"] = activate(
+                chain, moving[chunk], kept[chunk], state["inverse"], width
+            )
+            moving[chunk] = exchange(kept[chunk], req_size, bits - 1)
+        elif stage < 2 * bits:
+            kept[chunk] = join(chain, kept[chunk], moving[chunk])
+            moving[chunk] = exchange(kept[chunk], req_size, 2 * bits - 1 - stage)
+        else:
+            state["total"] = lower(
+                chain, kept[chunk], moving[chunk], down_weight, chunk, width, state["total"]
+            )
+
+    for chunk, stage in task_order(count, bits):
+        step(chunk, stage)
+    return chain, state["total"]
+
+
+def task_order(count, bits):
+    tasks = [(chunk, 0) for chunk in range(count)]
+    for slot in range(1, count + 2 * bits):
+        for chunk in range(count):
+            if 1 <= slot - chunk <= 2 * bits:
+                tasks.append((chunk, slot - chunk))
+    return tasks
 
 
 def shards(
@@ -183,51 +409,37 @@
         weight_rows,
         preferred_element_type=jnp.float32,
     ).astype(jnp.bfloat16)
-    total_rows = partial_mix.shape[0]
-    pieces = lax.all_to_all(
-        partial_mix.reshape(kv_size, total_rows // kv_size, -1), "kv", split_axis=0, concat_axis=0
-    )
-    mixed_share = jnp.sum(pieces.astype(jnp.float32), axis=0).astype(jnp.bfloat16)
-    mixed = lax.all_gather(mixed_share, "kv", axis=0, tiled=True)
+    mixed = kv_sum(partial_mix, kv_place, kv_size)
     middle = residual_rows + mixed.astype(jnp.float32)
     scaled = (middle * mlp_gain).astype(jnp.bfloat16)
     squares = jnp.sum(middle * middle, axis=-1, keepdims=True)
-    count = chunks_of(gate_weight.shape[1])
-    width = gate_weight.shape[1] // count
-    inverse = None
-    partial_out = None
-    sums = []
-    for chunk in range(count):
-        columns = slice(chunk * width, (chunk + 1) * width)
-        parts = [
-            jnp.dot(scaled, gate_weight[:, columns], preferred_element_type=jnp.float32),
-            jnp.dot(scaled, up_weight[:, columns], preferred_element_type=jnp.float32),
-        ]
-        if chunk == 0:
-            parts.append(jnp.broadcast_to(squares, (total_rows, 128)))
-        sums.append(scatter_sum(jnp.concatenate(parts, axis=1).astype(jnp.bfloat16), req_size))
-    for chunk in range(count):
-        total = sums[chunk].astype(jnp.float32)
-        if chunk == 0:
-            inverse = 1.0 / jnp.sqrt(total[:, 2 * width : 2 * width + 1] / MODEL_WIDTH + EPS)
-        hidden = (
-            jax.nn.silu(total[:, :width] * inverse) * (total[:, width : 2 * width] * inverse)
-        ).astype(jnp.bfloat16)
-        product = jnp.dot(
-            gather_rows(hidden, req_size),
-            down_weight[chunk * width : (chunk + 1) * width],
-            preferred_element_type=jnp.float32,
+    chain, total = feed_forward(scaled, squares, gate_weight, up_weight, down_weight, req_size)
+    places = jnp.stack([req_place, lax.rem(kv_place, 2)]).astype(jnp.int32)
+    send, kept = split_for_kv(chain, total, places, req_size, kv_size)
+    value = kept.astype(jnp.float32) + kv_exchange(send, kv_size, 0).astype(jnp.float32)
+    for bit in reversed(range(1, kv_size.bit_length() - 1)):
+        half = value.shape[0] // 2
+        mine = lax.rem(kv_place >> bit, 2)
+        other = kv_exchange(
+            lax.dynamic_slice_in_dim(value, (1 - mine) * half, half, 0).astype(jnp.bfloat16),
+            kv_size,
+            bit,
         )
-        partial_out = product if partial_out is None else partial_out + product
-    ordered = natural_order(partial_out.astype(jnp.bfloat16), req_place, req_size)
-    pieces = lax.all_to_all(
-        ordered.reshape(kv_size, total_rows // kv_size, -1), "kv", split_axis=0, concat_axis=0
-    )
-    share = total_rows // kv_size
-    base_rows = lax.dynamic_slice_in_dim(
-        natural_order(middle, req_place, req_size), kv_place * share, share, 0
-    )
-    return (base_rows + jnp.sum(pieces.astype(jnp.float32), axis=0)).astype(jnp.bfloat16)
+        value = lax.dynamic_slice_in_dim(value, mine * half, half, 0) + other.astype(jnp.float32)
+    per = req_size // kv_size
+    base_rows = jnp.concatenate(
+        [
+            lax.dynamic_slice_in_dim(
+                middle,
+                local_spot(req_place, kv_place * per + i, req_size) * local_rows,
+                local_rows,
+                0,
+            )
+            for i in range(per)
+        ],
+        axis=0,
+    )
+    return (base_rows + value).astype(jnp.bfloat16)
 
 
 def solution(mesh):

time: 206 us -> 172 us (0.83)
  waiting for transfers between devices: 114 us -> 84.5 us
  matrix products: 32.3 us -> 23.2 us
  starting transfers between devices: 40.4 us -> 47.3 us
  Pallas kernels: 0 us -> 6.7 us
  blocking collectives: 6.1 us -> 0 us
    ppermute x27, waiting for transfers between devices: 95.3 us -> 66.9 us  [exchange(): return lax.ppermute(value, 'req', [(i, i ^ 1 << bit) for i in range(size)])]
    all_to_all x2 -> x0, waiting for transfers between devices: 11.9 us -> none  [the longest x1 5.96 us: shards(): lax.all_to_all(partial_mix.reshape(kv_size, total_rows // kv_size, -1), '...]
    ppermute x0 -> x5, waiting for transfers between devices: none -> 10.8 us  [kv_exchange(): return lax.ppermute(value, 'kv', [(i, i ^ 1 << bit) for i in range(size)])]
    ppermute x27, starting transfers between devices: 26.2 us -> 36.5 us  [exchange(): return lax.ppermute(value, 'req', [(i, i ^ 1 << bit) for i in range(size)])]
    dot_general x12 -> x0, matrix products: 7.72 us -> none  [the longest x4 4.26 us: shards(): jnp.dot(scaled, up_weight[:, columns], preferred_element_type=jnp.float32)]
    all_to_all x2 -> x0, starting transfers between devices: 6.81 us -> none  [the longest x1 3.4 us: shards(): lax.all_to_all(partial_mix.reshape(kv_size, total_rows // kv_size, -1), '...]
    pallas_call x0 -> x29, Pallas kernels: none -> 6.7 us  [run(): pl.pallas_call(kernel, out_shape=outs, grid=(1,), in_specs=[*specs, pl.Bl...]
    all_gather x1 -> x0, blocking collectives: 6.1 us -> none  [shards(): mixed = lax.all_gather(mixed_share, 'kv', axis=0, tiled=True)]
  transfers between devices with their start and end apart: 30 -> 33, of which waited for: 24 -> 27; matrix products, arithmetic and copies ran while one was open for 2% -> 1% of each run, Pallas kernels for 0% -> 3%
where the time goes in v2:
time: 172 us
  waiting for transfers between devices  84.5 us (49%)
  starting transfers between devices  47.3 us (28%)
  matrix products  23.2 us (13%)
  Pallas kernels  6.7 us (4%)
  other arithmetic  4.65 us (3%)
  local copies, waits for them, and re-layouts  4.64 us (3%)
    ppermute x27, waiting for transfers between devices, exchange(): return lax.ppermute(value, 'req', [(i, i ^ 1 << bit) for i in range(size)])  66.9 us
    ppermute x27, starting transfers between devices, exchange(): return lax.ppermute(value, 'req', [(i, i ^ 1 << bit) for i in range(size)])  36.5 us
    ppermute x5, waiting for transfers between devices, kv_exchange(): return lax.ppermute(value, 'kv', [(i, i ^ 1 << bit) for i in range(size)])  10.8 us
    dot_general x2, matrix products, attend(): jnp.einsum('bgd,bjd->bgj', query_rows, keys, preferred_element_type=jnp.f...  8.61 us
    all_to_all x1, starting transfers between devices, shards(): lax.all_to_all(residual_in, 'req', split_axis=0, concat_axis=1, tiled=True)  7.38 us
    dot_general x2, matrix products, attend(): jnp.einsum('bgj,bjd->bgd', weights, values, preferred_element_type=jnp.fl...  7.03 us
    all_to_all x1, waiting for transfers between devices, shards(): lax.all_to_all(residual_in, 'req', split_axis=0, concat_axis=1, tiled=True)  6.83 us
    pallas_call x29, Pallas kernels, run(): pl.pallas_call(kernel, out_shape=outs, grid=(1,), in_specs=[*specs, pl.Bl...  6.7 us
  transfers between devices with their start and end apart: 33, of which 27 were waited for; matrix products, arithmetic and copies ran while one was open for 1% of the time, Pallas kernels for 3%

profile of v2, /device:TPU:0, one launch (start us, length us, event | category | flops | bytes accessed | tf_op | source)
XLA Modules:
  0.0 171.6 jit_solution(12656253494933819978)
XLA Ops:
  0.0 7.4 %all-to-all-start = ((bf16[8,32,512]{2,1,0:T(8,128)(2,1)}), bf16[8,32,512]{2,1,0:T(8,128)(2,1)S(1)}, u32[]{:S(2)}, u32[]{:S(2)}) async-start(bf16[8,32,512]{2,1,0:T(8,128)(2,1)} %bitcast.90), calls=%async_computation | async-start | bytes 524288 | tf_op jit(solution)/shard_map/all_to_all | solution.py:360
  9.5 6.8 %all-to-all-done = bf16[8,32,512]{2,1,0:T(8,128)(2,1)S(1)} async-done(((bf16[8,32,512]{2,1,0:T(8,128)(2,1)}), bf16[8,32,512]{2,1,0:T(8,128)(2,1)S(1)}, u32[]{:S(2)}, u32[]{:S(2)}) %all-to-all-start) | async-done | bytes 262176 | tf_op jit(solution)/shard_map/all_to_all | solution.py:360
  16.6 1.4 fusion.157
  18.0 2.6 %fusion.158 = f32[32,256]{1,0:T(8,128)S(1)} fusion(bf16[4096,256]{1,0:T(8,128)(2,1)} %param.17, f32[32,4096]{1,0:T(8,128)S(1)} %bitcast.88, f32[4096]{0:T(1024)S(1)} %copy-done.7, f32[32]{0:T(128)S(1)} %add_sqrt_fusion), kind=kOutput, calls=%fused_computation.190 | convolution fusion | flops 67502080 | bytes 2670720 | tf_op jit(solution)/shard_map/dot_general | solution.py:375
  20.6 1.6 fusion.159
  22.7 4.3 %fusion.161 = (f32[32,4]{1,0:T(8,128)S(1)}, f32[32,4,640]{2,1,0:T(4,128)S(1)}) fusion(bf16[32,2,640,128]{3,2,1,0:T(8,128)(2,1)} %param.19, bf16[32,2,4,128]{3,2,1,0:T(4,128)(2,1)S(1)} %convert_element_type.109, pred[32,640]{1,0:T(8,128)(4,1)S(1)} %fusion.63), kind=kOutput, calls=%fused_computation.193 | convolution fusion | flops 21217152 | bytes 5624320 | tf_op jit(solution)/shard_map/bgd,bjd->bgj/dot_general | solution.py:40
  27.0 4.3 %fusion.162 = (f32[32,4]{1,0:T(8,128)S(1)}, f32[32,4,640]{2,1,0:T(4,128)S(1)}) fusion(bf16[32,2,640,128]{3,2,1,0:T(8,128)(2,1)} %param.19, bf16[32,2,4,128]{3,2,1,0:T(4,128)(2,1)S(1)} %convert_element_type.109, pred[32,640]{1,0:T(8,128)(4,1)S(1)} %fusion.63), kind=kOutput, calls=%fused_computation.194 | convolution fusion | flops 21217152 | bytes 5624320 | tf_op jit(solution)/shard_map/bgd,bjd->bgj/dot_general | solution.py:40
  32.6 3.5 %fusion.30 = bf16[32,1,4,128]{3,2,0,1:T(4,128)(2,1)S(1)} fusion(bf16[32,2,640,128]{3,2,1,0:T(8,128)(2,1)} %param.20, f32[32,4,640]{2,1,0:T(4,128)S(1)} %get-tuple-element.102, f32[32,4]{1,0:T(8,128)S(1)} %get-tuple-element.90, f32[32,4]{1,0:T(8,128)S(1)} %multiply_maximum_fusion.1, pred[32,640]{1,0:T(8,128)(4,1)S(1)} %fusion.63, ...), kind=kOutput, calls=%fused_computation.19 | convolution fusion | flops 21348352 | bytes 5641728 | tf_op jit(solution)/shard_map/bgj,bjd->bgd/dot_general | solution.py:50
  36.1 3.5 %fusion.33 = bf16[32,1,4,128]{3,2,0,1:T(4,128)(2,1)S(1)} fusion(bf16[32,2,640,128]{3,2,1,0:T(8,128)(2,1)} %param.20, f32[32,4,640]{2,1,0:T(4,128)S(1)} %get-tuple-element.104, f32[32,4]{1,0:T(8,128)S(1)} %get-tuple-element.92, f32[32,4]{1,0:T(8,128)S(1)} %multiply_maximum_fusion, pred[32,640]{1,0:T(8,128)(4,1)S(1)} %fusion.63, f32[32,128]{1,0:T(8,128)S(1)} %bitcast.95, ...), kind=kOutput, calls=%fused_computation.20 | convolution fusion | flops 21348352 | bytes 5641728 | tf_op jit(solution)/shard_map/bgj,bjd->bgd/dot_general | solution.py:50
  40.9 4.9 %collective-permute-done = bf16[32,1024]{1,0:T(8,128)(2,1)S(1)} collective-permute-done((bf16[32,1024]{1,0:T(8,128)(2,1)S(1)}, bf16[32,1024]{1,0:T(8,128)(2,1)S(1)}, u32[]{:S(2)}, u32[]{:S(2)}) %collective-permute-start) | collective-permute-done | bytes 65568 | tf_op jit(solution)/shard_map/ppermute | solution.py:66
  46.3 4.6 %collective-permute-done.1 = bf16[64,1024]{1,0:T(8,128)(2,1)S(1)} collective-permute-done((bf16[64,1024]{1,0:T(8,128)(2,1)S(1)}, bf16[64,1024]{1,0:T(8,128)(2,1)S(1)}, u32[]{:S(2)}, u32[]{:S(2)}) %collective-permute-start.1) | collective-permute-done | bytes 131104 | tf_op jit(solution)/shard_map/ppermute | solution.py:66
  51.8 5.5 %collective-permute-done.2 = bf16[128,1024]{1,0:T(8,128)(2,1)S(1)} collective-permute-done((bf16[128,1024]{1,0:T(8,128)(2,1)S(1)}, bf16[128,1024]{1,0:T(8,128)(2,1)S(1)}, u32[]{:S(2)}, u32[]{:S(2)}) %collective-permute-start.2) | collective-permute-done | bytes 262176 | tf_op jit(solution)/shard_map/ppermute | solution.py:66
  57.4 1.7 convolution_convert_fusion
  59.2 1.4 collective-permute-done.3
  60.7 1.6 collective-permute-start.4
  62.3 4.0 %collective-permute-done.4 = bf16[128,512]{1,0:T(8,128)(2,1)S(1)} collective-permute-done((bf16[128,512]{1,0:T(8,128)(2,1)S(1)}, bf16[128,512]{1,0:T(8,128)(2,1)S(1)}, u32[]{:S(2)}, u32[]{:S(2)}) %collective-permute-start.4) | collective-permute-done | bytes 131104 | tf_op jit(solution)/shard_map/ppermute | solution.py:97
  66.5 1.3 collective-permute-done.5
  68.2 2.0 %copy-done.3 = bf16[512,3584]{1,0:T(8,128)(2,1)S(1)} copy-done((bf16[512,3584]{1,0:T(8,128)(2,1)S(1)}, bf16[512,3584]{1,0:T(8,128)(2,1)}, u32[]{:S(2)}) %copy-start.3) | copy-done | bytes 3670040
  70.2 2.0 %copy-done.4 = bf16[512,3584]{1,0:T(8,128)(2,1)S(1)} copy-done((bf16[512,3584]{1,0:T(8,128)(2,1)S(1)}, bf16[512,3584]{1,0:T(8,128)(2,1)}, u32[]{:S(2)}) %copy-start.4) | copy-done | bytes 3670040
  74.6 1.3 collective-permute-start.8
  77.4 9.7 %collective-permute-done.9.refs_0_ = bf16[128,1920]{1,0:T(8,128)(2,1)S(1)} collective-permute-done((bf16[128,1920]{1,0:T(8,128)(2,1)S(1)}, bf16[128,1920]{1,0:T(8,128)(2,1)S(1)}, u32[]{:S(2)}, u32[]{:S(2)}) %collective-permute-start.9) | collective-permute-done | bytes 491552 | tf_op jit(solution)/shard_map/ppermute | solution.py:66
  88.2 5.5 %collective-permute-done.10.refs_0_ = bf16[64,1920]{1,0:T(8,128)(2,1)S(1)} collective-permute-done((bf16[64,1920]{1,0:T(8,128)(2,1)S(1)}, bf16[64,1920]{1,0:T(8,128)(2,1)S(1)}, u32[]{:S(2)}, u32[]{:S(2)}) %collective-permute-start.10) | collective-permute-done | bytes 245792 | tf_op jit(solution)/shard_map/ppermute | solution.py:66
  93.7 3.2 %collective-permute-done.8.refs_0_ = bf16[128,1792]{1,0:T(8,128)(2,1)S(1)} collective-permute-done((bf16[128,1792]{1,0:T(8,128)(2,1)S(1)}, bf16[128,1792]{1,0:T(8,128)(2,1)S(1)}, u32[]{:S(2)}, u32[]{:S(2)}) %collective-permute-start.8) | collective-permute-done | bytes 458784 | tf_op jit(solution)/shard_map/ppermute | solution.py:66
  98.2 1.7 collective-permute-start.12
  99.9 5.9 %collective-permute-done.12.refs_0_ = bf16[32,1920]{1,0:T(8,128)(2,1)S(1)} collective-permute-done((bf16[32,1920]{1,0:T(8,128)(2,1)S(1)}, bf16[32,1920]{1,0:T(8,128)(2,1)S(1)}, u32[]{:S(2)}, u32[]{:S(2)}) %collective-permute-start.12) | collective-permute-done | bytes 122912 | tf_op jit(solution)/shard_map/ppermute | solution.py:66
  107.8 2.4 %collective-permute-start.14 = (bf16[32,1792]{1,0:T(8,128)(2,1)S(1)}, bf16[32,1792]{1,0:T(8,128)(2,1)S(1)}, u32[]{:S(2)}, u32[]{:S(2)}) collective-permute-start(bf16[32,1792]{1,0:T(8,128)(2,1)S(1)} %get-tuple-element.54.refs_2_), channel_id=1, source_target_pairs={{0,16},{4,20},{8,24},{12,28},{16,0},{20,4},{24,8},{28,12},{1,17},{... | collective-permute-start | bytes 344072 | tf_op jit(solution)/shard_map/ppermute | solution.py:66
  110.2 4.3 %collective-permute-done.15.refs_1_ = bf16[32,896]{1,0:T(8,128)(2,1)S(1)} collective-permute-done((bf16[32,896]{1,0:T(8,128)(2,1)S(1)}, bf16[32,896]{1,0:T(8,128)(2,1)S(1)}, u32[]{:S(2)}, u32[]{:S(2)}) %collective-permute-start.15) | collective-permute-done | bytes 57376 | tf_op jit(solution)/shard_map/ppermute | solution.py:66
  114.6 1.3 collective-permute-start.19
  116.0 1.8 %collective-permute-done.13.refs_0_ = bf16[64,1792]{1,0:T(8,128)(2,1)S(1)} collective-permute-done((bf16[64,1792]{1,0:T(8,128)(2,1)S(1)}, bf16[64,1792]{1,0:T(8,128)(2,1)S(1)}, u32[]{:S(2)}, u32[]{:S(2)}) %collective-permute-start.13) | collective-permute-done | bytes 229408 | tf_op jit(solution)/shard_map/ppermute | solution.py:66
  118.5 2.0 %collective-permute-done.19.refs_1_ = bf16[64,896]{1,0:T(8,128)(2,1)S(1)} collective-permute-done((bf16[64,896]{1,0:T(8,128)(2,1)S(1)}, bf16[64,896]{1,0:T(8,128)(2,1)S(1)}, u32[]{:S(2)}, u32[]{:S(2)}) %collective-permute-start.19) | collective-permute-done | bytes 114720 | tf_op jit(solution)/shard_map/ppermute | solution.py:66
  121.2 2.8 %collective-permute-start.18 = (bf16[32,896]{1,0:T(8,128)(2,1)S(1)}, bf16[32,896]{1,0:T(8,128)(2,1)S(1)}, u32[]{:S(2)}, u32[]{:S(2)}) collective-permute-start(bf16[32,896]{1,0:T(8,128)(2,1)S(1)} %shard_map.147.refs_2_.refs_0_), channel_id=1, source_target_pairs={{0,16},{4,20},{8,24},{12,28},{16,0},{20,4},{24,8},{28,12},{1,17},{... | collective-permute-start | bytes 172040 | tf_op jit(solution)/shard_map/ppermute | solution.py:66
  124.1 2.3 %collective-permute-done.18.refs_1_ = bf16[32,896]{1,0:T(8,128)(2,1)S(1)} collective-permute-done((bf16[32,896]{1,0:T(8,128)(2,1)S(1)}, bf16[32,896]{1,0:T(8,128)(2,1)S(1)}, u32[]{:S(2)}, u32[]{:S(2)}) %collective-permute-start.18) | collective-permute-done | bytes 57376 | tf_op jit(solution)/shard_map/ppermute | solution.py:66
  126.4 2.7 %collective-permute-start.22 = (bf16[64,896]{1,0:T(8,128)(2,1)S(1)}, bf16[64,896]{1,0:T(8,128)(2,1)S(1)}, u32[]{:S(2)}, u32[]{:S(2)}) collective-permute-start(bf16[64,896]{1,0:T(8,128)(2,1)S(1)} %shard_map.151.refs_3_.refs_0_), channel_id=1, source_target_pairs={{0,8},{4,12},{8,0},{12,4},{16,24},{20,28},{24,16},{28,20},{1,9},{5... | collective-permute-start | bytes 344072 | tf_op jit(solution)/shard_map/ppermute | solution.py:66
  129.1 1.9 %collective-permute-done.17.refs_0_ = bf16[32,1792]{1,0:T(8,128)(2,1)S(1)} collective-permute-done((bf16[32,1792]{1,0:T(8,128)(2,1)S(1)}, bf16[32,1792]{1,0:T(8,128)(2,1)S(1)}, u32[]{:S(2)}, u32[]{:S(2)}) %collective-permute-start.17) | collective-permute-done | bytes 114720 | tf_op jit(solution)/shard_map/ppermute | solution.py:66
  132.1 1.3 collective-permute-start.26
  133.4 3.9 %collective-permute-start.21 = (bf16[32,896]{1,0:T(8,128)(2,1)S(1)}, bf16[32,896]{1,0:T(8,128)(2,1)S(1)}, u32[]{:S(2)}, u32[]{:S(2)}) collective-permute-start(bf16[32,896]{1,0:T(8,128)(2,1)S(1)} %shard_map.152.refs_2_.refs_0_), channel_id=1, source_target_pairs={{0,16},{4,20},{8,24},{12,28},{16,0},{20,4},{24,8},{28,12},{1,17},{... | collective-permute-start | bytes 172040 | tf_op jit(solution)/shard_map/ppermute | solution.py:66
  137.3 2.2 %collective-permute-done.21.refs_1_ = bf16[32,896]{1,0:T(8,128)(2,1)S(1)} collective-permute-done((bf16[32,896]{1,0:T(8,128)(2,1)S(1)}, bf16[32,896]{1,0:T(8,128)(2,1)S(1)}, u32[]{:S(2)}, u32[]{:S(2)}) %collective-permute-start.21) | collective-permute-done | bytes 57376 | tf_op jit(solution)/shard_map/ppermute | solution.py:66
  139.5 4.1 %collective-permute-start.25 = (bf16[64,896]{1,0:T(8,128)(2,1)S(1)}, bf16[64,896]{1,0:T(8,128)(2,1)S(1)}, u32[]{:S(2)}, u32[]{:S(2)}) collective-permute-start(bf16[64,896]{1,0:T(8,128)(2,1)S(1)} %shard_map.156.refs_3_.refs_0_), channel_id=1, source_target_pairs={{0,8},{4,12},{8,0},{12,4},{16,24},{20,28},{24,16},{28,20},{1,9},{5... | collective-permute-start | bytes 344072 | tf_op jit(solution)/shard_map/ppermute | solution.py:66
  143.6 1.4 collective-permute-done.20.refs_0_
  147.6 3.2 %collective-permute-start.24 = (bf16[32,896]{1,0:T(8,128)(2,1)S(1)}, bf16[32,896]{1,0:T(8,128)(2,1)S(1)}, u32[]{:S(2)}, u32[]{:S(2)}) collective-permute-start(bf16[32,896]{1,0:T(8,128)(2,1)S(1)} %shard_map.157.refs_4_.refs_0_), channel_id=1, source_target_pairs={{0,16},{4,20},{8,24},{12,28},{16,0},{20,4},{24,8},{28,12},{1,17},{... | collective-permute-start | bytes 172040 | tf_op jit(solution)/shard_map/ppermute | solution.py:66
  150.8 2.2 %collective-permute-done.24.refs_1_ = bf16[32,896]{1,0:T(8,128)(2,1)S(1)} collective-permute-done((bf16[32,896]{1,0:T(8,128)(2,1)S(1)}, bf16[32,896]{1,0:T(8,128)(2,1)S(1)}, u32[]{:S(2)}, u32[]{:S(2)}) %collective-permute-start.24) | collective-permute-done | bytes 57376 | tf_op jit(solution)/shard_map/ppermute | solution.py:66
  153.0 1.8 %collective-permute-start.27 = (bf16[64,896]{1,0:T(8,128)(2,1)S(1)}, bf16[64,896]{1,0:T(8,128)(2,1)S(1)}, u32[]{:S(2)}, u32[]{:S(2)}) collective-permute-start(bf16[64,896]{1,0:T(8,128)(2,1)S(1)} %shard_map.160.refs_4_.refs_0_), channel_id=1, source_target_pairs={{0,8},{4,12},{8,0},{12,4},{16,24},{20,28},{24,16},{28,20},{1,9},{5... | collective-permute-start | bytes 344072 | tf_op jit(solution)/shard_map/ppermute | solution.py:66
  155.5 2.4 %collective-permute-done.27.refs_1_ = bf16[64,896]{1,0:T(8,128)(2,1)S(1)} collective-permute-done((bf16[64,896]{1,0:T(8,128)(2,1)S(1)}, bf16[64,896]{1,0:T(8,128)(2,1)S(1)}, u32[]{:S(2)}, u32[]{:S(2)}) %collective-permute-start.27) | collective-permute-done | bytes 114720 | tf_op jit(solution)/shard_map/ppermute | solution.py:66
  157.9 1.7 collective-permute-start.29
  159.6 4.3 %collective-permute-done.29.refs_1_ = bf16[128,896]{1,0:T(8,128)(2,1)S(1)} collective-permute-done((bf16[128,896]{1,0:T(8,128)(2,1)S(1)}, bf16[128,896]{1,0:T(8,128)(2,1)S(1)}, u32[]{:S(2)}, u32[]{:S(2)}) %collective-permute-start.29) | collective-permute-done | bytes 229408 | tf_op jit(solution)/shard_map/ppermute | solution.py:66
  165.3 1.3 collective-permute-done.30
  166.6 1.6 collective-permute-start.31
  168.2 2.8 %collective-permute-done.31 = bf16[64,512]{1,0:T(8,128)(2,1)S(1)} collective-permute-done((bf16[64,512]{1,0:T(8,128)(2,1)S(1)}, bf16[64,512]{1,0:T(8,128)(2,1)S(1)}, u32[]{:S(2)}, u32[]{:S(2)}) %collective-permute-start.31) | collective-permute-done | bytes 65568 | tf_op jit(solution)/shard_map/ppermute | solution.py:97
  (123 shorter events, 23.6 us)
Async XLA Ops:
  0.0 16.6 %copy-start = (bf16[4096,256]{1,0:T(8,128)(2,1)S(1)}, bf16[4096,256]{1,0:T(8,128)(2,1)}, u32[]{:S(2)}) copy-start(bf16[4096,256]{1,0:T(8,128)(2,1)} %param.18) | copy-start | bytes 6291460
  0.0 18.0 %copy-start.7 = (f32[4096]{0:T(1024)S(1)}, f32[4096]{0:T(1024)}, u32[]{:S(2)}) copy-start(f32[4096]{0:T(1024)} %param.15) | copy-start | bytes 49156
  0.0 16.3 %all-to-all-start = ((bf16[8,32,512]{2,1,0:T(8,128)(2,1)}), bf16[8,32,512]{2,1,0:T(8,128)(2,1)S(1)}, u32[]{:S(2)}, u32[]{:S(2)}) async-start(bf16[8,32,512]{2,1,0:T(8,128)(2,1)} %bitcast.90), calls=%async_computation | async-start | bytes 524288 | tf_op jit(solution)/shard_map/all_to_all | solution.py:360
  16.3 4.3 %copy-start.5 = (bf16[4096,1024]{1,0:T(8,128)(2,1)S(1)}, bf16[4096,1024]{1,0:T(8,128)(2,1)}, u32[]{:S(2)}) copy-start(bf16[4096,1024]{1,0:T(8,128)(2,1)} %param.16) | copy-start | bytes 25165828
  36.1 15.7 %copy-start.6 = (bf16[256,512]{1,0:T(8,128)(2,1)S(1)}, bf16[256,512]{1,0:T(8,128)(2,1)}, u32[]{:S(2)}) copy-start(bf16[256,512]{1,0:T(8,128)(2,1)} %param.14) | copy-start | bytes 786436
  39.7 28.4 %copy-start.8 = (f32[512]{0:T(512)S(1)}, f32[512]{0:T(512)}, u32[]{:S(2)}) copy-start(f32[512]{0:T(512)} %param.24) | copy-start | bytes 6148
  39.8 6.0 %collective-permute-start = (bf16[32,1024]{1,0:T(8,128)(2,1)S(1)}, bf16[32,1024]{1,0:T(8,128)(2,1)S(1)}, u32[]{:S(2)}, u32[]{:S(2)}) collective-permute-start(bf16[32,1024]{1,0:T(8,128)(2,1)S(1)} %reshape.93), channel_id=1, source_target_pairs={{0,16},{4,20},{8,24},{12,28},{16,0},{20,4},{24,8},{28,12},{1,17},{... | collective-permute-start | bytes 196616 | tf_op jit(solution)/shard_map/ppermute | solution.py:66
  45.9 5.0 %collective-permute-start.1 = (bf16[64,1024]{1,0:T(8,128)(2,1)S(1)}, bf16[64,1024]{1,0:T(8,128)(2,1)S(1)}, u32[]{:S(2)}, u32[]{:S(2)}) collective-permute-start(bf16[64,1024]{1,0:T(8,128)(2,1)S(1)} %pad_maximum_fusion.1), channel_id=1, source_target_pairs={{0,8},{4,12},{8,0},{12,4},{16,24},{20,28},{24,16},{28,20},{1,9},{5... | collective-permute-start | bytes 393224 | tf_op jit(solution)/shard_map/ppermute | solution.py:66
  50.9 6.4 %collective-permute-start.2 = (bf16[128,1024]{1,0:T(8,128)(2,1)S(1)}, bf16[128,1024]{1,0:T(8,128)(2,1)S(1)}, u32[]{:S(2)}, u32[]{:S(2)}) collective-permute-start(bf16[128,1024]{1,0:T(8,128)(2,1)S(1)} %pad_maximum_fusion), channel_id=1, source_target_pairs={{0,4},{4,0},{8,12},{12,8},{16,20},{20,16},{24,28},{28,24},{1,5},{5... | collective-permute-start | bytes 786440 | tf_op jit(solution)/shard_map/ppermute | solution.py:66
  59.0 1.6 collective-permute-start.3
  60.7 5.6 %collective-permute-start.4 = (bf16[128,512]{1,0:T(8,128)(2,1)S(1)}, bf16[128,512]{1,0:T(8,128)(2,1)S(1)}, u32[]{:S(2)}, u32[]{:S(2)}) collective-permute-start(bf16[128,512]{1,0:T(8,128)(2,1)S(1)} %fusion.51), channel_id=1, source_target_pairs={{0,2},{1,3},{2,0},{3,1},{4,6},{5,7},{6,4},{7,5},{8,10},{9,11},{10,... | collective-permute-start | bytes 393224 | tf_op jit(solution)/shard_map/ppermute | solution.py:97
  66.3 1.4 collective-permute-start.5
  68.1 2.0 %copy-start.3 = (bf16[512,3584]{1,0:T(8,128)(2,1)S(1)}, bf16[512,3584]{1,0:T(8,128)(2,1)}, u32[]{:S(2)}) copy-start(bf16[512,3584]{1,0:T(8,128)(2,1)} %refs_1_.7) | copy-start | bytes 11010052
  70.2 2.0 %copy-start.4 = (bf16[512,3584]{1,0:T(8,128)(2,1)S(1)}, bf16[512,3584]{1,0:T(8,128)(2,1)}, u32[]{:S(2)}) copy-start(bf16[512,3584]{1,0:T(8,128)(2,1)} %refs_2_.11) | copy-start | bytes 11010052
  73.0 14.1 %collective-permute-start.9 = (bf16[128,1920]{1,0:T(8,128)(2,1)S(1)}, bf16[128,1920]{1,0:T(8,128)(2,1)S(1)}, u32[]{:S(2)}, u32[]{:S(2)}) collective-permute-start(bf16[128,1920]{1,0:T(8,128)(2,1)S(1)} %get-tuple-element.39.refs_3_), channel_id=1, source_target_pairs={{0,4},{4,0},{8,12},{12,8},{16,20},{20,16},{24,28},{28,24},{1,5},{5... | collective-permute-start | bytes 1474568 | tf_op jit(solution)/shard_map/ppermute | solution.py:66
  74.6 22.3 %collective-permute-start.8 = (bf16[128,1792]{1,0:T(8,128)(2,1)S(1)}, bf16[128,1792]{1,0:T(8,128)(2,1)S(1)}, u32[]{:S(2)}, u32[]{:S(2)}) collective-permute-start(bf16[128,1792]{1,0:T(8,128)(2,1)S(1)} %get-tuple-element.40.refs_3_), channel_id=1, source_target_pairs={{0,4},{4,0},{8,12},{12,8},{16,20},{20,16},{24,28},{28,24},{1,5},{5... | collective-permute-start | bytes 1376264 | tf_op jit(solution)/shard_map/ppermute | solution.py:66
  77.3 53.8 %copy-start.2 = (bf16[3584,512]{1,0:T(8,128)(2,1)S(1)}, bf16[3584,512]{1,0:T(8,128)(2,1)}, u32[]{:S(2)}) copy-start(bf16[3584,512]{1,0:T(8,128)(2,1)} %refs_2_.15) | copy-start | bytes 11010052
  87.2 6.5 %collective-permute-start.10 = (bf16[64,1920]{1,0:T(8,128)(2,1)S(1)}, bf16[64,1920]{1,0:T(8,128)(2,1)S(1)}, u32[]{:S(2)}, u32[]{:S(2)}) collective-permute-start(bf16[64,1920]{1,0:T(8,128)(2,1)S(1)} %get-tuple-element.47.refs_2_), channel_id=1, source_target_pairs={{0,8},{4,12},{8,0},{12,4},{16,24},{20,28},{24,16},{28,20},{1,9},{5... | collective-permute-start | bytes 737288 | tf_op jit(solution)/shard_map/ppermute | solution.py:66
  87.6 19.1 %collective-permute-start.7 = (bf16[128,1792]{1,0:T(8,128)(2,1)S(1)}, bf16[128,1792]{1,0:T(8,128)(2,1)S(1)}, u32[]{:S(2)}, u32[]{:S(2)}) collective-permute-start(bf16[128,1792]{1,0:T(8,128)(2,1)S(1)} %get-tuple-element.41.refs_3_), channel_id=1, source_target_pairs={{0,4},{4,0},{8,12},{12,8},{16,20},{20,16},{24,28},{28,24},{1,5},{5... | collective-permute-start | bytes 1376264 | tf_op jit(solution)/shard_map/ppermute | solution.py:66
  97.0 8.9 %collective-permute-start.11 = (bf16[64,1792]{1,0:T(8,128)(2,1)S(1)}, bf16[64,1792]{1,0:T(8,128)(2,1)S(1)}, u32[]{:S(2)}, u32[]{:S(2)}) collective-permute-start(bf16[64,1792]{1,0:T(8,128)(2,1)S(1)} %get-tuple-element.50.refs_2_), channel_id=1, source_target_pairs={{0,8},{4,12},{8,0},{12,4},{16,24},{20,28},{24,16},{28,20},{1,9},{5... | collective-permute-start | bytes 688136 | tf_op jit(solution)/shard_map/ppermute | solution.py:66
  97.5 20.5 %collective-permute-start.6 = (bf16[128,1792]{1,0:T(8,128)(2,1)S(1)}, bf16[128,1792]{1,0:T(8,128)(2,1)S(1)}, u32[]{:S(2)}, u32[]{:S(2)}) collective-permute-start(bf16[128,1792]{1,0:T(8,128)(2,1)S(1)} %get-tuple-element.42.refs_2_), channel_id=1, source_target_pairs={{0,4},{4,0},{8,12},{12,8},{16,20},{20,16},{24,28},{28,24},{1,5},{5... | collective-permute-start | bytes 1376264 | tf_op jit(solution)/shard_map/ppermute | solution.py:66
  98.2 7.6 %collective-permute-start.12 = (bf16[32,1920]{1,0:T(8,128)(2,1)S(1)}, bf16[32,1920]{1,0:T(8,128)(2,1)S(1)}, u32[]{:S(2)}, u32[]{:S(2)}) collective-permute-start(bf16[32,1920]{1,0:T(8,128)(2,1)S(1)} %get-tuple-element.49.refs_2_), channel_id=1, source_target_pairs={{0,16},{4,20},{8,24},{12,28},{16,0},{20,4},{24,8},{28,12},{1,17},{... | collective-permute-start | bytes 368648 | tf_op jit(solution)/shard_map/ppermute | solution.py:66
  106.9 11.0 %collective-permute-start.13 = (bf16[64,1792]{1,0:T(8,128)(2,1)S(1)}, bf16[64,1792]{1,0:T(8,128)(2,1)S(1)}, u32[]{:S(2)}, u32[]{:S(2)}) collective-permute-start(bf16[64,1792]{1,0:T(8,128)(2,1)S(1)} %get-tuple-element.55.refs_2_), channel_id=1, source_target_pairs={{0,8},{4,12},{8,0},{12,4},{16,24},{20,28},{24,16},{28,20},{1,9},{5... | collective-permute-start | bytes 688136 | tf_op jit(solution)/shard_map/ppermute | solution.py:66
  107.3 7.3 %collective-permute-start.15 = (bf16[32,896]{1,0:T(8,128)(2,1)S(1)}, bf16[32,896]{1,0:T(8,128)(2,1)S(1)}, u32[]{:S(2)}, u32[]{:S(2)}) collective-permute-start(bf16[32,896]{1,0:T(8,128)(2,1)S(1)} %get-tuple-element.53.refs_2_.refs_0_), channel_id=1, source_target_pairs={{0,16},{4,20},{8,24},{12,28},{16,0},{20,4},{24,8},{28,12},{1,17},{... | collective-permute-start | bytes 172040 | tf_op jit(solution)/shard_map/ppermute | solution.py:66
  107.8 8.1 %collective-permute-start.14 = (bf16[32,1792]{1,0:T(8,128)(2,1)S(1)}, bf16[32,1792]{1,0:T(8,128)(2,1)S(1)}, u32[]{:S(2)}, u32[]{:S(2)}) collective-permute-start(bf16[32,1792]{1,0:T(8,128)(2,1)S(1)} %get-tuple-element.54.refs_2_), channel_id=1, source_target_pairs={{0,16},{4,20},{8,24},{12,28},{16,0},{20,4},{24,8},{28,12},{1,17},{... | collective-permute-start | bytes 344072 | tf_op jit(solution)/shard_map/ppermute | solution.py:66
  114.6 6.0 %collective-permute-start.19 = (bf16[64,896]{1,0:T(8,128)(2,1)S(1)}, bf16[64,896]{1,0:T(8,128)(2,1)S(1)}, u32[]{:S(2)}, u32[]{:S(2)}) collective-permute-start(bf16[64,896]{1,0:T(8,128)(2,1)S(1)} %shard_map.146.refs_3_.refs_0_), channel_id=1, source_target_pairs={{0,8},{4,12},{8,0},{12,4},{16,24},{20,28},{24,16},{28,20},{1,9},{5... | collective-permute-start | bytes 344072 | tf_op jit(solution)/shard_map/ppermute | solution.py:66
  118.1 13.0 %collective-permute-start.16 = (bf16[64,1792]{1,0:T(8,128)(2,1)S(1)}, bf16[64,1792]{1,0:T(8,128)(2,1)S(1)}, u32[]{:S(2)}, u32[]{:S(2)}) collective-permute-start(bf16[64,1792]{1,0:T(8,128)(2,1)S(1)} %get-tuple-element.60.refs_2_), channel_id=1, source_target_pairs={{0,8},{4,12},{8,0},{12,4},{16,24},{20,28},{24,16},{28,20},{1,9},{5... | collective-permute-start | bytes 688136 | tf_op jit(solution)/shard_map/ppermute | solution.py:66
  120.6 10.6 %collective-permute-start.23 = (bf16[128,896]{1,0:T(8,128)(2,1)S(1)}, bf16[128,896]{1,0:T(8,128)(2,1)S(1)}, u32[]{:S(2)}, u32[]{:S(2)}) collective-permute-start(bf16[128,896]{1,0:T(8,128)(2,1)S(1)} %shard_map.150.refs_2_.refs_0_), channel_id=1, source_target_pairs={{0,4},{4,0},{8,12},{12,8},{16,20},{20,16},{24,28},{28,24},{1,5},{5... | collective-permute-start | bytes 688136 | tf_op jit(solution)/shard_map/ppermute | solution.py:66
  121.2 5.2 %collective-permute-start.18 = (bf16[32,896]{1,0:T(8,128)(2,1)S(1)}, bf16[32,896]{1,0:T(8,128)(2,1)S(1)}, u32[]{:S(2)}, u32[]{:S(2)}) collective-permute-start(bf16[32,896]{1,0:T(8,128)(2,1)S(1)} %shard_map.147.refs_2_.refs_0_), channel_id=1, source_target_pairs={{0,16},{4,20},{8,24},{12,28},{16,0},{20,4},{24,8},{28,12},{1,17},{... | collective-permute-start | bytes 172040 | tf_op jit(solution)/shard_map/ppermute | solution.py:66
  124.0 7.0 %collective-permute-start.17 = (bf16[32,1792]{1,0:T(8,128)(2,1)S(1)}, bf16[32,1792]{1,0:T(8,128)(2,1)S(1)}, u32[]{:S(2)}, u32[]{:S(2)}) collective-permute-start(bf16[32,1792]{1,0:T(8,128)(2,1)S(1)} %get-tuple-element.59.refs_2_), channel_id=1, source_target_pairs={{0,16},{4,20},{8,24},{12,28},{16,0},{20,4},{24,8},{28,12},{1,17},{... | collective-permute-start | bytes 344072 | tf_op jit(solution)/shard_map/ppermute | solution.py:66
  126.4 5.7 %collective-permute-start.22 = (bf16[64,896]{1,0:T(8,128)(2,1)S(1)}, bf16[64,896]{1,0:T(8,128)(2,1)S(1)}, u32[]{:S(2)}, u32[]{:S(2)}) collective-permute-start(bf16[64,896]{1,0:T(8,128)(2,1)S(1)} %shard_map.151.refs_3_.refs_0_), channel_id=1, source_target_pairs={{0,8},{4,12},{8,0},{12,4},{16,24},{20,28},{24,16},{28,20},{1,9},{5... | collective-permute-start | bytes 344072 | tf_op jit(solution)/shard_map/ppermute | solution.py:66
  132.1 13.1 %collective-permute-start.26 = (bf16[128,896]{1,0:T(8,128)(2,1)S(1)}, bf16[128,896]{1,0:T(8,128)(2,1)S(1)}, u32[]{:S(2)}, u32[]{:S(2)}) collective-permute-start(bf16[128,896]{1,0:T(8,128)(2,1)S(1)} %shard_map.155.refs_2_.refs_0_), channel_id=1, source_target_pairs={{0,4},{4,0},{8,12},{12,8},{16,20},{20,16},{24,28},{28,24},{1,5},{5... | collective-permute-start | bytes 688136 | tf_op jit(solution)/shard_map/ppermute | solution.py:66
  133.4 6.2 %collective-permute-start.21 = (bf16[32,896]{1,0:T(8,128)(2,1)S(1)}, bf16[32,896]{1,0:T(8,128)(2,1)S(1)}, u32[]{:S(2)}, u32[]{:S(2)}) collective-permute-start(bf16[32,896]{1,0:T(8,128)(2,1)S(1)} %shard_map.152.refs_2_.refs_0_), channel_id=1, source_target_pairs={{0,16},{4,20},{8,24},{12,28},{16,0},{20,4},{24,8},{28,12},{1,17},{... | collective-permute-start | bytes 172040 | tf_op jit(solution)/shard_map/ppermute | solution.py:66
  137.3 7.7 %collective-permute-start.20 = (bf16[32,1792]{1,0:T(8,128)(2,1)S(1)}, bf16[32,1792]{1,0:T(8,128)(2,1)S(1)}, u32[]{:S(2)}, u32[]{:S(2)}) collective-permute-start(bf16[32,1792]{1,0:T(8,128)(2,1)S(1)} %get-tuple-element.63.refs_3_), channel_id=1, source_target_pairs={{0,16},{4,20},{8,24},{12,28},{16,0},{20,4},{24,8},{28,12},{1,17},{... | collective-permute-start | bytes 344072 | tf_op jit(solution)/shard_map/ppermute | solution.py:66
  139.5 7.3 %collective-permute-start.25 = (bf16[64,896]{1,0:T(8,128)(2,1)S(1)}, bf16[64,896]{1,0:T(8,128)(2,1)S(1)}, u32[]{:S(2)}, u32[]{:S(2)}) collective-permute-start(bf16[64,896]{1,0:T(8,128)(2,1)S(1)} %shard_map.156.refs_3_.refs_0_), channel_id=1, source_target_pairs={{0,8},{4,12},{8,0},{12,4},{16,24},{20,28},{24,16},{28,20},{1,9},{5... | collective-permute-start | bytes 344072 | tf_op jit(solution)/shard_map/ppermute | solution.py:66
  146.9 8.2 %collective-permute-start.28 = (bf16[128,896]{1,0:T(8,128)(2,1)S(1)}, bf16[128,896]{1,0:T(8,128)(2,1)S(1)}, u32[]{:S(2)}, u32[]{:S(2)}) collective-permute-start(bf16[128,896]{1,0:T(8,128)(2,1)S(1)} %shard_map.159.refs_2_.refs_0_), channel_id=1, source_target_pairs={{0,4},{4,0},{8,12},{12,8},{16,20},{20,16},{24,28},{28,24},{1,5},{5... | collective-permute-start | bytes 688136 | tf_op jit(solution)/shard_map/ppermute | solution.py:66
  147.6 5.4 %collective-permute-start.24 = (bf16[32,896]{1,0:T(8,128)(2,1)S(1)}, bf16[32,896]{1,0:T(8,128)(2,1)S(1)}, u32[]{:S(2)}, u32[]{:S(2)}) collective-permute-start(bf16[32,896]{1,0:T(8,128)(2,1)S(1)} %shard_map.157.refs_4_.refs_0_), channel_id=1, source_target_pairs={{0,16},{4,20},{8,24},{12,28},{16,0},{20,4},{24,8},{28,12},{1,17},{... | collective-permute-start | bytes 172040 | tf_op jit(solution)/shard_map/ppermute | solution.py:66
  153.0 4.9 %collective-permute-start.27 = (bf16[64,896]{1,0:T(8,128)(2,1)S(1)}, bf16[64,896]{1,0:T(8,128)(2,1)S(1)}, u32[]{:S(2)}, u32[]{:S(2)}) collective-permute-start(bf16[64,896]{1,0:T(8,128)(2,1)S(1)} %shard_map.160.refs_4_.refs_0_), channel_id=1, source_target_pairs={{0,8},{4,12},{8,0},{12,4},{16,24},{20,28},{24,16},{28,20},{1,9},{5... | collective-permute-start | bytes 344072 | tf_op jit(solution)/shard_map/ppermute | solution.py:66
  155.0 16.6 %copy-start.1 = (bf16[4096,256]{1,0:T(8,128)(2,1)S(1)}, bf16[4096,256]{1,0:T(8,128)(2,1)}, u32[]{:S(2)}) copy-start(bf16[4096,256]{1,0:T(8,128)(2,1)} %param.18) | copy-start | bytes 6291460
  157.9 6.1 %collective-permute-start.29 = (bf16[128,896]{1,0:T(8,128)(2,1)S(1)}, bf16[128,896]{1,0:T(8,128)(2,1)S(1)}, u32[]{:S(2)}, u32[]{:S(2)}) collective-permute-start(bf16[128,896]{1,0:T(8,128)(2,1)S(1)} %shard_map.162.refs_0_.refs_4_), channel_id=1, source_target_pairs={{0,4},{4,0},{8,12},{12,8},{16,20},{20,16},{24,28},{28,24},{1,5},{5... | collective-permute-start | bytes 688136 | tf_op jit(solution)/shard_map/ppermute | solution.py:66
  165.1 1.4 collective-permute-start.30
  166.6 4.3 %collective-permute-start.31 = (bf16[64,512]{1,0:T(8,128)(2,1)S(1)}, bf16[64,512]{1,0:T(8,128)(2,1)S(1)}, u32[]{:S(2)}, u32[]{:S(2)}) collective-permute-start(bf16[64,512]{1,0:T(8,128)(2,1)S(1)} %dynamic-slice_convert_fusion), channel_id=1, source_target_pairs={{0,2},{1,3},{2,0},{3,1},{4,6},{5,7},{6,4},{7,5},{8,10},{9,11},{10,... | collective-permute-start | bytes 196616 | tf_op jit(solution)/shard_map/ppermute | solution.py:97

commit v3 on v2

v3 whole, which is shorter than its diff:
```python
import math

import jax
import jax.numpy as jnp
from jax import lax
from jax.experimental import pallas as pl
from jax.experimental.pallas import tpu as pltpu
from jax.sharding import PartitionSpec as P

MODEL_WIDTH = 4096
WINDOW = 512
SINKS = 4


EPS = 1e-05
THETA = 10000.0
JOINED = 4
SPLIT = 2
FETCH_VMEM = 32
EARLY_ROWS = (0, 128)
MIX_COST = 0
ATTENTION_VMEM = 56 * 1024 * 1024


def rotary_tables(places, head_size):
    half = head_size // 2
    freqs = jnp.exp(jnp.arange(half, dtype=jnp.float32) * (-2.0 * math.log(THETA) / head_size))
    angles = places.astype(jnp.float32)[:, None] * freqs[None, :]
    cosine, sine = jnp.cos(angles), jnp.sin(angles)
    return jnp.concatenate([cosine, cosine], axis=1), jnp.concatenate([-sine, sine], axis=1)


def attention(tokens, gain, weights, caches, tables, limits, heads_here, head_size):
    pieces, rows, depth = tokens.shape
    query_weight, key_matrix, value_matrix = weights
    keys, values = caches
    slots = keys.shape[2]
    heads = query_weight.shape[1] // head_size
    query_group = heads // heads_here
    members = min(rows, max(1, 128 // heads))
    lanes = members * heads
    factor = 1.0 / math.sqrt(head_size)

    def body(
        tokens_ref,
        gain_ref,
        query_far,
        key_far,
        value_far,
        keys_far,
        values_far,
        cosine_ref,
        sine_ref,
        limits_ref,
        out_ref,
        flat_ref,
        query_rows,
        key_rows,
        value_rows,
        mixed_rows,
        query_ref,
        key_ref,
        value_ref,
        keys_ref,
        values_ref,
        weight_sems,
        cache_sems,
    ):
        def weight_copies(piece):
            span = pl.ds(piece * depth, depth)
            return [
                pltpu.make_async_copy(far.at[span], near.at[span], weight_sems.at[piece, i])
                for i, (far, near) in enumerate(
                    ((query_far, query_ref), (key_far, key_ref), (value_far, value_ref))
                )
            ]

        def cache_copy(group, which):
            far, near = ((keys_far, keys_ref), (values_far, values_ref))[which]
            span = pl.ds(group * members, members)
            return pltpu.make_async_copy(far.at[span], near.at[span], cache_sems.at[group, which])

        for piece in range(pieces):
            for copy in weight_copies(piece):
                copy.start()
        for which in range(2):
            for group in range(rows // members):
                cache_copy(group, which).start()
        squares = jnp.zeros((rows, 1), jnp.float32)
        for piece in range(pieces):
            part = tokens_ref[piece].astype(jnp.float32)
            squares = squares + jnp.sum(part * part, axis=1, keepdims=True)
        scale = 1.0 / jnp.sqrt(squares / MODEL_WIDTH + EPS)
        sums = [None, None, None]
        for piece in range(pieces):
            span = slice(piece * depth, (piece + 1) * depth)
            part = tokens_ref[piece].astype(jnp.float32)
            normed = (part * scale * gain_ref[:, span]).astype(jnp.bfloat16)
            for copy in weight_copies(piece):
                copy.wait()
            for i, weight_ref in enumerate((query_ref, key_ref, value_ref)):
                product = jnp.dot(normed, weight_ref[span], preferred_element_type=jnp.float32)
                sums[i] = product if sums[i] is None else sums[i] + product
        cosine, sine = cosine_ref[...], sine_ref[...]

        def turned(value):
            swapped = jnp.concatenate(
                [value[:, head_size // 2 :], value[:, : head_size // 2]], axis=1
            )
            return (value * cosine + swapped * sine).astype(jnp.bfloat16).astype(jnp.float32)

        def put(ref, head, value):
            for group in range(rows // members):
                ref[pl.ds(group * lanes + head, members, stride=heads), :] = value[
                    group * members : (group + 1) * members
                ]

        for head in range(heads):
            own = head // query_group
            put(query_rows, head, turned(sums[0][:, head * head_size : (head + 1) * head_size]))
            if head % query_group == 0:
                new_key = turned(sums[1][:, own * head_size : (own + 1) * head_size])
                new_value = sums[2][:, own * head_size : (own + 1) * head_size]
                new_value = new_value.astype(jnp.bfloat16).astype(jnp.float32)
            put(key_rows, head, new_key)
            put(value_rows, head, new_value)
        slot = lax.broadcasted_iota(jnp.int32, (slots, lanes), 0)
        owner = lax.broadcasted_iota(jnp.int32, (head_size, lanes), 1) // query_group
        kept = []
        for group in range(rows // members):
            mine = slice(group * lanes, (group + 1) * lanes)
            query_columns = query_rows[mine].T
            own_score = (
                jnp.sum(query_columns * key_rows[mine].T, axis=0, keepdims=True) * factor
            )
            narrow = query_columns.astype(jnp.bfloat16)
            cache_copy(group, 0).wait()
            cut = slots // SPLIT
            parts = [None] * SPLIT
            for first in range(0, members, JOINED):
                pairs = [
                    (member, g)
                    for member in range(first, min(first + JOINED, members))
                    for g in range(heads_here)
                ]
                right = jnp.concatenate(
                    [
                        jnp.where(owner == member * heads_here + g, narrow, jnp.zeros_like(narrow))
                        for member, g in pairs
                    ],
                    axis=0,
                )
                for i in range(SPLIT):
                    left = jnp.concatenate(
                        [
                            keys_ref[group * members + member, g, i * cut : (i + 1) * cut]
                            for member, g in pairs
                        ],
                        axis=1,
                    )
                    product = jnp.dot(left, right, preferred_element_type=jnp.float32)
                    parts[i] = product if parts[i] is None else parts[i] + product
            scores = jnp.concatenate(parts, axis=0)
            lane_member = lax.broadcasted_iota(jnp.int32, (1, lanes), 1) // heads
            limit = jnp.zeros((1, lanes), jnp.int32)
            for member in range(members):
                limit = jnp.where(lane_member == member, limits_ref[group * members + member], limit)
            allowed = (slot < limit) & ((slot < SINKS) | (slot > limit - WINDOW))
            scores = jnp.where(allowed, scores * factor, -1e30)
            peak = jnp.maximum(jnp.max(scores, axis=0, keepdims=True), own_score)
            expo = jnp.where(allowed, jnp.exp(scores - peak), 0.0)
            own_expo = jnp.exp(own_score - peak)
            inverse = 1.0 / (jnp.sum(expo, axis=0, keepdims=True) + own_expo)
            shares = (expo * inverse).T
            own_share = (own_expo * inverse).astype(jnp.bfloat16).astype(jnp.float32)
            own_part = (
                jnp.broadcast_to(own_share, (head_size, lanes)).T * value_rows[mine]
            )
            kept.append((shares, own_part))
        for group, (shares, own_part) in enumerate(kept):
            cache_copy(group, 1).wait()
            for member in range(members):
                request = group * members + member
                span = slice(member * heads, (member + 1) * heads)
                wide = jnp.dot(
                    shares[span].astype(jnp.bfloat16),
                    jnp.concatenate([values_ref[request, g] for g in range(heads_here)], axis=1),
                    preferred_element_type=jnp.float32,
                )
                which = lax.broadcasted_iota(jnp.int32, (heads, head_size), 0) // query_group
                mixed = wide[:, :head_size]
                for g in range(1, heads_here):
                    mixed = jnp.where(which == g, wide[:, g * head_size : (g + 1) * head_size], mixed)
                mixed_rows[group * lanes + member * heads : group * lanes + (member + 1) * heads] = (
                    mixed + own_part[span]
                )
        for head in range(heads):
            for group in range(rows // members):
                flat_ref[group * members : (group + 1) * members, :] = mixed_rows[
                    pl.ds(group * lanes + head, members, stride=heads), :
                ]
            out_ref[:, head * head_size : (head + 1) * head_size] = flat_ref[...].astype(
                jnp.bfloat16
            )

    tall = pltpu.VMEM((rows * heads, head_size), jnp.float32)
    near = pl.BlockSpec(memory_space=pltpu.VMEM)
    return pl.pallas_call(
        body,
        out_shape=array((rows, heads * head_size), jnp.bfloat16),
        in_specs=[near, near, *[HBM] * 5, near, near, SCALARS],
        out_specs=pl.BlockSpec(memory_space=pltpu.VMEM),
        scratch_shapes=[
            pltpu.VMEM((rows, head_size), jnp.float32),
            *[tall] * 4,
            *[pltpu.VMEM(v.shape, v.dtype) for v in (*weights, *caches)],
            pltpu.SemaphoreType.DMA((pieces, 3)),
            pltpu.SemaphoreType.DMA((rows // members, 2)),
        ],
        compiler_params=pltpu.CompilerParams(vmem_limit_bytes=ATTENTION_VMEM),
    )(
        tokens,
        gain.reshape(1, -1),
        *weights,
        *caches,
        *tables,
        limits,
    )


def bit_reverse(value, bits):
    result = 0
    for bit in range(bits):
        result |= ((value >> bit) & 1) << (bits - 1 - bit)
    return result


def exchange(value, size, bit):
    return lax.ppermute(value, "req", [(i, i ^ (1 << bit)) for i in range(size)])


def local_spot(place, block, size):
    bits = size.bit_length() - 1
    other = place ^ block
    spot = jnp.int32(0)
    for bit in range(bits):
        spot = spot | (((other >> bit) & 1) << (bits - 1 - bit))
    return spot


def kv_exchange(value, size, bit):
    return lax.ppermute(value, "kv", [(i, i ^ (1 << bit)) for i in range(size)])


class Chain:
    def __init__(self, token):
        self.token = token

    def run(self, body, outs, ins, in_specs=None, after=(), scratch=(), vmem=32, cost=0):
        specs = list(in_specs or [None] * len(ins))
        specs = [pl.BlockSpec(memory_space=pltpu.VMEM) if v is None else v for v in specs]
        count = len(ins)
        unread = [self.token, *after]

        def kernel(*refs):
            body(*refs[:count], *refs[count + len(unread) :])

        results = pl.pallas_call(
            kernel,
            out_shape=outs,
            in_specs=[*specs, *[pl.BlockSpec(memory_space=pl.ANY)] * len(unread)],
            out_specs=[pl.BlockSpec(memory_space=pltpu.VMEM)] * len(outs),
            scratch_shapes=scratch,
            compiler_params=pltpu.CompilerParams(vmem_limit_bytes=vmem * 1024 * 1024),
            cost_estimate=pl.CostEstimate(flops=0, bytes_accessed=cost, transcendentals=0),
        )(*ins, *unread)
        self.token = results[0]
        return results


SCALARS = pl.BlockSpec(memory_space=pltpu.SMEM)
FAR = pl.BlockSpec(memory_space=pl.ANY)
HBM = pl.BlockSpec(memory_space=pltpu.HBM)


def array(shape, dtype):
    return jax.ShapeDtypeStruct(shape, dtype)


def corner(value):
    return value.reshape(-1, value.shape[-1])[:16, :128]


def tie(value, *after):
    def body(*refs):
        del refs

    return pl.pallas_call(
        body,
        out_shape=array(value.shape, value.dtype),
        in_specs=[FAR] * (1 + len(after)),
        out_specs=FAR,
        input_output_aliases={0: 0},
        cost_estimate=pl.CostEstimate(flops=0, bytes_accessed=0, transcendentals=0),
    )(value, *after)


def fetch(chain, places, features, output_weight, residual_in, req_size):
    total, columns = residual_in.shape
    bits = req_size.bit_length() - 1
    block = total // req_size

    def body(places_ref, weight_far, residual_ref, weight_ref, ordered_ref, sem):
        start = pl.multiple_of(places_ref[2] * features, features)
        copy = pltpu.make_async_copy(weight_far.at[pl.ds(start, features)], weight_ref, sem)
        copy.start()
        for spot in range(req_size):
            first = pl.multiple_of((places_ref[0] ^ bit_reverse(spot, bits)) * block, block)
            ordered_ref[spot * block : (spot + 1) * block] = residual_ref[pl.ds(first, block)]
        copy.wait()

    return chain.run(
        body,
        [
            array((features, columns), output_weight.dtype),
            array(residual_in.shape, residual_in.dtype),
        ],
        [places, output_weight, residual_in],
        [SCALARS, HBM, None],
        scratch=[pltpu.SemaphoreType.DMA(())],
        vmem=FETCH_VMEM,
    )


def mix(chain, rows, weight, req_size):
    block = rows.shape[0] // req_size
    back = local_from_pair(req_size, 0)

    def body(rows_ref, weight_ref, out_ref):
        left = jnp.concatenate([rows_ref[n * block : (n + 1) * block] for n in back], axis=0)
        out_ref[...] = jnp.dot(
            left, weight_ref[...], preferred_element_type=jnp.float32
        ).astype(jnp.bfloat16)

    out = array((rows.shape[0], weight.shape[1]), jnp.bfloat16)
    return chain.run(body, [out], [rows, weight], cost=MIX_COST)[0]


def half_sum(chain, places, rows, other):
    half, columns = rows.shape[0] // 2, rows.shape[1]

    def body(places_ref, rows_ref, other_ref, send_ref, part_ref):
        span = pl.ds(pl.multiple_of(places_ref[1] * half, half), half)
        part = rows_ref[span].astype(jnp.float32) + other_ref[span].astype(jnp.float32)
        part_ref[...] = part
        send_ref[...] = part.astype(jnp.bfloat16)

    return chain.run(
        body,
        [array((half, columns), jnp.bfloat16), array((half, columns), jnp.float32)],
        [places, rows, other],
        [SCALARS, None, None],
        cost=MIX_COST,
    )


def relay(chain, value):
    def body(value_ref, out_ref):
        out_ref[...] = value_ref[...]

    return chain.run(body, [array(value.shape, value.dtype)], [value])[0]


def next_sum(chain, part, other):
    def body(part_ref, other_ref, send_ref, sum_ref):
        total = part_ref[...] + other_ref[...].astype(jnp.float32)
        sum_ref[...] = total
        send_ref[...] = total.astype(jnp.bfloat16)

    return chain.run(
        body, [array(part.shape, jnp.bfloat16), array(part.shape, jnp.float32)], [part, other]
    )


def middle_half(chain, places, mixed, residual_rows, gain):
    half, columns = mixed.shape

    def body(places_ref, mixed_ref, residual_ref, gain_ref, out_ref):
        span = pl.ds(pl.multiple_of(places_ref[1] * half, half), half)
        middle = residual_ref[span].astype(jnp.float32) + mixed_ref[...].astype(jnp.float32)
        out_ref[:, :columns] = (middle * gain_ref[...]).astype(jnp.bfloat16)
        out_ref[:, columns:] = jnp.broadcast_to(
            jnp.sum(middle * middle, axis=1, keepdims=True), (half, 128)
        ).astype(jnp.bfloat16)

    return chain.run(
        body,
        [array((half, columns + 128), jnp.bfloat16)],
        [places, mixed, residual_rows, gain],
        [SCALARS, None, None, None],
    )[0]


def middle_rows(chain, places, mixed, other, residual_rows, gain):
    half, columns = mixed.shape
    rows = 2 * half

    def body(places_ref, mixed_ref, other_ref, residual_ref, gain_ref, scaled_ref, middle_ref, squares_ref):
        for mine, ref in ((0, mixed_ref), (1, other_ref)):
            first = places_ref[1] if mine == 0 else 1 - places_ref[1]
            span = pl.ds(pl.multiple_of(first * half, half), half)
            middle = residual_ref[span].astype(jnp.float32) + ref[...].astype(jnp.float32)
            middle_ref[span] = middle
            scaled_ref[span] = (middle * gain_ref[...]).astype(jnp.bfloat16)
            squares_ref[span] = jnp.broadcast_to(
                jnp.sum(middle * middle, axis=1, keepdims=True), (half, 128)
            )

    return chain.run(
        body,
        [
            array((rows, columns), jnp.bfloat16),
            array((rows, columns), jnp.float32),
            array((rows, 128), jnp.float32),
        ],
        [places, mixed, other, residual_rows, gain],
        [SCALARS, None, None, None, None],
    )


def project(chain, scaled, squares, gate, up, start, width):
    half = scaled.shape[0] // 2

    def body(scaled_ref, gate_ref, up_ref, squares_ref, send_ref, keep_ref):
        for first, out_ref in ((half, send_ref), (0, keep_ref)):
            left = scaled_ref[first : first + half]
            for i, weight_ref in enumerate((gate_ref, up_ref)):
                out_ref[:, i * width : (i + 1) * width] = jnp.dot(
                    left, weight_ref[:, start : start + width], preferred_element_type=jnp.float32
                ).astype(jnp.bfloat16)

            out_ref[:, 2 * width :] = squares_ref[first : first + half].astype(jnp.bfloat16)

    out = array((half, 2 * width + 128), jnp.bfloat16)
    return chain.run(body, [out, out], [scaled, gate, up, squares])


def pair_order(size, pair):
    bits = size.bit_length() - 1
    sums = [bit for bit in range(bits) if bit != pair]
    spots = []
    for n in range(size):
        spot = (n & 1) << (bits - 1 - pair)
        for i, bit in enumerate(sums):
            spot |= ((n >> (bits - 1 - i)) & 1) << (bits - 1 - bit)
        spots.append(spot)
    return spots


def local_from_pair(size, pair):
    order = pair_order(size, pair)
    return [order.index(spot) for spot in range(size)]


def project_pair(chain, places, scaled, squares, far, got, gate, up, pair, area, start, skip, width, req_size):
    rows, depth = scaled.shape
    half, block = rows // 2, rows // req_size
    order = pair_order(req_size, pair)
    flip = 1 << (req_size.bit_length() - 2 - pair)
    cut = got[0].shape[0] - depth
    total = 2 * width + (0 if squares is None else 128)

    def body(places_ref, scaled_ref, far_ref, away_ref, *refs):
        early_ref, late_ref = refs[:2]
        weight_fars = refs[2:4]
        send_ref, keep_ref, all_far, weights, sems = refs[-5:]
        mine = lax.rem(places_ref[0] // (1 << pair), 2)
        columns = pl.ds(pl.multiple_of(start + mine * area + skip, 128), width)
        copies = [
            pltpu.make_async_copy(weight_fars[i].at[:, columns], weights.at[i], sems.at[i])
            for i in range(2)
        ]
        for copy in copies:
            copy.start()
        for away, ref in ((0, far_ref), (1, away_ref)):
            first = 1 - places_ref[1] if away else places_ref[1]
            all_far[pl.ds(pl.multiple_of(first * half, half), half)] = ref[...]
        outs = ((order[req_size // 2 :], send_ref), (order[: req_size // 2], keep_ref))

        def take(ref, spots, span, change=0):
            return jnp.concatenate(
                [
                    ref[(spot ^ change) * block : ((spot ^ change) + 1) * block, span]
                    for spot in spots
                ],
                axis=0,
            )

        others = []
        for spots, out_ref in outs:
            for i in range(2):
                spans = [(early_ref, 0, 0, depth)]
                if i == 1:
                    spans = [(early_ref, depth, 0, cut), (late_ref, 0, cut, depth)]
                product = None
                for ref, top, begin, end in spans:
                    if end > begin:
                        part = jnp.dot(
                            take(all_far, spots, slice(begin, end), flip),
                            ref[top : top + end - begin, skip : skip + width],
                            preferred_element_type=jnp.float32,
                        )
                        product = part if product is None else product + part
                others.append(product)
            if squares is not None:
                out_ref[:, 2 * width :] = (
                    take(refs[4], spots, slice(0, 128))
                    + take(all_far, spots, slice(depth, depth + 128), flip).astype(jnp.float32)
                ).astype(jnp.bfloat16)
        for copy in copies:
            copy.wait()
        for j, (spots, out_ref) in enumerate(outs):
            for i in range(2):
                near = jnp.dot(
                    take(scaled_ref, spots, slice(0, depth)),
                    weights[i],
                    preferred_element_type=jnp.float32,
                )
                out_ref[:, i * width : (i + 1) * width] = (near + others[2 * j + i]).astype(
                    jnp.bfloat16
                )

    ins = [places, scaled, *far, *got, gate, up] + ([] if squares is None else [squares])
    specs = [SCALARS, None, None, None, None, None, HBM, HBM] + [None] * (len(ins) - 8)
    out = array((half, total), jnp.bfloat16)
    return chain.run(
        body,
        [out, out],
        ins,
        specs,
        scratch=[
            pltpu.VMEM((rows, depth + 128), jnp.bfloat16),
            pltpu.VMEM((2, depth, width), gate.dtype),
            pltpu.SemaphoreType.DMA((2,)),
        ],
    )


def add_halve(chain, other, kept):
    half = kept.shape[0] // 2

    def body(other_ref, kept_ref, send_ref, keep_ref):
        for start, out_ref in ((half, send_ref), (0, keep_ref)):
            rows = slice(start, start + half)
            out_ref[...] = (
                other_ref[rows].astype(jnp.float32) + kept_ref[rows].astype(jnp.float32)
            ).astype(jnp.bfloat16)

    out = array((half, kept.shape[1]), jnp.bfloat16)
    return chain.run(body, [out, out], [other, kept])


def activate(chain, other, kept, inverse, width):
    rows = kept.shape[0]
    first = inverse is None

    def body(other_ref, kept_ref, *refs):
        def total(columns):
            return other_ref[:, columns].astype(jnp.float32) + kept_ref[:, columns].astype(
                jnp.float32
            )

        if first:
            hidden_ref, inverse_ref = refs
            scale = 1.0 / jnp.sqrt(total(slice(2 * width, 2 * width + 128)) / MODEL_WIDTH + EPS)
            inverse_ref[...] = scale
        else:
            scale_ref, hidden_ref = refs
            scale = scale_ref[:rows]
        scale = scale[:, :1]
        gate = total(slice(0, width)) * scale
        up = total(slice(width, 2 * width)) * scale
        hidden_ref[...] = (gate / (1.0 + jnp.exp(-gate)) * up).astype(jnp.bfloat16)

    outs = [array((rows, width), jnp.bfloat16)]
    ins = [other, kept]
    if first:
        outs.append(array((rows, 128), jnp.float32))
    else:
        ins.append(inverse)
    results = chain.run(body, outs, ins)
    return results if first else (results[0], inverse)


def join(chain, kept, other, after=()):
    rows = kept.shape[0]

    def body(kept_ref, other_ref, out_ref):
        out_ref[:rows] = kept_ref[...]
        out_ref[rows:] = other_ref[...]

    return chain.run(
        body, [array((2 * rows, kept.shape[1]), kept.dtype)], [kept, other], after=after
    )[0]


def lower(chain, places, kept, other, down, pair, area, start, skip, width, carried, req_size):
    columns = down.shape[1]
    paired = pair is not None
    rows = kept.shape[0] * (1 if paired else 2)
    half, block = rows // 2, rows // req_size
    back = local_from_pair(req_size, pair) if paired else None

    def body(places_ref, kept_ref, other_ref, down_ref, *refs):
        out_ref = refs[-1]

        def product(left, first):
            return jnp.dot(
                left, down_ref[pl.ds(first, width)], preferred_element_type=jnp.float32
            )

        def take(ref, flip):
            return jnp.concatenate(
                [ref[(n ^ flip) * block : ((n ^ flip) + 1) * block] for n in back], axis=0
            )

        if paired:
            mine = lax.rem(places_ref[0] // (1 << pair), 2)
            total = product(take(kept_ref, 0), pl.multiple_of(start + mine * area + skip, 128))
            total = total + product(
                take(other_ref, 1), pl.multiple_of(start + (1 - mine) * area + skip, 128)
            )
            out_ref[...] = total if carried is None else refs[0][...] + total
        else:
            for first, ref in ((0, kept_ref), (half, other_ref)):
                span = slice(first, first + half)
                total = product(ref[...], start)
                out_ref[span] = total if carried is None else refs[0][span] + total

    ins = [places, kept, other, down] + ([] if carried is None else [carried])
    return chain.run(
        body, [array((rows, columns), jnp.float32)], ins, [SCALARS] + [None] * (len(ins) - 1)
    )[0]


def split_for_kv(chain, total, places, req_size, kv_size):
    rows, columns = total.shape
    bits = req_size.bit_length() - 1
    block = rows // req_size
    per = req_size // kv_size

    def body(places_ref, total_ref, send_ref, keep_ref):
        req_place, mine = places_ref[0], places_ref[1]
        for spot in range(req_size):
            actual = req_place ^ bit_reverse(spot, bits)
            owner = actual // per
            start = pl.multiple_of(((owner // 2) * per + actual % per) * block, block)
            value = total_ref[spot * block : (spot + 1) * block].astype(jnp.bfloat16)

            @pl.when(owner % 2 == mine)
            def _():
                keep_ref[pl.ds(start, block)] = value

            @pl.when(owner % 2 != mine)
            def _():
                send_ref[pl.ds(start, block)] = value

    out = array((rows // 2, columns), jnp.bfloat16)
    return chain.run(
        body,
        [out, out],
        [places, total],
        [SCALARS, None],
    )


class Chunk:
    def __init__(self, pair, start, area, skip, width, bits):
        self.pair, self.start, self.area, self.skip, self.width = pair, start, area, skip, width
        self.sums = [bit for bit in range(bits) if bit != pair]
        self.gathers = [*reversed(self.sums), *([] if pair is None else [pair])]
        self.kept = self.moving = None


def areas_of(columns):
    tiles = columns // 128
    return tiles // 4 * 128, tiles // 4 * 128


def plan(columns, bits):
    first, second = areas_of(columns)
    rest = columns - 2 * first - 2 * second
    chunks = [Chunk(0, 0, first, 0, first, bits), Chunk(1, 2 * first, second, 0, second, bits)]
    if rest:
        chunks.insert(0, Chunk(None, columns - rest, 0, 0, rest, bits))
    stages = 2 * bits + 1
    tasks = [
        (i, stage)
        for stage in range(stages)
        for i, chunk in enumerate(chunks)
        if stage <= len(chunk.sums) + len(chunk.gathers)
    ]
    return chunks, tasks


def feed_forward(chain, places, scaled, squares, far_parts, gots, gate, up, down, req_size, kv_size):
    bits = req_size.bit_length() - 1
    total = None
    inverses, fars = {}, {}
    chunks, tasks = plan(gate.shape[1], bits)
    for i, stage in tasks:
        chunk = chunks[i]
        pair, sums, gathers = chunk.pair, chunk.sums, chunk.gathers
        if stage == 0:
            if pair is not None:
                if pair not in fars:
                    far = relay(chain, far_parts[pair])
                    fars[pair] = (far, kv_exchange(far, kv_size, 0))
                send, chunk.kept = project_pair(
                    chain,
                    places,
                    scaled,
                    squares if chunk.skip == 0 else None,
                    fars[pair],
                    gots[pair],
                    gate,
                    up,
                    pair,
                    chunk.area,
                    chunk.start,
                    chunk.skip,
                    chunk.width,
                    req_size,
                )
            else:
                send, chunk.kept = project(
                    chain, scaled, squares, gate, up, chunk.start, chunk.width
                )
            chunk.moving = exchange(send, req_size, sums[0])
        elif stage < len(sums):
            send, chunk.kept = add_halve(chain, chunk.moving, chunk.kept)
            chunk.moving = exchange(send, req_size, sums[stage])
        elif stage == len(sums):
            chunk.kept, inverses[pair] = activate(
                chain,
                chunk.moving,
                chunk.kept,
                inverses.get(pair),
                chunk.width,
            )
            chunk.moving = exchange(chunk.kept, req_size, gathers[0])
        elif stage < len(sums) + len(gathers):
            chunk.kept = join(chain, chunk.kept, chunk.moving)
            chunk.moving = exchange(chunk.kept, req_size, gathers[stage - len(sums)])
        else:
            total = lower(
                chain,
                places,
                chunk.kept,
                chunk.moving,
                down,
                pair,
                chunk.area,
                chunk.start,
                chunk.skip,
                chunk.width,
                total,
                req_size,
            )
    return total


def shards(
    residual_in,
    attn_gain,
    query_weight,
    key_matrix,
    value_matrix,
    key_cache,
    cached_values,
    cache_lengths,
    positions,
    output_weight,
    mlp_gain,
    gate_weight,
    up_weight,
    down_weight,
):
    req_size = lax.axis_size("req")
    kv_size = lax.axis_size("kv")
    req_place = lax.axis_index("req")
    kv_place = lax.axis_index("kv")
    local_rows = residual_in.shape[0] // req_size
    heads_here, head_size = key_cache.shape[1], key_cache.shape[3]
    tokens = lax.all_to_all(
        residual_in.reshape(req_size, local_rows, -1), "req", split_axis=0, concat_axis=0
    )
    attended_rows = attention(
        tokens,
        attn_gain,
        (query_weight, key_matrix, value_matrix),
        (key_cache, cached_values),
        rotary_tables(positions, head_size),
        cache_lengths,
        heads_here,
        head_size,
    )
    features = attended_rows.shape[1]
    places = jnp.stack([req_place, lax.rem(kv_place, 2), kv_place]).astype(jnp.int32)
    areas = areas_of(gate_weight.shape[1])
    theirs = []
    for pair, area in enumerate(areas):
        first = 2 * sum(areas[:pair]) + (1 - lax.rem(req_place // (1 << pair), 2)) * area
        slices = [lax.dynamic_slice_in_dim(v, first, area, 1) for v in (gate_weight, up_weight)]
        cut = EARLY_ROWS[pair] * gate_weight.shape[0] // 512
        early = jnp.concatenate([slices[0], slices[1][:cut]], axis=0) if cut else slices[0]
        theirs.append((early, slices[1][cut:]))
    start = corner(tokens)
    gots = [
        [exchange(tie(theirs[0][0], start, theirs[0][1], *theirs[1]), req_size, 0)],
        [exchange(tie(theirs[1][0], start), req_size, 1)],
    ]
    chain = Chain(attended_rows)
    output_rows, residual_rows = fetch(
        chain, places, features, output_weight, residual_in, req_size
    )
    gathered = attended_rows
    bits = req_size.bit_length() - 1
    for bit in (0, *reversed(range(1, bits))):
        other = exchange(gathered, req_size, bit)
        gathered = join(chain, gathered, other, [gots[0][0], gots[1][0]] if bit == 0 else [])
        if bit == 0:
            gots[0].append(exchange(tie(theirs[0][1], corner(gathered)), req_size, 0))
    gots[1].append(exchange(tie(theirs[1][1], corner(gathered)), req_size, 1))
    partial_mix = mix(chain, gathered, output_rows, req_size)
    gain = mlp_gain.reshape(1, -1)
    send, part = half_sum(chain, places, partial_mix, kv_exchange(partial_mix, kv_size, 0))
    for bit in range(1, kv_size.bit_length() - 1):
        send, part = next_sum(chain, part, kv_exchange(send, kv_size, bit))
    beside = kv_exchange(send, kv_size, 0)
    near_part = middle_half(chain, places, send, residual_rows, gain)
    far_parts = [exchange(near_part, req_size, pair) for pair in range(2)]
    scaled, middle, squares = middle_rows(chain, places, send, beside, residual_rows, gain)
    gate, up, down = gate_weight, up_weight, down_weight
    total = feed_forward(
        chain, places, scaled, squares, far_parts, gots, gate, up, down, req_size, kv_size
    )
    send, kept = split_for_kv(chain, total, places, req_size, kv_size)
    value = kept.astype(jnp.float32) + kv_exchange(send, kv_size, 0).astype(jnp.float32)
    for bit in reversed(range(1, kv_size.bit_length() - 1)):
        half = value.shape[0] // 2
        mine = lax.rem(kv_place >> bit, 2)
        other = kv_exchange(
            lax.dynamic_slice_in_dim(value, (1 - mine) * half, half, 0).astype(jnp.bfloat16),
            kv_size,
            bit,
        )
        value = lax.dynamic_slice_in_dim(value, mine * half, half, 0) + other.astype(jnp.float32)
    per = req_size // kv_size
    base_rows = jnp.concatenate(
        [
            lax.dynamic_slice_in_dim(
                middle,
                local_spot(req_place, kv_place * per + i, req_size) * local_rows,
                local_rows,
                0,
            )
            for i in range(per)
        ],
        axis=0,
    )
    return (base_rows + value).astype(jnp.bfloat16)


def solution(mesh):
    return jax.shard_map(
        shards,
        mesh=mesh,
        in_specs=(
            P(None, "req"),
            P(),
            P(None, "kv"),
            P(None, "kv"),
            P(None, "kv"),
            P("req", "kv", None, None),
            P("req", "kv", None, None),
            P("req"),
            P("req"),
            P(None, "req"),
            P("req"),
            P("req", "kv"),
            P("req", "kv"),
            P("kv", "req"),
        ),
        out_specs=P("kv", "req"),
        check_vma=False,
    )
```

time: 172 us -> 162 us (0.942)
  Pallas kernels: 6.7 us -> 32.3 us
  matrix products: 23.2 us -> 0 us
  waiting for transfers between devices: 84.5 us -> 71.4 us
  local copies, waits for them, and re-layouts: 4.64 us -> 14.6 us
  starting transfers between devices: 47.3 us -> 40.1 us
  other arithmetic: 4.65 us -> 2.75 us
    pallas_call x29, Pallas kernels: 6.7 us -> 32.3 us  [the longest x1 17.2 us: attention(): pl.pallas_call(body, out_shape=array((rows, heads * head_size), jnp.bfloa...]
    dot_general x10 -> x0, matrix products: 23.2 us -> none  [the longest x2 8.61 us: attend(): jnp.einsum('bgd,bjd->bgj', query_rows, keys, preferred_element_type=jnp.f...]
    ppermute x27 -> x19, starting transfers between devices: 36.5 us -> 29.3 us  [exchange(): return lax.ppermute(value, 'req', [(i, i ^ 1 << bit) for i in range(size)])]
    all_to_all x1, waiting for transfers between devices: 6.83 us -> 0.05 us  [shards(): lax.all_to_all(residual_in.reshape(req_size, local_rows, -1), 'req', spli...]
    ppermute x27 -> x19, waiting for transfers between devices: 66.9 us -> 61.4 us  [exchange(): return lax.ppermute(value, 'req', [(i, i ^ 1 << bit) for i in range(size)])]
    slice x1 -> x5, local copies, waits for them, and re-layouts: 0.03 us -> 4.78 us  [the longest x1 2.01 us: shards(): theirs.append((early, slices[1][cut:]))]
    dynamic_slice x0 -> x2, local copies, waits for them, and re-layouts: none -> 4.73 us  [shards(): lax.dynamic_slice_in_dim(v, first, area, 1)]
    concatenate x3 -> x2, other arithmetic: 0.11 us -> 1.83 us  [the longest x1 1.15 us: shards(): jnp.concatenate([slices[0], slices[1][:cut]], axis=0)]
  transfers between devices with their start and end apart: 33 -> 27, of which waited for: 27 -> 19; matrix products, arithmetic and copies ran while one was open for 1% -> 7% of each run, Pallas kernels for 3% -> 19%
where the time goes in v3:
time: 162 us; the launch traced here: 161 us
  waiting for transfers between devices  71.4 us (44%)
  starting transfers between devices  40.1 us (25%)
  Pallas kernels  32.3 us (20%)
  local copies, waits for them, and re-layouts  14.6 us (9%)
  other arithmetic  2.75 us (2%)
    ppermute x19, waiting for transfers between devices, exchange(): return lax.ppermute(value, 'req', [(i, i ^ 1 << bit) for i in range(size)])  61.4 us
    ppermute x19, starting transfers between devices, exchange(): return lax.ppermute(value, 'req', [(i, i ^ 1 << bit) for i in range(size)])  29.3 us
    pallas_call x1, Pallas kernels, attention(): pl.pallas_call(body, out_shape=array((rows, heads * head_size), jnp.bfloa...  17.2 us
    pallas_call x24, Pallas kernels, run(): pl.pallas_call(kernel, out_shape=outs, in_specs=[*specs, *[pl.BlockSpec(m...  15.1 us
    ppermute x7, waiting for transfers between devices, kv_exchange(): return lax.ppermute(value, 'kv', [(i, i ^ 1 << bit) for i in range(size)])  9.9 us
    all_to_all x1, starting transfers between devices, shards(): lax.all_to_all(residual_in.reshape(req_size, local_rows, -1), 'req', spli...  7.25 us
    unnamed x26, local copies, waits for them, and re-layouts  5.04 us
    dynamic_slice x2, local copies, waits for them, and re-layouts, shards(): lax.dynamic_slice_in_dim(v, first, area, 1)  4.73 us
  transfers between devices with their start and end apart: 27, of which 19 were waited for; matrix products, arithmetic and copies ran while one was open for 7% of the time, Pallas kernels for 19%

profile of v3, /device:TPU:0, one launch (start us, length us, event | category | flops | bytes accessed | tf_op | source)
XLA Modules:
  0.0 161.5 jit_solution(12681056186369060240)
XLA Ops:
  0.0 7.3 %all-to-all-start = ((bf16[8,32,512]{2,1,0:T(8,128)(2,1)}), bf16[8,32,512]{2,1,0:T(8,128)(2,1)S(1)}, u32[]{:S(2)}, u32[]{:S(2)}) async-start(bf16[8,32,512]{2,1,0:T(8,128)(2,1)} %bitcast.7), calls=%async_computation | async-start | bytes 524288 | tf_op jit(solution)/shard_map/all_to_all | solution.py:795
  7.3 1.0 constant_dynamic-slice_fusion
  8.2 2.0 %dynamic-slice.1.refs_4_.refs_0_ = bf16[384,896]{1,0:T(8,128)(2,1)} dynamic-slice(bf16[512,3584]{1,0:T(8,128)(2,1)} %refs_7_.3, s32[]{:T(128)S(6)} %add.48, s32[]{:T(128)S(6)} %select_n.28), dynamic_slice_sizes={384,896} | dynamic-slice | bytes 1376260 | tf_op jit(solution)/shard_map/slice | solution.py:817
  10.2 2.2 %constant_dynamic-slice_fusion.4.refs_2_.refs_0_ = bf16[512,896]{1,0:T(8,128)(2,1)} fusion(bf16[512,3584]{1,0:T(8,128)(2,1)} %refs_7_.3, s32[]{:T(128)S(6)} %select_n.26), kind=kLoop, calls=%fused_computation.14 | loop fusion | bytes 1835012 | tf_op jit(solution)/shard_map/dynamic_slice | solution.py:814
  12.4 2.5 %constant_dynamic-slice_fusion.3 = (bf16[512,896]{1,0:T(8,128)(2,1)S(1)}, bf16[512,896]{1,0:T(8,128)(2,1)}) fusion(bf16[512,3584]{1,0:T(8,128)(2,1)} %refs_6_.3, s32[]{:T(128)S(6)} %select_n.28, s32[]{:T(128)S(6)} %select_n.26), kind=kLoop, calls=%fused_computation.13 | loop fusion | bytes 3670024 | tf_op jit(solution)/shard_map/dynamic_slice | solution.py:814
  15.0 1.2 pad_maximum_fusion.refs_3_.refs_0_
  16.9 2.0 %collective-permute-start.2 = (bf16[640,896]{1,0:T(8,128)(2,1)}, bf16[640,896]{1,0:T(8,128)(2,1)S(1)}, u32[]{:S(2)}, u32[]{:S(2)}) collective-permute-start(bf16[640,896]{1,0:T(8,128)(2,1)} %shard_map.139), channel_id=1, source_target_pairs={{0,8},{4,12},{8,0},{12,4},{16,24},{20,28},{24,16},{28,20},{1,9},{5... | collective-permute-start | bytes 3440648 | tf_op jit(solution)/shard_map/ppermute | solution.py:239
  18.9 1.5 collective-permute-start.1
  21.2 17.2 %shard_map.136.refs_3_.refs_0_ = bf16[32,1024]{1,0:T(8,128)(2,1)} custom-call(bf16[8,32,512]{2,1,0:T(8,128)(2,1)} %copy-done.11, f32[1,4096]{1,0:T(1,128)} %bitcast.11, bf16[4096,1024]{1,0:T(8,128)(2,1)} %query_far.1, bf16[4096,256]{1,0:T(8,128)(2,1)} %key_far.1, bf16[4096,256]{1,0:T(8,128)(2,1)} %value_far.1, bf16[32,2,640,128]{3,2,1,0:T(8,128)(2,1)} %keys_far.1, ...), custom_call_target="tpu_custom_call" | custom-call | tf_op jit(solution)/shard_map/pallas_call | solution.py:208
  39.1 0.8 copy-done.9
  40.6 2.3 %collective-permute-done.refs_1_ = bf16[32,1024]{1,0:T(8,128)(2,1)S(1)} collective-permute-done((bf16[32,1024]{1,0:T(8,128)(2,1)}, bf16[32,1024]{1,0:T(8,128)(2,1)S(1)}, u32[]{:S(2)}, u32[]{:S(2)}) %collective-permute-start) | collective-permute-done | bytes 65568 | tf_op jit(solution)/shard_map/ppermute | solution.py:239
  42.9 0.8 collective-permute-done.2.refs_4_
  43.8 2.7 %collective-permute-start.3 = (bf16[64,1024]{1,0:T(8,128)(2,1)S(1)}, bf16[64,1024]{1,0:T(8,128)(2,1)S(1)}, u32[]{:S(2)}, u32[]{:S(2)}) collective-permute-start(bf16[64,1024]{1,0:T(8,128)(2,1)S(1)} %shard_map.140.refs_0_.refs_2_), channel_id=1, source_target_pairs={{0,16},{4,20},{8,24},{12,28},{16,0},{20,4},{24,8},{28,12},{1,17},{... | collective-permute-start | bytes 393224 | tf_op jit(solution)/shard_map/ppermute | solution.py:239
  46.5 5.0 %collective-permute-done.3.refs_1_ = bf16[64,1024]{1,0:T(8,128)(2,1)S(1)} collective-permute-done((bf16[64,1024]{1,0:T(8,128)(2,1)S(1)}, bf16[64,1024]{1,0:T(8,128)(2,1)S(1)}, u32[]{:S(2)}, u32[]{:S(2)}) %collective-permute-start.3) | collective-permute-done | bytes 131104 | tf_op jit(solution)/shard_map/ppermute | solution.py:239
  52.7 1.5 collective-permute-start.11
  54.2 3.9 %collective-permute-done.4.refs_1_ = bf16[128,1024]{1,0:T(8,128)(2,1)} collective-permute-done((bf16[128,1024]{1,0:T(8,128)(2,1)S(1)}, bf16[128,1024]{1,0:T(8,128)(2,1)}, u32[]{:S(2)}, u32[]{:S(2)}) %collective-permute-start.4) | collective-permute-done | bytes 262176 | tf_op jit(solution)/shard_map/ppermute | solution.py:239
  58.1 1.0 shard_map.142.refs_0_.refs_2_
  61.7 1.6 collective-permute-start.6
  63.3 4.0 %collective-permute-done.6.refs_1_ = bf16[128,512]{1,0:T(8,128)(2,1)S(1)} collective-permute-done((bf16[128,512]{1,0:T(8,128)(2,1)S(1)}, bf16[128,512]{1,0:T(8,128)(2,1)S(1)}, u32[]{:S(2)}, u32[]{:S(2)}) %collective-permute-start.6) | collective-permute-done | bytes 131104 | tf_op jit(solution)/shard_map/ppermute | solution.py:252
  67.4 0.7 shard_map.145
  68.8 1.6 collective-permute-start.9
  70.3 1.3 collective-permute-done.7.refs_2_
  72.4 3.4 %collective-permute-done.9.refs_0_ = bf16[128,640]{1,0:T(8,128)(2,1)S(1)} collective-permute-done((bf16[128,640]{1,0:T(8,128)(2,1)S(1)}, bf16[128,640]{1,0:T(8,128)(2,1)S(1)}, u32[]{:S(2)}, u32[]{:S(2)}) %collective-permute-start.9) | collective-permute-done | bytes 163872 | tf_op jit(solution)/shard_map/ppermute | solution.py:239
  75.9 1.8 %collective-permute-start.8 = (bf16[128,640]{1,0:T(8,128)(2,1)S(1)}, bf16[128,640]{1,0:T(8,128)(2,1)S(1)}, u32[]{:S(2)}, u32[]{:S(2)}) collective-permute-start(bf16[128,640]{1,0:T(8,128)(2,1)S(1)} %shard_map.146.refs_5_), channel_id=1, source_target_pairs={{0,8},{4,12},{8,0},{12,4},{16,24},{20,28},{24,16},{28,20},{1,9},{5... | collective-permute-start | bytes 491528 | tf_op jit(solution)/shard_map/ppermute | solution.py:239
  77.7 2.0 %copy-done = bf16[512,3584]{1,0:T(8,128)(2,1)S(1)} copy-done((bf16[512,3584]{1,0:T(8,128)(2,1)S(1)}, bf16[512,3584]{1,0:T(8,128)(2,1)}, u32[]{:S(2)}) %copy-start) | copy-done | bytes 3670040
  79.8 2.0 %copy-done.2 = bf16[512,3584]{1,0:T(8,128)(2,1)S(1)} copy-done((bf16[512,3584]{1,0:T(8,128)(2,1)S(1)}, bf16[512,3584]{1,0:T(8,128)(2,1)}, u32[]{:S(2)}) %copy-start.2) | copy-done | bytes 3670040
  81.8 2.9 %shard_map.150 = (bf16[128,1920]{1,0:T(8,128)(2,1)S(1)}, bf16[128,1920]{1,0:T(8,128)(2,1)S(1)}) custom-call(s32[3]{0:T(128)S(1)} %pad_add_fusion.refs_0_, bf16[256,512]{1,0:T(8,128)(2,1)S(1)} %get-tuple-element.31.refs_1_, bf16[128,640]{1,0:T(8,128)(2,1)S(1)} %shard_map.148.refs_2_.refs_9_, bf16[128,640]{1,0:T(8,128)(2,1)S(1)} %collective-permute-done.10.refs_3_, ...), custom_call_target="tpu_custom_call" | custom-call | tf_op jit(solution)/shard_map/pallas_call | solution.py:268
  85.0 1.3 collective-permute-start.15
  86.3 2.5 %shard_map.153 = (bf16[128,1920]{1,0:T(8,128)(2,1)S(1)}, bf16[128,1920]{1,0:T(8,128)(2,1)S(1)}) custom-call(s32[3]{0:T(128)S(1)} %pad_add_fusion.refs_0_, bf16[256,512]{1,0:T(8,128)(2,1)S(1)} %get-tuple-element.31.refs_1_, bf16[128,640]{1,0:T(8,128)(2,1)S(1)} %shard_map.151.refs_2_.refs_9_, bf16[128,640]{1,0:T(8,128)(2,1)S(1)} %collective-permute-done.12.refs_3_, ...), custom_call_target="tpu_custom_call" | custom-call | tf_op jit(solution)/shard_map/pallas_call | solution.py:268
  88.8 1.4 collective-permute-start.14
  90.2 8.3 %collective-permute-done.15.refs_0_ = bf16[128,1920]{1,0:T(8,128)(2,1)S(1)} collective-permute-done((bf16[128,1920]{1,0:T(8,128)(2,1)S(1)}, bf16[128,1920]{1,0:T(8,128)(2,1)S(1)}, u32[]{:S(2)}, u32[]{:S(2)}) %collective-permute-start.15) | collective-permute-done | bytes 491552 | tf_op jit(solution)/shard_map/ppermute | solution.py:239
  98.6 4.4 %collective-permute-start.17 = (bf16[64,1920]{1,0:T(8,128)(2,1)S(1)}, bf16[64,1920]{1,0:T(8,128)(2,1)S(1)}, u32[]{:S(2)}, u32[]{:S(2)}) collective-permute-start(bf16[64,1920]{1,0:T(8,128)(2,1)S(1)} %get-tuple-element.37.refs_2_), channel_id=1, source_target_pairs={{0,16},{4,20},{8,24},{12,28},{16,0},{20,4},{24,8},{28,12},{1,17},{... | collective-permute-start | bytes 737288 | tf_op jit(solution)/shard_map/ppermute | solution.py:239
  103.2 3.5 %collective-permute-start.16 = (bf16[64,1920]{1,0:T(8,128)(2,1)S(1)}, bf16[64,1920]{1,0:T(8,128)(2,1)S(1)}, u32[]{:S(2)}, u32[]{:S(2)}) collective-permute-start(bf16[64,1920]{1,0:T(8,128)(2,1)S(1)} %get-tuple-element.38.refs_2_), channel_id=1, source_target_pairs={{0,16},{4,20},{8,24},{12,28},{16,0},{20,4},{24,8},{28,12},{1,17},{... | collective-permute-start | bytes 737288 | tf_op jit(solution)/shard_map/ppermute | solution.py:239
  106.6 12.9 %collective-permute-done.17.refs_0_ = bf16[64,1920]{1,0:T(8,128)(2,1)S(1)} collective-permute-done((bf16[64,1920]{1,0:T(8,128)(2,1)S(1)}, bf16[64,1920]{1,0:T(8,128)(2,1)S(1)}, u32[]{:S(2)}, u32[]{:S(2)}) %collective-permute-start.17) | collective-permute-done | bytes 245792 | tf_op jit(solution)/shard_map/ppermute | solution.py:239
  120.2 7.1 %collective-permute-done.16.refs_0_ = bf16[64,1920]{1,0:T(8,128)(2,1)S(1)} collective-permute-done((bf16[64,1920]{1,0:T(8,128)(2,1)S(1)}, bf16[64,1920]{1,0:T(8,128)(2,1)S(1)}, u32[]{:S(2)}, u32[]{:S(2)}) %collective-permute-start.16) | collective-permute-done | bytes 245792 | tf_op jit(solution)/shard_map/ppermute | solution.py:239
  127.9 1.6 collective-permute-done.19.refs_1_
  129.5 2.5 %collective-permute-start.21 = (bf16[128,896]{1,0:T(8,128)(2,1)S(1)}, bf16[128,896]{1,0:T(8,128)(2,1)S(1)}, u32[]{:S(2)}, u32[]{:S(2)}) collective-permute-start(bf16[128,896]{1,0:T(8,128)(2,1)S(1)} %shard_map.158.refs_2_.refs_0_), channel_id=1, source_target_pairs={{0,8},{4,12},{8,0},{12,4},{16,24},{20,28},{24,16},{28,20},{1,9},{5... | collective-permute-start | bytes 688136 | tf_op jit(solution)/shard_map/ppermute | solution.py:239
  132.0 3.4 %collective-permute-done.18.refs_1_ = bf16[64,896]{1,0:T(8,128)(2,1)S(1)} collective-permute-done((bf16[64,896]{1,0:T(8,128)(2,1)S(1)}, bf16[64,896]{1,0:T(8,128)(2,1)S(1)}, u32[]{:S(2)}, u32[]{:S(2)}) %collective-permute-start.18) | collective-permute-done | bytes 114720 | tf_op jit(solution)/shard_map/ppermute | solution.py:239
  135.4 1.5 collective-permute-start.20
  137.0 2.1 %collective-permute-done.21.refs_1_ = bf16[128,896]{1,0:T(8,128)(2,1)S(1)} collective-permute-done((bf16[128,896]{1,0:T(8,128)(2,1)S(1)}, bf16[128,896]{1,0:T(8,128)(2,1)S(1)}, u32[]{:S(2)}, u32[]{:S(2)}) %collective-permute-start.21) | collective-permute-done | bytes 229408 | tf_op jit(solution)/shard_map/ppermute | solution.py:239
  139.1 1.5 collective-permute-start.23
  140.6 1.6 %collective-permute-done.20.refs_1_ = bf16[128,896]{1,0:T(8,128)(2,1)S(1)} collective-permute-done((bf16[128,896]{1,0:T(8,128)(2,1)S(1)}, bf16[128,896]{1,0:T(8,128)(2,1)S(1)}, u32[]{:S(2)}, u32[]{:S(2)}) %collective-permute-start.20) | collective-permute-done | bytes 229408 | tf_op jit(solution)/shard_map/ppermute | solution.py:239
  142.8 8.9 %collective-permute-done.23.refs_2_ = bf16[256,896]{1,0:T(8,128)(2,1)S(1)} collective-permute-done((bf16[256,896]{1,0:T(8,128)(2,1)S(1)}, bf16[256,896]{1,0:T(8,128)(2,1)S(1)}, u32[]{:S(2)}, u32[]{:S(2)}) %collective-permute-start.23) | collective-permute-done | bytes 458784 | tf_op jit(solution)/shard_map/ppermute | solution.py:239
  151.7 1.3 shard_map.162.refs_4_.refs_5_
  153.0 1.3 shard_map.163.refs_1_.refs_2_
  155.1 1.3 collective-permute-done.24
  156.5 1.5 collective-permute-start.25
  158.0 2.8 %collective-permute-done.25 = bf16[64,512]{1,0:T(8,128)(2,1)S(1)} collective-permute-done((bf16[64,512]{1,0:T(8,128)(2,1)S(1)}, bf16[64,512]{1,0:T(8,128)(2,1)S(1)}, u32[]{:S(2)}, u32[]{:S(2)}) %collective-permute-start.25) | collective-permute-done | bytes 65568 | tf_op jit(solution)/shard_map/ppermute | solution.py:252
  (78 shorter events, 12.2 us)
Async XLA Ops:
  0.0 16.2 %all-to-all-start = ((bf16[8,32,512]{2,1,0:T(8,128)(2,1)}), bf16[8,32,512]{2,1,0:T(8,128)(2,1)S(1)}, u32[]{:S(2)}, u32[]{:S(2)}) async-start(bf16[8,32,512]{2,1,0:T(8,128)(2,1)} %bitcast.7), calls=%async_computation | async-start | bytes 524288 | tf_op jit(solution)/shard_map/all_to_all | solution.py:795
  16.2 0.7 copy-start.11
  16.9 3.4 %copy-start.12 = (s32[32]{0:T(128)S(1)}, s32[32]{0:T(128)}, u32[]{:S(2)}) copy-start(s32[32]{0:T(128)} %param.22) | copy-start | bytes 388
  16.9 26.9 %collective-permute-start.2 = (bf16[640,896]{1,0:T(8,128)(2,1)}, bf16[640,896]{1,0:T(8,128)(2,1)S(1)}, u32[]{:S(2)}, u32[]{:S(2)}) collective-permute-start(bf16[640,896]{1,0:T(8,128)(2,1)} %shard_map.139), channel_id=1, source_target_pairs={{0,8},{4,12},{8,0},{12,4},{16,24},{20,28},{24,16},{28,20},{1,9},{5... | collective-permute-start | bytes 3440648 | tf_op jit(solution)/shard_map/ppermute | solution.py:239
  18.9 24.1 %collective-permute-start.1 = (bf16[512,896]{1,0:T(8,128)(2,1)}, bf16[512,896]{1,0:T(8,128)(2,1)S(1)}, u32[]{:S(2)}, u32[]{:S(2)}) collective-permute-start(bf16[512,896]{1,0:T(8,128)(2,1)} %shard_map.138), channel_id=1, source_target_pairs={{0,4},{4,0},{8,12},{12,8},{16,20},{20,16},{24,28},{28,24},{1,5},{5... | collective-permute-start | bytes 2752520 | tf_op jit(solution)/shard_map/ppermute | solution.py:239
  21.2 17.9 %copy-start.5 = (bf16[4096,512]{1,0:T(8,128)(2,1)S(1)}, bf16[4096,512]{1,0:T(8,128)(2,1)}, u32[]{:S(2)}) copy-start(bf16[4096,512]{1,0:T(8,128)(2,1)} %refs_1_.1) | copy-start | bytes 12582916
  21.2 17.9 %copy-start.6 = (bf16[256,512]{1,0:T(8,128)(2,1)S(1)}, bf16[256,512]{1,0:T(8,128)(2,1)}, u32[]{:S(2)}) copy-start(bf16[256,512]{1,0:T(8,128)(2,1)} %refs_2_.1) | copy-start | bytes 786436
  38.4 4.5 %collective-permute-start = (bf16[32,1024]{1,0:T(8,128)(2,1)}, bf16[32,1024]{1,0:T(8,128)(2,1)S(1)}, u32[]{:S(2)}, u32[]{:S(2)}) collective-permute-start(bf16[32,1024]{1,0:T(8,128)(2,1)} %shard_map.136.refs_3_.refs_0_), channel_id=1, source_target_pairs={{0,4},{4,0},{8,12},{12,8},{16,20},{20,16},{24,28},{28,24},{1,5},{5... | collective-permute-start | bytes 196616 | tf_op jit(solution)/shard_map/ppermute | solution.py:239
  39.1 0.8 copy-start.9
  40.6 10.9 %copy-start.7 = (bf16[256,512]{1,0:T(8,128)(2,1)}, bf16[256,512]{1,0:T(8,128)(2,1)S(1)}, u32[]{:S(2)}) copy-start(bf16[256,512]{1,0:T(8,128)(2,1)S(1)} %get-tuple-element.29.refs_2_.refs_3_) | copy-start | bytes 786436
  43.8 7.8 %collective-permute-start.3 = (bf16[64,1024]{1,0:T(8,128)(2,1)S(1)}, bf16[64,1024]{1,0:T(8,128)(2,1)S(1)}, u32[]{:S(2)}, u32[]{:S(2)}) collective-permute-start(bf16[64,1024]{1,0:T(8,128)(2,1)S(1)} %shard_map.140.refs_0_.refs_2_), channel_id=1, source_target_pairs={{0,16},{4,20},{8,24},{12,28},{16,0},{20,4},{24,8},{28,12},{1,17},{... | collective-permute-start | bytes 393224 | tf_op jit(solution)/shard_map/ppermute | solution.py:239
  51.6 6.5 %collective-permute-start.4 = (bf16[128,1024]{1,0:T(8,128)(2,1)S(1)}, bf16[128,1024]{1,0:T(8,128)(2,1)}, u32[]{:S(2)}, u32[]{:S(2)}) collective-permute-start(bf16[128,1024]{1,0:T(8,128)(2,1)S(1)} %shard_map.141.refs_0_.refs_2_), channel_id=1, source_target_pairs={{0,8},{4,12},{8,0},{12,4},{16,24},{20,28},{24,16},{28,20},{1,9},{5... | collective-permute-start | bytes 786440 | tf_op jit(solution)/shard_map/ppermute | solution.py:239
  52.7 25.0 %collective-permute-start.11 = (bf16[512,896]{1,0:T(8,128)(2,1)}, bf16[512,896]{1,0:T(8,128)(2,1)}, u32[]{:S(2)}, u32[]{:S(2)}) collective-permute-start(bf16[512,896]{1,0:T(8,128)(2,1)} %shard_map.149), channel_id=1, source_target_pairs={{0,4},{4,0},{8,12},{12,8},{16,20},{20,16},{24,28},{28,24},{1,5},{5... | collective-permute-start | bytes 2752520 | tf_op jit(solution)/shard_map/ppermute | solution.py:239
  59.1 9.0 %copy-start.10 = (f32[512]{0:T(512)S(1)}, f32[512]{0:T(512)}, u32[]{:S(2)}) copy-start(f32[512]{0:T(512)} %param.24) | copy-start | bytes 6148
  59.5 8.5 %copy-start.8 = (bf16[256,512]{1,0:T(8,128)(2,1)S(1)}, bf16[256,512]{1,0:T(8,128)(2,1)}, u32[]{:S(2)}) copy-start(bf16[256,512]{1,0:T(8,128)(2,1)} %copy-done.7) | copy-start | bytes 786436
  59.6 1.6 collective-permute-start.5
  60.2 26.1 %collective-permute-start.13 = (bf16[384,896]{1,0:T(8,128)(2,1)}, bf16[384,896]{1,0:T(8,128)(2,1)S(1)}, u32[]{:S(2)}, u32[]{:S(2)}) collective-permute-start(bf16[384,896]{1,0:T(8,128)(2,1)} %shard_map.152), channel_id=1, source_target_pairs={{0,8},{4,12},{8,0},{12,4},{16,24},{20,28},{24,16},{28,20},{1,9},{5... | collective-permute-start | bytes 2064392 | tf_op jit(solution)/shard_map/ppermute | solution.py:239
  61.7 5.6 %collective-permute-start.6 = (bf16[128,512]{1,0:T(8,128)(2,1)S(1)}, bf16[128,512]{1,0:T(8,128)(2,1)S(1)}, u32[]{:S(2)}, u32[]{:S(2)}) collective-permute-start(bf16[128,512]{1,0:T(8,128)(2,1)S(1)} %get-tuple-element.27.refs_2_), channel_id=1, source_target_pairs={{0,2},{1,3},{2,0},{3,1},{4,6},{5,7},{6,4},{7,5},{8,10},{9,11},{10,... | collective-permute-start | bytes 393224 | tf_op jit(solution)/shard_map/ppermute | solution.py:252
  68.8 7.0 %collective-permute-start.9 = (bf16[128,640]{1,0:T(8,128)(2,1)S(1)}, bf16[128,640]{1,0:T(8,128)(2,1)S(1)}, u32[]{:S(2)}, u32[]{:S(2)}) collective-permute-start(bf16[128,640]{1,0:T(8,128)(2,1)S(1)} %shard_map.146.refs_5_), channel_id=1, source_target_pairs={{0,4},{4,0},{8,12},{12,8},{16,20},{20,16},{24,28},{28,24},{1,5},{5... | collective-permute-start | bytes 491528 | tf_op jit(solution)/shard_map/ppermute | solution.py:239
  70.3 1.3 collective-permute-start.7
  75.8 1.9 %collective-permute-start.10 = (bf16[128,640]{1,0:T(8,128)(2,1)S(1)}, bf16[128,640]{1,0:T(8,128)(2,1)S(1)}, u32[]{:S(2)}, u32[]{:S(2)}) collective-permute-start(bf16[128,640]{1,0:T(8,128)(2,1)S(1)} %shard_map.148.refs_2_.refs_9_), channel_id=1, source_target_pairs={{0,1},{1,0},{2,3},{3,2},{4,5},{5,4},{6,7},{7,6},{8,9},{9,8},{10,11... | collective-permute-start | bytes 491528 | tf_op jit(solution)/shard_map/ppermute | solution.py:252
  75.9 8.8 %collective-permute-start.8 = (bf16[128,640]{1,0:T(8,128)(2,1)S(1)}, bf16[128,640]{1,0:T(8,128)(2,1)S(1)}, u32[]{:S(2)}, u32[]{:S(2)}) collective-permute-start(bf16[128,640]{1,0:T(8,128)(2,1)S(1)} %shard_map.146.refs_5_), channel_id=1, source_target_pairs={{0,8},{4,12},{8,0},{12,4},{16,24},{20,28},{24,16},{28,20},{1,9},{5... | collective-permute-start | bytes 491528 | tf_op jit(solution)/shard_map/ppermute | solution.py:239
  77.7 2.0 %copy-start = (bf16[512,3584]{1,0:T(8,128)(2,1)S(1)}, bf16[512,3584]{1,0:T(8,128)(2,1)}, u32[]{:S(2)}) copy-start(bf16[512,3584]{1,0:T(8,128)(2,1)} %refs_6_.3) | copy-start | bytes 11010052
  79.8 2.0 %copy-start.2 = (bf16[512,3584]{1,0:T(8,128)(2,1)S(1)}, bf16[512,3584]{1,0:T(8,128)(2,1)}, u32[]{:S(2)}) copy-start(bf16[512,3584]{1,0:T(8,128)(2,1)} %refs_7_.3) | copy-start | bytes 11010052
  81.8 4.5 %copy-start.1 = (bf16[512,3584]{1,0:T(8,128)(2,1)S(1)}, bf16[512,3584]{1,0:T(8,128)(2,1)}, u32[]{:S(2)}) copy-start(bf16[512,3584]{1,0:T(8,128)(2,1)} %refs_6_.3) | copy-start | bytes 11010052
  81.8 4.5 %copy-start.3 = (bf16[512,3584]{1,0:T(8,128)(2,1)S(1)}, bf16[512,3584]{1,0:T(8,128)(2,1)}, u32[]{:S(2)}) copy-start(bf16[512,3584]{1,0:T(8,128)(2,1)} %refs_7_.3) | copy-start | bytes 11010052
  84.8 1.5 collective-permute-start.12
  85.0 13.5 %collective-permute-start.15 = (bf16[128,1920]{1,0:T(8,128)(2,1)S(1)}, bf16[128,1920]{1,0:T(8,128)(2,1)S(1)}, u32[]{:S(2)}, u32[]{:S(2)}) collective-permute-start(bf16[128,1920]{1,0:T(8,128)(2,1)S(1)} %get-tuple-element.33.refs_1_), channel_id=1, source_target_pairs={{0,8},{4,12},{8,0},{12,4},{16,24},{20,28},{24,16},{28,20},{1,9},{5... | collective-permute-start | bytes 1474568 | tf_op jit(solution)/shard_map/ppermute | solution.py:239
  88.8 14.2 %collective-permute-start.14 = (bf16[128,1920]{1,0:T(8,128)(2,1)S(1)}, bf16[128,1920]{1,0:T(8,128)(2,1)S(1)}, u32[]{:S(2)}, u32[]{:S(2)}) collective-permute-start(bf16[128,1920]{1,0:T(8,128)(2,1)S(1)} %get-tuple-element.34.refs_2_), channel_id=1, source_target_pairs={{0,4},{4,0},{8,12},{12,8},{16,20},{20,16},{24,28},{28,24},{1,5},{5... | collective-permute-start | bytes 1474568 | tf_op jit(solution)/shard_map/ppermute | solution.py:239
  98.6 20.9 %collective-permute-start.17 = (bf16[64,1920]{1,0:T(8,128)(2,1)S(1)}, bf16[64,1920]{1,0:T(8,128)(2,1)S(1)}, u32[]{:S(2)}, u32[]{:S(2)}) collective-permute-start(bf16[64,1920]{1,0:T(8,128)(2,1)S(1)} %get-tuple-element.37.refs_2_), channel_id=1, source_target_pairs={{0,16},{4,20},{8,24},{12,28},{16,0},{20,4},{24,8},{28,12},{1,17},{... | collective-permute-start | bytes 737288 | tf_op jit(solution)/shard_map/ppermute | solution.py:239
  103.2 24.1 %collective-permute-start.16 = (bf16[64,1920]{1,0:T(8,128)(2,1)S(1)}, bf16[64,1920]{1,0:T(8,128)(2,1)S(1)}, u32[]{:S(2)}, u32[]{:S(2)}) collective-permute-start(bf16[64,1920]{1,0:T(8,128)(2,1)S(1)} %get-tuple-element.38.refs_2_), channel_id=1, source_target_pairs={{0,16},{4,20},{8,24},{12,28},{16,0},{20,4},{24,8},{28,12},{1,17},{... | collective-permute-start | bytes 737288 | tf_op jit(solution)/shard_map/ppermute | solution.py:239
  120.1 31.6 %copy-start.4 = (bf16[3584,512]{1,0:T(8,128)(2,1)S(1)}, bf16[3584,512]{1,0:T(8,128)(2,1)}, u32[]{:S(2)}) copy-start(bf16[3584,512]{1,0:T(8,128)(2,1)} %refs_3_.3) | copy-start | bytes 11010052
  120.1 9.3 %collective-permute-start.19 = (bf16[64,896]{1,0:T(8,128)(2,1)S(1)}, bf16[64,896]{1,0:T(8,128)(2,1)S(1)}, u32[]{:S(2)}, u32[]{:S(2)}) collective-permute-start(bf16[64,896]{1,0:T(8,128)(2,1)S(1)} %get-tuple-element.41.refs_2_.refs_0_), channel_id=1, source_target_pairs={{0,16},{4,20},{8,24},{12,28},{16,0},{20,4},{24,8},{28,12},{1,17},{... | collective-permute-start | bytes 344072 | tf_op jit(solution)/shard_map/ppermute | solution.py:239
  127.9 7.5 %collective-permute-start.18 = (bf16[64,896]{1,0:T(8,128)(2,1)S(1)}, bf16[64,896]{1,0:T(8,128)(2,1)S(1)}, u32[]{:S(2)}, u32[]{:S(2)}) collective-permute-start(bf16[64,896]{1,0:T(8,128)(2,1)S(1)} %get-tuple-element.42.refs_2_.refs_0_), channel_id=1, source_target_pairs={{0,16},{4,20},{8,24},{12,28},{16,0},{20,4},{24,8},{28,12},{1,17},{... | collective-permute-start | bytes 344072 | tf_op jit(solution)/shard_map/ppermute | solution.py:239
  129.5 9.6 %collective-permute-start.21 = (bf16[128,896]{1,0:T(8,128)(2,1)S(1)}, bf16[128,896]{1,0:T(8,128)(2,1)S(1)}, u32[]{:S(2)}, u32[]{:S(2)}) collective-permute-start(bf16[128,896]{1,0:T(8,128)(2,1)S(1)} %shard_map.158.refs_2_.refs_0_), channel_id=1, source_target_pairs={{0,8},{4,12},{8,0},{12,4},{16,24},{20,28},{24,16},{28,20},{1,9},{5... | collective-permute-start | bytes 688136 | tf_op jit(solution)/shard_map/ppermute | solution.py:239
  135.4 6.9 %collective-permute-start.20 = (bf16[128,896]{1,0:T(8,128)(2,1)S(1)}, bf16[128,896]{1,0:T(8,128)(2,1)S(1)}, u32[]{:S(2)}, u32[]{:S(2)}) collective-permute-start(bf16[128,896]{1,0:T(8,128)(2,1)S(1)} %shard_map.159.refs_2_.refs_0_), channel_id=1, source_target_pairs={{0,4},{4,0},{8,12},{12,8},{16,20},{20,16},{24,28},{28,24},{1,5},{5... | collective-permute-start | bytes 688136 | tf_op jit(solution)/shard_map/ppermute | solution.py:239
  139.1 12.6 %collective-permute-start.23 = (bf16[256,896]{1,0:T(8,128)(2,1)S(1)}, bf16[256,896]{1,0:T(8,128)(2,1)S(1)}, u32[]{:S(2)}, u32[]{:S(2)}) collective-permute-start(bf16[256,896]{1,0:T(8,128)(2,1)S(1)} %shard_map.160.refs_2_.refs_1_), channel_id=1, source_target_pairs={{0,4},{4,0},{8,12},{12,8},{16,20},{20,16},{24,28},{28,24},{1,5},{5... | collective-permute-start | bytes 1376264 | tf_op jit(solution)/shard_map/ppermute | solution.py:239
  142.3 10.7 %collective-permute-start.22 = (bf16[256,896]{1,0:T(8,128)(2,1)S(1)}, bf16[256,896]{1,0:T(8,128)(2,1)S(1)}, u32[]{:S(2)}, u32[]{:S(2)}) collective-permute-start(bf16[256,896]{1,0:T(8,128)(2,1)S(1)} %shard_map.161.refs_4_.refs_1_), channel_id=1, source_target_pairs={{0,8},{4,12},{8,0},{12,4},{16,24},{20,28},{24,16},{28,20},{1,9},{5... | collective-permute-start | bytes 1376264 | tf_op jit(solution)/shard_map/ppermute | solution.py:239
  155.0 1.4 collective-permute-start.24
  156.5 4.3 %collective-permute-start.25 = (bf16[64,512]{1,0:T(8,128)(2,1)S(1)}, bf16[64,512]{1,0:T(8,128)(2,1)S(1)}, u32[]{:S(2)}, u32[]{:S(2)}) collective-permute-start(bf16[64,512]{1,0:T(8,128)(2,1)S(1)} %dynamic-slice_convert_fusion), channel_id=1, source_target_pairs={{0,2},{1,3},{2,0},{3,1},{4,6},{5,7},{6,4},{7,5},{8,10},{9,11},{10,... | collective-permute-start | bytes 196616 | tf_op jit(solution)/shard_map/ppermute | solution.py:252

commit v4 on v3

--- a/solution.py
+++ b/solution.py
@@ -17,9 +17,9 @@
 JOINED = 4
 SPLIT = 2
 FETCH_VMEM = 32
-EARLY_ROWS = (0, 128)
-MIX_COST = 0
-ATTENTION_VMEM = 56 * 1024 * 1024
+EARLY_ROWS = (256, 0)
+PRELOAD_VMEM = 40 * 1024 * 1024
+ATTENTION_VMEM = 32 * 1024 * 1024
 
 
 def rotary_tables(places, head_size):
@@ -44,9 +44,9 @@
     def body(
         tokens_ref,
         gain_ref,
-        query_far,
-        key_far,
-        value_far,
+        query_ref,
+        key_ref,
+        value_ref,
         keys_far,
         values_far,
         cosine_ref,
@@ -58,31 +58,15 @@
         key_rows,
         value_rows,
         mixed_rows,
-        query_ref,
-        key_ref,
-        value_ref,
         keys_ref,
         values_ref,
-        weight_sems,
         cache_sems,
     ):
-        def weight_copies(piece):
-            span = pl.ds(piece * depth, depth)
-            return [
-                pltpu.make_async_copy(far.at[span], near.at[span], weight_sems.at[piece, i])
-                for i, (far, near) in enumerate(
-                    ((query_far, query_ref), (key_far, key_ref), (value_far, value_ref))
-                )
-            ]
-
         def cache_copy(group, which):
             far, near = ((keys_far, keys_ref), (values_far, values_ref))[which]
             span = pl.ds(group * members, members)
             return pltpu.make_async_copy(far.at[span], near.at[span], cache_sems.at[group, which])
 
-        for piece in range(pieces):
-            for copy in weight_copies(piece):
-                copy.start()
         for which in range(2):
             for group in range(rows // members):
                 cache_copy(group, which).start()
@@ -96,8 +80,6 @@
             span = slice(piece * depth, (piece + 1) * depth)
             part = tokens_ref[piece].astype(jnp.float32)
             normed = (part * scale * gain_ref[:, span]).astype(jnp.bfloat16)
-            for copy in weight_copies(piece):
-                copy.wait()
             for i, weight_ref in enumerate((query_ref, key_ref, value_ref)):
                 product = jnp.dot(normed, weight_ref[span], preferred_element_type=jnp.float32)
                 sums[i] = product if sums[i] is None else sums[i] + product
@@ -208,13 +190,12 @@
     return pl.pallas_call(
         body,
         out_shape=array((rows, heads * head_size), jnp.bfloat16),
-        in_specs=[near, near, *[HBM] * 5, near, near, SCALARS],
+        in_specs=[*[near] * 5, HBM, HBM, near, near, SCALARS],
         out_specs=pl.BlockSpec(memory_space=pltpu.VMEM),
         scratch_shapes=[
             pltpu.VMEM((rows, head_size), jnp.float32),
             *[tall] * 4,
-            *[pltpu.VMEM(v.shape, v.dtype) for v in (*weights, *caches)],
-            pltpu.SemaphoreType.DMA((pieces, 3)),
+            *[pltpu.VMEM(v.shape, v.dtype) for v in caches],
             pltpu.SemaphoreType.DMA((rows // members, 2)),
         ],
         compiler_params=pltpu.CompilerParams(vmem_limit_bytes=ATTENTION_VMEM),
@@ -332,18 +313,14 @@
     )
 
 
-def mix(chain, rows, weight, req_size):
-    block = rows.shape[0] // req_size
-    back = local_from_pair(req_size, 0)
-
+def mix(chain, rows, weight):
     def body(rows_ref, weight_ref, out_ref):
-        left = jnp.concatenate([rows_ref[n * block : (n + 1) * block] for n in back], axis=0)
         out_ref[...] = jnp.dot(
-            left, weight_ref[...], preferred_element_type=jnp.float32
+            rows_ref[...], weight_ref[...], preferred_element_type=jnp.float32
         ).astype(jnp.bfloat16)
 
     out = array((rows.shape[0], weight.shape[1]), jnp.bfloat16)
-    return chain.run(body, [out], [rows, weight], cost=MIX_COST)[0]
+    return chain.run(body, [out], [rows, weight])[0]
 
 
 def half_sum(chain, places, rows, other):
@@ -360,7 +337,6 @@
         [array((half, columns), jnp.bfloat16), array((half, columns), jnp.float32)],
         [places, rows, other],
         [SCALARS, None, None],
-        cost=MIX_COST,
     )
 
 
@@ -462,26 +438,44 @@
     return [order.index(spot) for spot in range(size)]
 
 
-def project_pair(chain, places, scaled, squares, far, got, gate, up, pair, area, start, skip, width, req_size):
+def project_near(chain, places, scaled, gate, up, pair, area, start, skip, width, req_size):
     rows, depth = scaled.shape
     half, block = rows // 2, rows // req_size
+    order = pair_order(req_size, pair)
+
+    def body(places_ref, scaled_ref, gate_ref, up_ref, send_ref, keep_ref):
+        mine = lax.rem(places_ref[0] // (1 << pair), 2)
+        columns = pl.ds(pl.multiple_of(start + mine * area + skip, 128), width)
+        for first, out_ref in ((req_size // 2, send_ref), (0, keep_ref)):
+            left = jnp.concatenate(
+                [
+                    scaled_ref[spot * block : (spot + 1) * block]
+                    for spot in order[first : first + req_size // 2]
+                ],
+                axis=0,
+            )
+            for i, weight_ref in enumerate((gate_ref, up_ref)):
+                out_ref[:, i * width : (i + 1) * width] = jnp.dot(
+                    left, weight_ref[:, columns], preferred_element_type=jnp.float32
+                ).astype(jnp.bfloat16)
+
+    out = array((half, 2 * width), jnp.bfloat16)
+    return chain.run(body, [out, out], [places, scaled, gate, up], [SCALARS, None, None, None])
+
+
+def project_pair(chain, places, near, squares, far, got, pair, skip, width, req_size):
+    half = near[0].shape[0]
+    rows = 2 * half
+    block = rows // req_size
+    depth = far[0].shape[1] - 128
     order = pair_order(req_size, pair)
     flip = 1 << (req_size.bit_length() - 2 - pair)
     cut = got[0].shape[0] - depth
     total = 2 * width + (0 if squares is None else 128)
 
-    def body(places_ref, scaled_ref, far_ref, away_ref, *refs):
-        early_ref, late_ref = refs[:2]
-        weight_fars = refs[2:4]
-        send_ref, keep_ref, all_far, weights, sems = refs[-5:]
-        mine = lax.rem(places_ref[0] // (1 << pair), 2)
-        columns = pl.ds(pl.multiple_of(start + mine * area + skip, 128), width)
-        copies = [
-            pltpu.make_async_copy(weight_fars[i].at[:, columns], weights.at[i], sems.at[i])
-            for i in range(2)
-        ]
-        for copy in copies:
-            copy.start()
+    def body(places_ref, *refs):
+        near_refs, (far_ref, away_ref), (early_ref, late_ref) = refs[:2], refs[2:4], refs[4:6]
+        send_ref, keep_ref, all_far = refs[-3:]
         for away, ref in ((0, far_ref), (1, away_ref)):
             first = 1 - places_ref[1] if away else places_ref[1]
             all_far[pl.ds(pl.multiple_of(first * half, half), half)] = ref[...]
@@ -496,53 +490,35 @@
                 axis=0,
             )
 
-        others = []
-        for spots, out_ref in outs:
+        for near_ref, (spots, out_ref) in zip(near_refs, outs, strict=True):
             for i in range(2):
                 spans = [(early_ref, 0, 0, depth)]
                 if i == 1:
                     spans = [(early_ref, depth, 0, cut), (late_ref, 0, cut, depth)]
-                product = None
+                columns = slice(i * width, (i + 1) * width)
+                product = near_ref[:, columns].astype(jnp.float32)
                 for ref, top, begin, end in spans:
                     if end > begin:
-                        part = jnp.dot(
+                        product = product + jnp.dot(
                             take(all_far, spots, slice(begin, end), flip),
                             ref[top : top + end - begin, skip : skip + width],
                             preferred_element_type=jnp.float32,
                         )
-                        product = part if product is None else product + part
-                others.append(product)
+                out_ref[:, columns] = product.astype(jnp.bfloat16)
             if squares is not None:
                 out_ref[:, 2 * width :] = (
-                    take(refs[4], spots, slice(0, 128))
+                    take(refs[6], spots, slice(0, 128))
                     + take(all_far, spots, slice(depth, depth + 128), flip).astype(jnp.float32)
                 ).astype(jnp.bfloat16)
-        for copy in copies:
-            copy.wait()
-        for j, (spots, out_ref) in enumerate(outs):
-            for i in range(2):
-                near = jnp.dot(
-                    take(scaled_ref, spots, slice(0, depth)),
-                    weights[i],
-                    preferred_element_type=jnp.float32,
-                )
-                out_ref[:, i * width : (i + 1) * width] = (near + others[2 * j + i]).astype(
-                    jnp.bfloat16
-                )
-
-    ins = [places, scaled, *far, *got, gate, up] + ([] if squares is None else [squares])
-    specs = [SCALARS, None, None, None, None, None, HBM, HBM] + [None] * (len(ins) - 8)
+
+    ins = [places, *near, *far, *got] + ([] if squares is None else [squares])
     out = array((half, total), jnp.bfloat16)
     return chain.run(
         body,
         [out, out],
         ins,
-        specs,
-        scratch=[
-            pltpu.VMEM((rows, depth + 128), jnp.bfloat16),
-            pltpu.VMEM((2, depth, width), gate.dtype),
-            pltpu.SemaphoreType.DMA((2,)),
-        ],
+        [SCALARS] + [None] * (len(ins) - 1),
+        scratch=[pltpu.VMEM((rows, depth + 128), jnp.bfloat16)],
     )
 
 
@@ -706,28 +682,31 @@
 def feed_forward(chain, places, scaled, squares, far_parts, gots, gate, up, down, req_size, kv_size):
     bits = req_size.bit_length() - 1
     total = None
-    inverses, fars = {}, {}
+    inverses = {}
     chunks, tasks = plan(gate.shape[1], bits)
+    nears = [
+        project_near(
+            chain, places, scaled, gate, up, c.pair, c.area, c.start, c.skip, c.width, req_size
+        )
+        if c.pair is not None
+        else None
+        for c in chunks
+    ]
+    fars = [relay(chain, v) for v in far_parts]
+    fars = [(v, kv_exchange(v, kv_size, 0)) for v in fars]
     for i, stage in tasks:
         chunk = chunks[i]
         pair, sums, gathers = chunk.pair, chunk.sums, chunk.gathers
         if stage == 0:
             if pair is not None:
-                if pair not in fars:
-                    far = relay(chain, far_parts[pair])
-                    fars[pair] = (far, kv_exchange(far, kv_size, 0))
                 send, chunk.kept = project_pair(
                     chain,
                     places,
-                    scaled,
+                    nears[i],
                     squares if chunk.skip == 0 else None,
                     fars[pair],
                     gots[pair],
-                    gate,
-                    up,
                     pair,
-                    chunk.area,
-                    chunk.start,
                     chunk.skip,
                     chunk.width,
                     req_size,
@@ -795,17 +774,7 @@
     tokens = lax.all_to_all(
         residual_in.reshape(req_size, local_rows, -1), "req", split_axis=0, concat_axis=0
     )
-    attended_rows = attention(
-        tokens,
-        attn_gain,
-        (query_weight, key_matrix, value_matrix),
-        (key_cache, cached_values),
-        rotary_tables(positions, head_size),
-        cache_lengths,
-        heads_here,
-        head_size,
-    )
-    features = attended_rows.shape[1]
+    features = query_weight.shape[1]
     places = jnp.stack([req_place, lax.rem(kv_place, 2), kv_place]).astype(jnp.int32)
     areas = areas_of(gate_weight.shape[1])
     theirs = []
@@ -820,19 +789,30 @@
         [exchange(tie(theirs[0][0], start, theirs[0][1], *theirs[1]), req_size, 0)],
         [exchange(tie(theirs[1][0], start), req_size, 1)],
     ]
+    attended_rows = attention(
+        tokens,
+        attn_gain,
+        (query_weight, key_matrix, value_matrix),
+        (key_cache, cached_values),
+        rotary_tables(positions, head_size),
+        cache_lengths,
+        heads_here,
+        head_size,
+    )
     chain = Chain(attended_rows)
     output_rows, residual_rows = fetch(
         chain, places, features, output_weight, residual_in, req_size
     )
     gathered = attended_rows
     bits = req_size.bit_length() - 1
-    for bit in (0, *reversed(range(1, bits))):
+    for bit in reversed(range(bits)):
         other = exchange(gathered, req_size, bit)
-        gathered = join(chain, gathered, other, [gots[0][0], gots[1][0]] if bit == 0 else [])
-        if bit == 0:
-            gots[0].append(exchange(tie(theirs[0][1], corner(gathered)), req_size, 0))
-    gots[1].append(exchange(tie(theirs[1][1], corner(gathered)), req_size, 1))
-    partial_mix = mix(chain, gathered, output_rows, req_size)
+        early = {bits - 1: [gots[1][0]], 0: [gots[0][0]]}.get(bit, [])
+        gathered = join(chain, gathered, other, early)
+        if bit < 2:
+            late = tie(theirs[bit][1], corner(gathered))
+            gots[bit].append(exchange(late, req_size, bit))
+    partial_mix = mix(chain, gathered, output_rows)
     gain = mlp_gain.reshape(1, -1)
     send, part = half_sum(chain, places, partial_mix, kv_exchange(partial_mix, kv_size, 0))
     for bit in range(1, kv_size.bit_length() - 1):

time: 162 us -> 154 us (0.951)
  Pallas kernels: 32.3 us -> 25.4 us
  local copies, waits for them, and re-layouts: 14.6 us -> 20.9 us
  waiting for transfers between devices: 71.4 us -> 65.4 us
    pallas_call x1, Pallas kernels: 17.2 us -> 8.91 us  [attention(): pl.pallas_call(body, out_shape=array((rows, heads * head_size), jnp.bfloa...]
    unnamed x26 -> x30, local copies, waits for them, and re-layouts: 5.04 us -> 11.6 us
    ppermute x19, waiting for transfers between devices: 61.4 us -> 55 us  [exchange(): return lax.ppermute(value, 'req', [(i, i ^ 1 << bit) for i in range(size)])]
    pallas_call x24 -> x26, Pallas kernels: 15.1 us -> 16.4 us  [run(): pl.pallas_call(kernel, out_shape=outs, in_specs=[*specs, *[pl.BlockSpec(m...]
  transfers between devices with their start and end apart: 27 -> 27, of which waited for: 19 -> 18; matrix products, arithmetic and copies ran while one was open for 7% -> 7% of each run, Pallas kernels for 19% -> 15%
where the time goes in v4:
time: 154 us; the launch traced here: 153 us
  waiting for transfers between devices  65.4 us (42%)
  starting transfers between devices  39.1 us (25%)
  Pallas kernels  25.4 us (16%)
  local copies, waits for them, and re-layouts  20.9 us (14%)
  other arithmetic  2.21 us (1%)
    ppermute x19, waiting for transfers between devices, exchange(): return lax.ppermute(value, 'req', [(i, i ^ 1 << bit) for i in range(size)])  55 us
    ppermute x19, starting transfers between devices, exchange(): return lax.ppermute(value, 'req', [(i, i ^ 1 << bit) for i in range(size)])  27.9 us
    pallas_call x26, Pallas kernels, run(): pl.pallas_call(kernel, out_shape=outs, in_specs=[*specs, *[pl.BlockSpec(m...  16.4 us
    unnamed x30, local copies, waits for them, and re-layouts  11.6 us
    ppermute x7, waiting for transfers between devices, kv_exchange(): return lax.ppermute(value, 'kv', [(i, i ^ 1 << bit) for i in range(size)])  9.5 us
    pallas_call x1, Pallas kernels, attention(): pl.pallas_call(body, out_shape=array((rows, heads * head_size), jnp.bfloa...  8.91 us
    all_to_all x1, starting transfers between devices, shards(): lax.all_to_all(residual_in.reshape(req_size, local_rows, -1), 'req', spli...  7.25 us
    dynamic_slice x2, local copies, waits for them, and re-layouts, shards(): lax.dynamic_slice_in_dim(v, first, area, 1)  4.73 us
  transfers between devices with their start and end apart: 27, of which 18 were waited for; matrix products, arithmetic and copies ran while one was open for 7% of the time, Pallas kernels for 15%

profile of v4, /device:TPU:0, one launch (start us, length us, event | category | flops | bytes accessed | tf_op | source)
XLA Modules:
  0.0 153.3 jit_solution(12699643305666191084)
XLA Ops:
  0.0 7.3 %all-to-all-start = ((bf16[8,32,512]{2,1,0:T(8,128)(2,1)}), bf16[8,32,512]{2,1,0:T(8,128)(2,1)S(1)}, u32[]{:S(2)}, u32[]{:S(2)}) async-start(bf16[8,32,512]{2,1,0:T(8,128)(2,1)} %bitcast.8), calls=%async_computation | async-start | bytes 524288 | tf_op jit(solution)/shard_map/all_to_all | solution.py:774
  7.3 2.2 %constant_dynamic-slice_fusion.3.refs_4_.refs_0_ = bf16[512,896]{1,0:T(8,128)(2,1)} fusion(bf16[512,3584]{1,0:T(8,128)(2,1)} %refs_3_.5, s32[]{:T(128)S(6)} %select_n.27), kind=kLoop, calls=%fused_computation.13 | loop fusion | bytes 1835012 | tf_op jit(solution)/shard_map/dynamic_slice | solution.py:783
  9.4 2.0 %fusion.2 = (bf16[256,896]{1,0:T(8,128)(2,1)}, bf16[256,896]{1,0:T(8,128)(2,1)S(1)}) fusion(bf16[512,3584]{1,0:T(8,128)(2,1)} %refs_3_.5, s32[]{:T(128)S(6)} %add.48, s32[]{:T(128)S(6)} %select_n.28), kind=kLoop, calls=%fused_computation.18 | loop fusion | bytes 1835016 | tf_op jit(solution)/shard_map/slice | solution.py:786
  11.4 2.5 %constant_dynamic-slice_fusion.4 = (bf16[512,896]{1,0:T(8,128)(2,1)S(1)}, bf16[512,896]{1,0:T(8,128)(2,1)}) fusion(bf16[512,3584]{1,0:T(8,128)(2,1)} %refs_2_.5, s32[]{:T(128)S(6)} %select_n.28, s32[]{:T(128)S(6)} %select_n.27), kind=kLoop, calls=%fused_computation.14 | loop fusion | bytes 3670024 | tf_op jit(solution)/shard_map/dynamic_slice | solution.py:783
  14.0 1.2 pad_maximum_fusion.refs_0_
  16.8 1.4 collective-permute-start.4
  19.6 3.4 %copy-done.3 = bf16[4096,1024]{1,0:T(8,128)(2,1)S(1)} copy-done((bf16[4096,1024]{1,0:T(8,128)(2,1)S(1)}, bf16[4096,1024]{1,0:T(8,128)(2,1)}, u32[]{:S(2)}) %copy-start.3) | copy-done | bytes 8388632
  22.9 1.6 %copy-done.5 = bf16[4096,256]{1,0:T(8,128)(2,1)S(1)} copy-done((bf16[4096,256]{1,0:T(8,128)(2,1)S(1)}, bf16[4096,256]{1,0:T(8,128)(2,1)}, u32[]{:S(2)}) %copy-start.5) | copy-done | bytes 2097176
  24.5 1.6 %copy-done.6 = bf16[4096,256]{1,0:T(8,128)(2,1)S(1)} copy-done((bf16[4096,256]{1,0:T(8,128)(2,1)S(1)}, bf16[4096,256]{1,0:T(8,128)(2,1)}, u32[]{:S(2)}) %copy-start.6) | copy-done | bytes 2097176
  26.1 8.9 %shard_map.136.refs_3_.refs_0_ = bf16[32,1024]{1,0:T(8,128)(2,1)S(1)} custom-call(bf16[8,32,512]{2,1,0:T(8,128)(2,1)S(1)} %all-to-all-done.tokens_ref, f32[1,4096]{1,0:T(1,128)S(1)} %bitcast.9, bf16[4096,1024]{1,0:T(8,128)(2,1)S(1)} %copy-done.3, bf16[4096,256]{1,0:T(8,128)(2,1)S(1)} %copy-done.5, bf16[4096,256]{1,0:T(8,128)(2,1)S(1)} %copy-done.6, ...), custom_call_target="tpu_custom_call" | custom-call | tf_op jit(solution)/shard_map/pallas_call | solution.py:190
  35.0 2.4 %collective-permute-start = (bf16[32,1024]{1,0:T(8,128)(2,1)S(1)}, bf16[32,1024]{1,0:T(8,128)(2,1)S(1)}, u32[]{:S(2)}, u32[]{:S(2)}) collective-permute-start(bf16[32,1024]{1,0:T(8,128)(2,1)S(1)} %shard_map.136.refs_3_.refs_0_), channel_id=1, source_target_pairs={{0,16},{4,20},{8,24},{12,28},{16,0},{20,4},{24,8},{28,12},{1,17},{... | collective-permute-start | bytes 196616 | tf_op jit(solution)/shard_map/ppermute | solution.py:220
  38.4 2.3 %collective-permute-done.refs_1_ = bf16[32,1024]{1,0:T(8,128)(2,1)S(1)} collective-permute-done((bf16[32,1024]{1,0:T(8,128)(2,1)S(1)}, bf16[32,1024]{1,0:T(8,128)(2,1)S(1)}, u32[]{:S(2)}, u32[]{:S(2)}) %collective-permute-start) | collective-permute-done | bytes 65568 | tf_op jit(solution)/shard_map/ppermute | solution.py:220
  40.7 2.4 %collective-permute-start.2 = (bf16[64,1024]{1,0:T(8,128)(2,1)S(1)}, bf16[64,1024]{1,0:T(8,128)(2,1)S(1)}, u32[]{:S(2)}, u32[]{:S(2)}) collective-permute-start(bf16[64,1024]{1,0:T(8,128)(2,1)S(1)} %shard_map.139.refs_0_.refs_2_), channel_id=1, source_target_pairs={{0,8},{4,12},{8,0},{12,4},{16,24},{20,28},{24,16},{28,20},{1,9},{5... | collective-permute-start | bytes 393224 | tf_op jit(solution)/shard_map/ppermute | solution.py:220
  43.1 2.9 %collective-permute-done.2.refs_1_ = bf16[64,1024]{1,0:T(8,128)(2,1)S(1)} collective-permute-done((bf16[64,1024]{1,0:T(8,128)(2,1)S(1)}, bf16[64,1024]{1,0:T(8,128)(2,1)S(1)}, u32[]{:S(2)}, u32[]{:S(2)}) %collective-permute-start.2) | collective-permute-done | bytes 131104 | tf_op jit(solution)/shard_map/ppermute | solution.py:220
  47.4 1.3 slice.21.refs_1_
  48.7 2.0 %collective-permute-start.11 = (bf16[512,896]{1,0:T(8,128)(2,1)}, bf16[512,896]{1,0:T(8,128)(2,1)}, u32[]{:S(2)}, u32[]{:S(2)}) collective-permute-start(bf16[512,896]{1,0:T(8,128)(2,1)} %shard_map.152), channel_id=1, source_target_pairs={{0,8},{4,12},{8,0},{12,4},{16,24},{20,28},{24,16},{28,20},{1,9},{5... | collective-permute-start | bytes 2752520 | tf_op jit(solution)/shard_map/ppermute | solution.py:220
  50.7 2.8 %collective-permute-done.3.refs_1_ = bf16[128,1024]{1,0:T(8,128)(2,1)} collective-permute-done((bf16[128,1024]{1,0:T(8,128)(2,1)}, bf16[128,1024]{1,0:T(8,128)(2,1)}, u32[]{:S(2)}, u32[]{:S(2)}) %collective-permute-start.3) | collective-permute-done | bytes 262176 | tf_op jit(solution)/shard_map/ppermute | solution.py:220
  55.1 1.5 collective-permute-done.5.refs_2_
  57.2 1.6 %collective-permute-start.6 = (bf16[128,512]{1,0:T(8,128)(2,1)S(1)}, bf16[128,512]{1,0:T(8,128)(2,1)S(1)}, u32[]{:S(2)}, u32[]{:S(2)}) collective-permute-start(bf16[128,512]{1,0:T(8,128)(2,1)S(1)} %get-tuple-element.31.refs_2_), channel_id=1, source_target_pairs={{0,2},{1,3},{2,0},{3,1},{4,6},{5,7},{6,4},{7,5},{8,10},{9,11},{10,... | collective-permute-start | bytes 393224 | tf_op jit(solution)/shard_map/ppermute | solution.py:233
  59.4 1.6 %collective-permute-start.13 = (bf16[256,896]{1,0:T(8,128)(2,1)}, bf16[256,896]{1,0:T(8,128)(2,1)S(1)}, u32[]{:S(2)}, u32[]{:S(2)}) collective-permute-start(bf16[256,896]{1,0:T(8,128)(2,1)} %shard_map.153), channel_id=1, source_target_pairs={{0,4},{4,0},{8,12},{12,8},{16,20},{20,16},{24,28},{28,24},{1,5},{5... | collective-permute-start | bytes 1376264 | tf_op jit(solution)/shard_map/ppermute | solution.py:220
  61.0 1.8 %collective-permute-done.6.refs_1_ = bf16[128,512]{1,0:T(8,128)(2,1)S(1)} collective-permute-done((bf16[128,512]{1,0:T(8,128)(2,1)S(1)}, bf16[128,512]{1,0:T(8,128)(2,1)S(1)}, u32[]{:S(2)}, u32[]{:S(2)}) %collective-permute-start.6) | collective-permute-done | bytes 131104 | tf_op jit(solution)/shard_map/ppermute | solution.py:233
  65.2 1.7 %collective-permute-start.9 = (bf16[128,640]{1,0:T(8,128)(2,1)S(1)}, bf16[128,640]{1,0:T(8,128)(2,1)S(1)}, u32[]{:S(2)}, u32[]{:S(2)}) collective-permute-start(bf16[128,640]{1,0:T(8,128)(2,1)S(1)} %shard_map.146.refs_5_), channel_id=1, source_target_pairs={{0,4},{4,0},{8,12},{12,8},{16,20},{20,16},{24,28},{28,24},{1,5},{5... | collective-permute-start | bytes 491528 | tf_op jit(solution)/shard_map/ppermute | solution.py:220
  66.9 1.5 collective-permute-start.8
  68.3 1.3 collective-permute-done.7.refs_2_
  70.4 2.0 %copy-done = bf16[512,3584]{1,0:T(8,128)(2,1)S(1)} copy-done((bf16[512,3584]{1,0:T(8,128)(2,1)S(1)}, bf16[512,3584]{1,0:T(8,128)(2,1)}, u32[]{:S(2)}) %copy-start) | copy-done | bytes 3670040
  72.5 2.0 %copy-done.1 = bf16[512,3584]{1,0:T(8,128)(2,1)S(1)} copy-done((bf16[512,3584]{1,0:T(8,128)(2,1)S(1)}, bf16[512,3584]{1,0:T(8,128)(2,1)}, u32[]{:S(2)}) %copy-start.1) | copy-done | bytes 3670040
  74.5 1.3 shard_map.148
  75.8 1.3 shard_map.149
  78.5 1.3 shard_map.154
  80.5 1.9 %shard_map.155 = (bf16[128,1920]{1,0:T(8,128)(2,1)S(1)}, bf16[128,1920]{1,0:T(8,128)(2,1)S(1)}) custom-call(s32[3]{0:T(128)S(1)} %pad_add_fusion.refs_0_, bf16[128,1792]{1,0:T(8,128)(2,1)S(1)} %get-tuple-element.37.refs_1_, bf16[128,1792]{1,0:T(8,128)(2,1)S(1)} %get-tuple-element.38.refs_2_, bf16[128,640]{1,0:T(8,128)(2,1)S(1)} %shard_map.151.refs_8_.refs_3_, ...), custom_call_target="tpu_custom_call" | custom-call | tf_op jit(solution)/shard_map/pallas_call | solution.py:249
  83.3 9.9 %collective-permute-done.15.refs_0_ = bf16[128,1920]{1,0:T(8,128)(2,1)S(1)} collective-permute-done((bf16[128,1920]{1,0:T(8,128)(2,1)S(1)}, bf16[128,1920]{1,0:T(8,128)(2,1)S(1)}, u32[]{:S(2)}, u32[]{:S(2)}) %collective-permute-start.15) | collective-permute-done | bytes 491552 | tf_op jit(solution)/shard_map/ppermute | solution.py:220
  93.3 2.4 %collective-permute-start.17 = (bf16[64,1920]{1,0:T(8,128)(2,1)S(1)}, bf16[64,1920]{1,0:T(8,128)(2,1)S(1)}, u32[]{:S(2)}, u32[]{:S(2)}) collective-permute-start(bf16[64,1920]{1,0:T(8,128)(2,1)S(1)} %get-tuple-element.45.refs_2_), channel_id=1, source_target_pairs={{0,16},{4,20},{8,24},{12,28},{16,0},{20,4},{24,8},{28,12},{1,17},{... | collective-permute-start | bytes 737288 | tf_op jit(solution)/shard_map/ppermute | solution.py:220
  95.9 2.2 %collective-permute-start.16 = (bf16[64,1920]{1,0:T(8,128)(2,1)S(1)}, bf16[64,1920]{1,0:T(8,128)(2,1)S(1)}, u32[]{:S(2)}, u32[]{:S(2)}) collective-permute-start(bf16[64,1920]{1,0:T(8,128)(2,1)S(1)} %get-tuple-element.46.refs_2_), channel_id=1, source_target_pairs={{0,16},{4,20},{8,24},{12,28},{16,0},{20,4},{24,8},{28,12},{1,17},{... | collective-permute-start | bytes 737288 | tf_op jit(solution)/shard_map/ppermute | solution.py:220
  98.0 14.1 %collective-permute-done.17.refs_0_ = bf16[64,1920]{1,0:T(8,128)(2,1)S(1)} collective-permute-done((bf16[64,1920]{1,0:T(8,128)(2,1)S(1)}, bf16[64,1920]{1,0:T(8,128)(2,1)S(1)}, u32[]{:S(2)}, u32[]{:S(2)}) %collective-permute-start.17) | collective-permute-done | bytes 245792 | tf_op jit(solution)/shard_map/ppermute | solution.py:220
  112.7 7.1 %collective-permute-done.16.refs_0_ = bf16[64,1920]{1,0:T(8,128)(2,1)S(1)} collective-permute-done((bf16[64,1920]{1,0:T(8,128)(2,1)S(1)}, bf16[64,1920]{1,0:T(8,128)(2,1)S(1)}, u32[]{:S(2)}, u32[]{:S(2)}) %collective-permute-start.16) | collective-permute-done | bytes 245792 | tf_op jit(solution)/shard_map/ppermute | solution.py:220
  120.4 1.7 %collective-permute-done.19.refs_1_ = bf16[64,896]{1,0:T(8,128)(2,1)S(1)} collective-permute-done((bf16[64,896]{1,0:T(8,128)(2,1)S(1)}, bf16[64,896]{1,0:T(8,128)(2,1)S(1)}, u32[]{:S(2)}, u32[]{:S(2)}) %collective-permute-start.19) | collective-permute-done | bytes 114720 | tf_op jit(solution)/shard_map/ppermute | solution.py:220
  122.2 2.2 %collective-permute-start.21 = (bf16[128,896]{1,0:T(8,128)(2,1)S(1)}, bf16[128,896]{1,0:T(8,128)(2,1)S(1)}, u32[]{:S(2)}, u32[]{:S(2)}) collective-permute-start(bf16[128,896]{1,0:T(8,128)(2,1)S(1)} %shard_map.160.refs_2_.refs_0_), channel_id=1, source_target_pairs={{0,8},{4,12},{8,0},{12,4},{16,24},{20,28},{24,16},{28,20},{1,9},{5... | collective-permute-start | bytes 688136 | tf_op jit(solution)/shard_map/ppermute | solution.py:220
  124.4 2.9 %collective-permute-done.18.refs_1_ = bf16[64,896]{1,0:T(8,128)(2,1)S(1)} collective-permute-done((bf16[64,896]{1,0:T(8,128)(2,1)S(1)}, bf16[64,896]{1,0:T(8,128)(2,1)S(1)}, u32[]{:S(2)}, u32[]{:S(2)}) %collective-permute-start.18) | collective-permute-done | bytes 114720 | tf_op jit(solution)/shard_map/ppermute | solution.py:220
  127.3 1.5 collective-permute-start.20
  128.8 2.4 %collective-permute-done.21.refs_1_ = bf16[128,896]{1,0:T(8,128)(2,1)S(1)} collective-permute-done((bf16[128,896]{1,0:T(8,128)(2,1)S(1)}, bf16[128,896]{1,0:T(8,128)(2,1)S(1)}, u32[]{:S(2)}, u32[]{:S(2)}) %collective-permute-start.21) | collective-permute-done | bytes 229408 | tf_op jit(solution)/shard_map/ppermute | solution.py:220
  131.3 1.2 collective-permute-start.23
  133.5 2.1 %collective-permute-start.22 = (bf16[256,896]{1,0:T(8,128)(2,1)S(1)}, bf16[256,896]{1,0:T(8,128)(2,1)S(1)}, u32[]{:S(2)}, u32[]{:S(2)}) collective-permute-start(bf16[256,896]{1,0:T(8,128)(2,1)S(1)} %shard_map.163.refs_4_.refs_1_), channel_id=1, source_target_pairs={{0,8},{4,12},{8,0},{12,4},{16,24},{20,28},{24,16},{28,20},{1,9},{5... | collective-permute-start | bytes 1376264 | tf_op jit(solution)/shard_map/ppermute | solution.py:220
  135.7 7.9 %collective-permute-done.23.refs_2_ = bf16[256,896]{1,0:T(8,128)(2,1)S(1)} collective-permute-done((bf16[256,896]{1,0:T(8,128)(2,1)S(1)}, bf16[256,896]{1,0:T(8,128)(2,1)S(1)}, u32[]{:S(2)}, u32[]{:S(2)}) %collective-permute-start.23) | collective-permute-done | bytes 458784 | tf_op jit(solution)/shard_map/ppermute | solution.py:220
  143.5 1.3 shard_map.164.refs_4_.refs_5_
  144.8 1.3 shard_map.165.refs_1_.refs_2_
  146.9 1.3 collective-permute-done.24
  148.3 1.6 %collective-permute-start.25 = (bf16[64,512]{1,0:T(8,128)(2,1)S(1)}, bf16[64,512]{1,0:T(8,128)(2,1)S(1)}, u32[]{:S(2)}, u32[]{:S(2)}) collective-permute-start(bf16[64,512]{1,0:T(8,128)(2,1)S(1)} %dynamic-slice_convert_fusion), channel_id=1, source_target_pairs={{0,2},{1,3},{2,0},{3,1},{4,6},{5,7},{6,4},{7,5},{8,10},{9,11},{10,... | collective-permute-start | bytes 196616 | tf_op jit(solution)/shard_map/ppermute | solution.py:233
  149.9 2.7 %collective-permute-done.25 = bf16[64,512]{1,0:T(8,128)(2,1)S(1)} collective-permute-done((bf16[64,512]{1,0:T(8,128)(2,1)S(1)}, bf16[64,512]{1,0:T(8,128)(2,1)S(1)}, u32[]{:S(2)}, u32[]{:S(2)}) %collective-permute-start.25) | collective-permute-done | bytes 65568 | tf_op jit(solution)/shard_map/ppermute | solution.py:233
  (83 shorter events, 18.2 us)
Async XLA Ops:
  0.0 16.2 %all-to-all-start = ((bf16[8,32,512]{2,1,0:T(8,128)(2,1)}), bf16[8,32,512]{2,1,0:T(8,128)(2,1)S(1)}, u32[]{:S(2)}, u32[]{:S(2)}) async-start(bf16[8,32,512]{2,1,0:T(8,128)(2,1)} %bitcast.8), calls=%async_computation | async-start | bytes 524288 | tf_op jit(solution)/shard_map/all_to_all | solution.py:774
  16.8 2.5 %copy-start.14 = (s32[32]{0:T(128)S(1)}, s32[32]{0:T(128)}, u32[]{:S(2)}) copy-start(s32[32]{0:T(128)} %param.22) | copy-start | bytes 388
  16.8 2.8 %copy-start.11 = (f32[4096]{0:T(1024)S(1)}, f32[4096]{0:T(1024)}, u32[]{:S(2)}) copy-start(f32[4096]{0:T(1024)} %param.15) | copy-start | bytes 49156
  16.8 2.8 %copy-start.13 = (s32[32]{0:T(128)S(1)}, s32[32]{0:T(128)}, u32[]{:S(2)}) copy-start(s32[32]{0:T(128)} %limits_ref.1) | copy-start | bytes 388
  16.8 36.7 %collective-permute-start.4 = (bf16[768,896]{1,0:T(8,128)(2,1)}, bf16[768,896]{1,0:T(8,128)(2,1)S(1)}, u32[]{:S(2)}, u32[]{:S(2)}) collective-permute-start(bf16[768,896]{1,0:T(8,128)(2,1)} %shard_map.141), channel_id=1, source_target_pairs={{0,4},{4,0},{8,12},{12,8},{16,20},{20,16},{24,28},{28,24},{1,5},{5... | collective-permute-start | bytes 4128776 | tf_op jit(solution)/shard_map/ppermute | solution.py:220
  18.2 22.5 %collective-permute-start.1 = (bf16[512,896]{1,0:T(8,128)(2,1)}, bf16[512,896]{1,0:T(8,128)(2,1)S(1)}, u32[]{:S(2)}, u32[]{:S(2)}) collective-permute-start(bf16[512,896]{1,0:T(8,128)(2,1)} %shard_map.138), channel_id=1, source_target_pairs={{0,8},{4,12},{8,0},{12,4},{16,24},{20,28},{24,16},{28,20},{1,9},{5... | collective-permute-start | bytes 2752520 | tf_op jit(solution)/shard_map/ppermute | solution.py:220
  19.6 3.4 %copy-start.3 = (bf16[4096,1024]{1,0:T(8,128)(2,1)S(1)}, bf16[4096,1024]{1,0:T(8,128)(2,1)}, u32[]{:S(2)}) copy-start(bf16[4096,1024]{1,0:T(8,128)(2,1)} %query_ref.1) | copy-start | bytes 25165828
  22.9 1.6 %copy-start.5 = (bf16[4096,256]{1,0:T(8,128)(2,1)S(1)}, bf16[4096,256]{1,0:T(8,128)(2,1)}, u32[]{:S(2)}) copy-start(bf16[4096,256]{1,0:T(8,128)(2,1)} %key_ref.1) | copy-start | bytes 6291460
  24.5 1.6 %copy-start.6 = (bf16[4096,256]{1,0:T(8,128)(2,1)S(1)}, bf16[4096,256]{1,0:T(8,128)(2,1)}, u32[]{:S(2)}) copy-start(bf16[4096,256]{1,0:T(8,128)(2,1)} %value_ref.1) | copy-start | bytes 6291460
  26.1 11.4 %copy-start.4 = (bf16[4096,512]{1,0:T(8,128)(2,1)S(1)}, bf16[4096,512]{1,0:T(8,128)(2,1)}, u32[]{:S(2)}) copy-start(bf16[4096,512]{1,0:T(8,128)(2,1)} %refs_1_.1) | copy-start | bytes 12582916
  26.1 11.4 %copy-start.7 = (bf16[256,512]{1,0:T(8,128)(2,1)S(1)}, bf16[256,512]{1,0:T(8,128)(2,1)}, u32[]{:S(2)}) copy-start(bf16[256,512]{1,0:T(8,128)(2,1)} %refs_2_.3) | copy-start | bytes 786436
  35.0 5.7 %collective-permute-start = (bf16[32,1024]{1,0:T(8,128)(2,1)S(1)}, bf16[32,1024]{1,0:T(8,128)(2,1)S(1)}, u32[]{:S(2)}, u32[]{:S(2)}) collective-permute-start(bf16[32,1024]{1,0:T(8,128)(2,1)S(1)} %shard_map.136.refs_3_.refs_0_), channel_id=1, source_target_pairs={{0,16},{4,20},{8,24},{12,28},{16,0},{20,4},{24,8},{28,12},{1,17},{... | collective-permute-start | bytes 196616 | tf_op jit(solution)/shard_map/ppermute | solution.py:220
  38.4 8.4 %copy-start.8 = (bf16[256,512]{1,0:T(8,128)(2,1)}, bf16[256,512]{1,0:T(8,128)(2,1)S(1)}, u32[]{:S(2)}) copy-start(bf16[256,512]{1,0:T(8,128)(2,1)S(1)} %get-tuple-element.33.refs_2_.refs_3_) | copy-start | bytes 786436
  40.7 5.4 %collective-permute-start.2 = (bf16[64,1024]{1,0:T(8,128)(2,1)S(1)}, bf16[64,1024]{1,0:T(8,128)(2,1)S(1)}, u32[]{:S(2)}, u32[]{:S(2)}) collective-permute-start(bf16[64,1024]{1,0:T(8,128)(2,1)S(1)} %shard_map.139.refs_0_.refs_2_), channel_id=1, source_target_pairs={{0,8},{4,12},{8,0},{12,4},{16,24},{20,28},{24,16},{28,20},{1,9},{5... | collective-permute-start | bytes 393224 | tf_op jit(solution)/shard_map/ppermute | solution.py:220
  46.8 6.7 %collective-permute-start.3 = (bf16[128,1024]{1,0:T(8,128)(2,1)}, bf16[128,1024]{1,0:T(8,128)(2,1)}, u32[]{:S(2)}, u32[]{:S(2)}) collective-permute-start(bf16[128,1024]{1,0:T(8,128)(2,1)} %shard_map.140.refs_0_.refs_2_), channel_id=1, source_target_pairs={{0,4},{4,0},{8,12},{12,8},{16,20},{20,16},{24,28},{28,24},{1,5},{5... | collective-permute-start | bytes 786440 | tf_op jit(solution)/shard_map/ppermute | solution.py:220
  48.7 31.8 %collective-permute-start.11 = (bf16[512,896]{1,0:T(8,128)(2,1)}, bf16[512,896]{1,0:T(8,128)(2,1)}, u32[]{:S(2)}, u32[]{:S(2)}) collective-permute-start(bf16[512,896]{1,0:T(8,128)(2,1)} %shard_map.152), channel_id=1, source_target_pairs={{0,8},{4,12},{8,0},{12,4},{16,24},{20,28},{24,16},{28,20},{1,9},{5... | collective-permute-start | bytes 2752520 | tf_op jit(solution)/shard_map/ppermute | solution.py:220
  54.6 9.0 %copy-start.12 = (f32[512]{0:T(512)S(1)}, f32[512]{0:T(512)}, u32[]{:S(2)}) copy-start(f32[512]{0:T(512)} %param.24) | copy-start | bytes 6148
  55.0 14.6 %copy-start.10 = (bf16[256,512]{1,0:T(8,128)(2,1)S(1)}, bf16[256,512]{1,0:T(8,128)(2,1)}, u32[]{:S(2)}) copy-start(bf16[256,512]{1,0:T(8,128)(2,1)} %copy-done.8) | copy-start | bytes 786436
  55.1 1.6 %collective-permute-start.5 = (bf16[256,512]{1,0:T(8,128)(2,1)S(1)}, bf16[256,512]{1,0:T(8,128)(2,1)S(1)}, u32[]{:S(2)}, u32[]{:S(2)}) collective-permute-start(bf16[256,512]{1,0:T(8,128)(2,1)S(1)} %shard_map.143.refs_1_.refs_3_), channel_id=1, source_target_pairs={{0,1},{1,0},{2,3},{3,2},{4,5},{5,4},{6,7},{7,6},{8,9},{9,8},{10,11... | collective-permute-start | bytes 786440 | tf_op jit(solution)/shard_map/ppermute | solution.py:233
  57.2 5.6 %collective-permute-start.6 = (bf16[128,512]{1,0:T(8,128)(2,1)S(1)}, bf16[128,512]{1,0:T(8,128)(2,1)S(1)}, u32[]{:S(2)}, u32[]{:S(2)}) collective-permute-start(bf16[128,512]{1,0:T(8,128)(2,1)S(1)} %get-tuple-element.31.refs_2_), channel_id=1, source_target_pairs={{0,2},{1,3},{2,0},{3,1},{4,6},{5,7},{6,4},{7,5},{8,10},{9,11},{10,... | collective-permute-start | bytes 393224 | tf_op jit(solution)/shard_map/ppermute | solution.py:233
  59.4 18.3 %collective-permute-start.13 = (bf16[256,896]{1,0:T(8,128)(2,1)}, bf16[256,896]{1,0:T(8,128)(2,1)S(1)}, u32[]{:S(2)}, u32[]{:S(2)}) collective-permute-start(bf16[256,896]{1,0:T(8,128)(2,1)} %shard_map.153), channel_id=1, source_target_pairs={{0,4},{4,0},{8,12},{12,8},{16,20},{20,16},{24,28},{28,24},{1,5},{5... | collective-permute-start | bytes 1376264 | tf_op jit(solution)/shard_map/ppermute | solution.py:220
  63.6 1.0 copy-start.9
  65.2 11.8 %collective-permute-start.9 = (bf16[128,640]{1,0:T(8,128)(2,1)S(1)}, bf16[128,640]{1,0:T(8,128)(2,1)S(1)}, u32[]{:S(2)}, u32[]{:S(2)}) collective-permute-start(bf16[128,640]{1,0:T(8,128)(2,1)S(1)} %shard_map.146.refs_5_), channel_id=1, source_target_pairs={{0,4},{4,0},{8,12},{12,8},{16,20},{20,16},{24,28},{28,24},{1,5},{5... | collective-permute-start | bytes 491528 | tf_op jit(solution)/shard_map/ppermute | solution.py:220
  66.9 10.4 %collective-permute-start.8 = (bf16[128,640]{1,0:T(8,128)(2,1)S(1)}, bf16[128,640]{1,0:T(8,128)(2,1)S(1)}, u32[]{:S(2)}, u32[]{:S(2)}) collective-permute-start(bf16[128,640]{1,0:T(8,128)(2,1)S(1)} %shard_map.146.refs_5_), channel_id=1, source_target_pairs={{0,8},{4,12},{8,0},{12,4},{16,24},{20,28},{24,16},{28,20},{1,9},{5... | collective-permute-start | bytes 491528 | tf_op jit(solution)/shard_map/ppermute | solution.py:220
  68.3 1.3 collective-permute-start.7
  70.4 2.0 %copy-start = (bf16[512,3584]{1,0:T(8,128)(2,1)S(1)}, bf16[512,3584]{1,0:T(8,128)(2,1)}, u32[]{:S(2)}) copy-start(bf16[512,3584]{1,0:T(8,128)(2,1)} %refs_3_.5) | copy-start | bytes 11010052
  72.5 2.0 %copy-start.1 = (bf16[512,3584]{1,0:T(8,128)(2,1)S(1)}, bf16[512,3584]{1,0:T(8,128)(2,1)}, u32[]{:S(2)}) copy-start(bf16[512,3584]{1,0:T(8,128)(2,1)} %refs_2_.5) | copy-start | bytes 11010052
  77.1 1.5 collective-permute-start.12
  77.3 3.2 %collective-permute-start.10 = (bf16[128,640]{1,0:T(8,128)(2,1)S(1)}, bf16[128,640]{1,0:T(8,128)(2,1)S(1)}, u32[]{:S(2)}, u32[]{:S(2)}) collective-permute-start(bf16[128,640]{1,0:T(8,128)(2,1)S(1)} %shard_map.151.refs_8_.refs_3_), channel_id=1, source_target_pairs={{0,1},{1,0},{2,3},{3,2},{4,5},{5,4},{6,7},{7,6},{8,9},{9,8},{10,11... | collective-permute-start | bytes 491528 | tf_op jit(solution)/shard_map/ppermute | solution.py:233
  79.8 13.3 %collective-permute-start.15 = (bf16[128,1920]{1,0:T(8,128)(2,1)S(1)}, bf16[128,1920]{1,0:T(8,128)(2,1)S(1)}, u32[]{:S(2)}, u32[]{:S(2)}) collective-permute-start(bf16[128,1920]{1,0:T(8,128)(2,1)S(1)} %get-tuple-element.41.refs_8_), channel_id=1, source_target_pairs={{0,8},{4,12},{8,0},{12,4},{16,24},{20,28},{24,16},{28,20},{1,9},{5... | collective-permute-start | bytes 1474568 | tf_op jit(solution)/shard_map/ppermute | solution.py:220
  82.4 13.3 %collective-permute-start.14 = (bf16[128,1920]{1,0:T(8,128)(2,1)S(1)}, bf16[128,1920]{1,0:T(8,128)(2,1)S(1)}, u32[]{:S(2)}, u32[]{:S(2)}) collective-permute-start(bf16[128,1920]{1,0:T(8,128)(2,1)S(1)} %get-tuple-element.42.refs_2_), channel_id=1, source_target_pairs={{0,4},{4,0},{8,12},{12,8},{16,20},{20,16},{24,28},{28,24},{1,5},{5... | collective-permute-start | bytes 1474568 | tf_op jit(solution)/shard_map/ppermute | solution.py:220
  93.3 18.8 %collective-permute-start.17 = (bf16[64,1920]{1,0:T(8,128)(2,1)S(1)}, bf16[64,1920]{1,0:T(8,128)(2,1)S(1)}, u32[]{:S(2)}, u32[]{:S(2)}) collective-permute-start(bf16[64,1920]{1,0:T(8,128)(2,1)S(1)} %get-tuple-element.45.refs_2_), channel_id=1, source_target_pairs={{0,16},{4,20},{8,24},{12,28},{16,0},{20,4},{24,8},{28,12},{1,17},{... | collective-permute-start | bytes 737288 | tf_op jit(solution)/shard_map/ppermute | solution.py:220
  95.9 47.7 %copy-start.2 = (bf16[3584,512]{1,0:T(8,128)(2,1)S(1)}, bf16[3584,512]{1,0:T(8,128)(2,1)}, u32[]{:S(2)}) copy-start(bf16[3584,512]{1,0:T(8,128)(2,1)} %refs_3_.7) | copy-start | bytes 11010052
  95.9 23.9 %collective-permute-start.16 = (bf16[64,1920]{1,0:T(8,128)(2,1)S(1)}, bf16[64,1920]{1,0:T(8,128)(2,1)S(1)}, u32[]{:S(2)}, u32[]{:S(2)}) collective-permute-start(bf16[64,1920]{1,0:T(8,128)(2,1)S(1)} %get-tuple-element.46.refs_2_), channel_id=1, source_target_pairs={{0,16},{4,20},{8,24},{12,28},{16,0},{20,4},{24,8},{28,12},{1,17},{... | collective-permute-start | bytes 737288 | tf_op jit(solution)/shard_map/ppermute | solution.py:220
  112.7 9.4 %collective-permute-start.19 = (bf16[64,896]{1,0:T(8,128)(2,1)S(1)}, bf16[64,896]{1,0:T(8,128)(2,1)S(1)}, u32[]{:S(2)}, u32[]{:S(2)}) collective-permute-start(bf16[64,896]{1,0:T(8,128)(2,1)S(1)} %get-tuple-element.49.refs_2_.refs_0_), channel_id=1, source_target_pairs={{0,16},{4,20},{8,24},{12,28},{16,0},{20,4},{24,8},{28,12},{1,17},{... | collective-permute-start | bytes 344072 | tf_op jit(solution)/shard_map/ppermute | solution.py:220
  120.4 6.9 %collective-permute-start.18 = (bf16[64,896]{1,0:T(8,128)(2,1)S(1)}, bf16[64,896]{1,0:T(8,128)(2,1)S(1)}, u32[]{:S(2)}, u32[]{:S(2)}) collective-permute-start(bf16[64,896]{1,0:T(8,128)(2,1)S(1)} %get-tuple-element.50.refs_2_.refs_0_), channel_id=1, source_target_pairs={{0,16},{4,20},{8,24},{12,28},{16,0},{20,4},{24,8},{28,12},{1,17},{... | collective-permute-start | bytes 344072 | tf_op jit(solution)/shard_map/ppermute | solution.py:220
  122.2 9.0 %collective-permute-start.21 = (bf16[128,896]{1,0:T(8,128)(2,1)S(1)}, bf16[128,896]{1,0:T(8,128)(2,1)S(1)}, u32[]{:S(2)}, u32[]{:S(2)}) collective-permute-start(bf16[128,896]{1,0:T(8,128)(2,1)S(1)} %shard_map.160.refs_2_.refs_0_), channel_id=1, source_target_pairs={{0,8},{4,12},{8,0},{12,4},{16,24},{20,28},{24,16},{28,20},{1,9},{5... | collective-permute-start | bytes 688136 | tf_op jit(solution)/shard_map/ppermute | solution.py:220
  127.3 6.2 %collective-permute-start.20 = (bf16[128,896]{1,0:T(8,128)(2,1)S(1)}, bf16[128,896]{1,0:T(8,128)(2,1)S(1)}, u32[]{:S(2)}, u32[]{:S(2)}) collective-permute-start(bf16[128,896]{1,0:T(8,128)(2,1)S(1)} %shard_map.161.refs_2_.refs_0_), channel_id=1, source_target_pairs={{0,4},{4,0},{8,12},{12,8},{16,20},{20,16},{24,28},{28,24},{1,5},{5... | collective-permute-start | bytes 688136 | tf_op jit(solution)/shard_map/ppermute | solution.py:220
  131.3 12.3 %collective-permute-start.23 = (bf16[256,896]{1,0:T(8,128)(2,1)S(1)}, bf16[256,896]{1,0:T(8,128)(2,1)S(1)}, u32[]{:S(2)}, u32[]{:S(2)}) collective-permute-start(bf16[256,896]{1,0:T(8,128)(2,1)S(1)} %shard_map.162.refs_2_.refs_1_), channel_id=1, source_target_pairs={{0,4},{4,0},{8,12},{12,8},{16,20},{20,16},{24,28},{28,24},{1,5},{5... | collective-permute-start | bytes 1376264 | tf_op jit(solution)/shard_map/ppermute | solution.py:220
  133.5 11.3 %collective-permute-start.22 = (bf16[256,896]{1,0:T(8,128)(2,1)S(1)}, bf16[256,896]{1,0:T(8,128)(2,1)S(1)}, u32[]{:S(2)}, u32[]{:S(2)}) collective-permute-start(bf16[256,896]{1,0:T(8,128)(2,1)S(1)} %shard_map.163.refs_4_.refs_1_), channel_id=1, source_target_pairs={{0,8},{4,12},{8,0},{12,4},{16,24},{20,28},{24,16},{28,20},{1,9},{5... | collective-permute-start | bytes 1376264 | tf_op jit(solution)/shard_map/ppermute | solution.py:220
  146.8 1.4 collective-permute-start.24
  148.3 4.3 %collective-permute-start.25 = (bf16[64,512]{1,0:T(8,128)(2,1)S(1)}, bf16[64,512]{1,0:T(8,128)(2,1)S(1)}, u32[]{:S(2)}, u32[]{:S(2)}) collective-permute-start(bf16[64,512]{1,0:T(8,128)(2,1)S(1)} %dynamic-slice_convert_fusion), channel_id=1, source_target_pairs={{0,2},{1,3},{2,0},{3,1},{4,6},{5,7},{6,4},{7,5},{8,10},{9,11},{10,... | collective-permute-start | bytes 196616 | tf_op jit(solution)/shard_map/ppermute | solution.py:233

commit v5 on v4

--- a/solution.py
+++ b/solution.py
@@ -648,6 +648,27 @@
         [places, total],
         [SCALARS, None],
     )
+
+
+def lower_half(chain, places, hidden, away, down, pair, area, start, skip, width, carried, req_size):
+    rows, columns = hidden.shape[0], down.shape[1]
+    block = rows // req_size
+    back = local_from_pair(req_size, pair)
+
+    def body(places_ref, hidden_ref, down_ref, *refs):
+        mine = lax.rem(places_ref[0] // (1 << pair), 2)
+        which = 1 - mine if away else mine
+        left = jnp.concatenate(
+            [hidden_ref[(n ^ away) * block : ((n ^ away) + 1) * block] for n in back], axis=0
+        )
+        first = pl.multiple_of(start + which * area + skip, 128)
+        total = jnp.dot(left, down_ref[pl.ds(first, width)], preferred_element_type=jnp.float32)
+        refs[-1][...] = total if carried is None else refs[0][...] + total
+
+    ins = [places, hidden, down] + ([] if carried is None else [carried])
+    return chain.run(
+        body, [array((rows, columns), jnp.float32)], ins, [SCALARS] + [None] * (len(ins) - 1)
+    )[0]
 
 
 class Chunk:
@@ -731,6 +752,36 @@
         elif stage < len(sums) + len(gathers):
             chunk.kept = join(chain, chunk.kept, chunk.moving)
             chunk.moving = exchange(chunk.kept, req_size, gathers[stage - len(sums)])
+            if pair is not None and stage == len(sums) + len(gathers) - 1:
+                total = lower_half(
+                    chain,
+                    places,
+                    chunk.kept,
+                    0,
+                    down,
+                    pair,
+                    chunk.area,
+                    chunk.start,
+                    chunk.skip,
+                    chunk.width,
+                    total,
+                    req_size,
+                )
+        elif pair is not None:
+            total = lower_half(
+                chain,
+                places,
+                chunk.moving,
+                1,
+                down,
+                pair,
+                chunk.area,
+                chunk.start,
+                chunk.skip,
+                chunk.width,
+                total,
+                req_size,
+            )
         else:
             total = lower(
                 chain,

time: 154 us -> 154 us (level)
    pallas_call x26 -> x28, Pallas kernels: 16.4 us -> 17.8 us  [run(): pl.pallas_call(kernel, out_shape=outs, in_specs=[*specs, *[pl.BlockSpec(m...]
  transfers between devices with their start and end apart: 27 -> 27, of which waited for: 18 -> 19; matrix products, arithmetic and copies ran while one was open for 7% -> 7% of each run, Pallas kernels for 15% -> 16%
where the time goes in v5:
time: 154 us
  waiting for transfers between devices  64.7 us (42%)
  starting transfers between devices  38.8 us (25%)
  Pallas kernels  26.8 us (17%)
  local copies, waits for them, and re-layouts  20.9 us (14%)
  other arithmetic  2.21 us (1%)
    ppermute x19, waiting for transfers between devices, exchange(): return lax.ppermute(value, 'req', [(i, i ^ 1 << bit) for i in range(size)])  53.9 us
    ppermute x19, starting transfers between devices, exchange(): return lax.ppermute(value, 'req', [(i, i ^ 1 << bit) for i in range(size)])  27.8 us
    pallas_call x28, Pallas kernels, run(): pl.pallas_call(kernel, out_shape=outs, in_specs=[*specs, *[pl.BlockSpec(m...  17.8 us
    unnamed x30, local copies, waits for them, and re-layouts  11.6 us
    ppermute x7, waiting for transfers between devices, kv_exchange(): return lax.ppermute(value, 'kv', [(i, i ^ 1 << bit) for i in range(size)])  9.8 us
    pallas_call x1, Pallas kernels, attention(): pl.pallas_call(body, out_shape=array((rows, heads * head_size), jnp.bfloa...  8.91 us
    all_to_all x1, starting transfers between devices, shards(): lax.all_to_all(residual_in.reshape(req_size, local_rows, -1), 'req', spli...  7.25 us
    dynamic_slice x2, local copies, waits for them, and re-layouts, shards(): lax.dynamic_slice_in_dim(v, first, area, 1)  4.73 us
  transfers between devices with their start and end apart: 27, of which 19 were waited for; matrix products, arithmetic and copies ran while one was open for 7% of the time, Pallas kernels for 16%

profile of v5, /device:TPU:0, one launch (start us, length us, event | category | flops | bytes accessed | tf_op | source)
XLA Modules:
  0.0 153.6 jit_solution(15358445816944414550)
XLA Ops:
  0.0 7.3 %all-to-all-start = ((bf16[8,32,512]{2,1,0:T(8,128)(2,1)}), bf16[8,32,512]{2,1,0:T(8,128)(2,1)S(1)}, u32[]{:S(2)}, u32[]{:S(2)}) async-start(bf16[8,32,512]{2,1,0:T(8,128)(2,1)} %bitcast.8), calls=%async_computation | async-start | bytes 524288 | tf_op jit(solution)/shard_map/all_to_all | solution.py:825
  7.3 2.2 %constant_dynamic-slice_fusion.3.refs_4_.refs_0_ = bf16[512,896]{1,0:T(8,128)(2,1)} fusion(bf16[512,3584]{1,0:T(8,128)(2,1)} %refs_3_.3, s32[]{:T(128)S(6)} %select_n.27), kind=kLoop, calls=%fused_computation.13 | loop fusion | bytes 1835012 | tf_op jit(solution)/shard_map/dynamic_slice | solution.py:834
  9.4 2.0 %fusion.2 = (bf16[256,896]{1,0:T(8,128)(2,1)}, bf16[256,896]{1,0:T(8,128)(2,1)S(1)}) fusion(bf16[512,3584]{1,0:T(8,128)(2,1)} %refs_3_.3, s32[]{:T(128)S(6)} %add.48, s32[]{:T(128)S(6)} %select_n.28), kind=kLoop, calls=%fused_computation.18 | loop fusion | bytes 1835016 | tf_op jit(solution)/shard_map/slice | solution.py:837
  11.4 2.5 %constant_dynamic-slice_fusion.4 = (bf16[512,896]{1,0:T(8,128)(2,1)S(1)}, bf16[512,896]{1,0:T(8,128)(2,1)}) fusion(bf16[512,3584]{1,0:T(8,128)(2,1)} %refs_2_.9, s32[]{:T(128)S(6)} %select_n.28, s32[]{:T(128)S(6)} %select_n.27), kind=kLoop, calls=%fused_computation.14 | loop fusion | bytes 3670024 | tf_op jit(solution)/shard_map/dynamic_slice | solution.py:834
  14.0 1.2 pad_maximum_fusion.refs_0_
  16.8 1.4 collective-permute-start.4
  18.2 1.1 collective-permute-start.1
  19.6 3.4 %copy-done.3 = bf16[4096,1024]{1,0:T(8,128)(2,1)S(1)} copy-done((bf16[4096,1024]{1,0:T(8,128)(2,1)S(1)}, bf16[4096,1024]{1,0:T(8,128)(2,1)}, u32[]{:S(2)}) %copy-start.3) | copy-done | bytes 8388632
  22.9 1.6 %copy-done.5 = bf16[4096,256]{1,0:T(8,128)(2,1)S(1)} copy-done((bf16[4096,256]{1,0:T(8,128)(2,1)S(1)}, bf16[4096,256]{1,0:T(8,128)(2,1)}, u32[]{:S(2)}) %copy-start.5) | copy-done | bytes 2097176
  24.5 1.6 %copy-done.6 = bf16[4096,256]{1,0:T(8,128)(2,1)S(1)} copy-done((bf16[4096,256]{1,0:T(8,128)(2,1)S(1)}, bf16[4096,256]{1,0:T(8,128)(2,1)}, u32[]{:S(2)}) %copy-start.6) | copy-done | bytes 2097176
  26.1 8.9 %shard_map.136.refs_3_.refs_0_ = bf16[32,1024]{1,0:T(8,128)(2,1)S(1)} custom-call(bf16[8,32,512]{2,1,0:T(8,128)(2,1)S(1)} %all-to-all-done.tokens_ref, f32[1,4096]{1,0:T(1,128)S(1)} %bitcast.9, bf16[4096,1024]{1,0:T(8,128)(2,1)S(1)} %copy-done.3, bf16[4096,256]{1,0:T(8,128)(2,1)S(1)} %copy-done.5, bf16[4096,256]{1,0:T(8,128)(2,1)S(1)} %copy-done.6, ...), custom_call_target="tpu_custom_call" | custom-call | tf_op jit(solution)/shard_map/pallas_call | solution.py:190
  35.0 2.4 %collective-permute-start = (bf16[32,1024]{1,0:T(8,128)(2,1)S(1)}, bf16[32,1024]{1,0:T(8,128)(2,1)S(1)}, u32[]{:S(2)}, u32[]{:S(2)}) collective-permute-start(bf16[32,1024]{1,0:T(8,128)(2,1)S(1)} %shard_map.136.refs_3_.refs_0_), channel_id=1, source_target_pairs={{0,16},{4,20},{8,24},{12,28},{16,0},{20,4},{24,8},{28,12},{1,17},{... | collective-permute-start | bytes 196616 | tf_op jit(solution)/shard_map/ppermute | solution.py:220
  38.4 2.3 %collective-permute-done.refs_1_ = bf16[32,1024]{1,0:T(8,128)(2,1)S(1)} collective-permute-done((bf16[32,1024]{1,0:T(8,128)(2,1)S(1)}, bf16[32,1024]{1,0:T(8,128)(2,1)S(1)}, u32[]{:S(2)}, u32[]{:S(2)}) %collective-permute-start) | collective-permute-done | bytes 65568 | tf_op jit(solution)/shard_map/ppermute | solution.py:220
  40.7 2.4 %collective-permute-start.2 = (bf16[64,1024]{1,0:T(8,128)(2,1)S(1)}, bf16[64,1024]{1,0:T(8,128)(2,1)S(1)}, u32[]{:S(2)}, u32[]{:S(2)}) collective-permute-start(bf16[64,1024]{1,0:T(8,128)(2,1)S(1)} %shard_map.139.refs_0_.refs_2_), channel_id=1, source_target_pairs={{0,8},{4,12},{8,0},{12,4},{16,24},{20,28},{24,16},{28,20},{1,9},{5... | collective-permute-start | bytes 393224 | tf_op jit(solution)/shard_map/ppermute | solution.py:220
  43.1 2.9 %collective-permute-done.2.refs_1_ = bf16[64,1024]{1,0:T(8,128)(2,1)S(1)} collective-permute-done((bf16[64,1024]{1,0:T(8,128)(2,1)S(1)}, bf16[64,1024]{1,0:T(8,128)(2,1)S(1)}, u32[]{:S(2)}, u32[]{:S(2)}) %collective-permute-start.2) | collective-permute-done | bytes 131104 | tf_op jit(solution)/shard_map/ppermute | solution.py:220
  47.4 1.3 slice.21.refs_1_
  48.7 2.0 %collective-permute-start.11 = (bf16[512,896]{1,0:T(8,128)(2,1)}, bf16[512,896]{1,0:T(8,128)(2,1)}, u32[]{:S(2)}, u32[]{:S(2)}) collective-permute-start(bf16[512,896]{1,0:T(8,128)(2,1)} %shard_map.152), channel_id=1, source_target_pairs={{0,8},{4,12},{8,0},{12,4},{16,24},{20,28},{24,16},{28,20},{1,9},{5... | collective-permute-start | bytes 2752520 | tf_op jit(solution)/shard_map/ppermute | solution.py:220
  50.7 2.8 %collective-permute-done.3.refs_1_ = bf16[128,1024]{1,0:T(8,128)(2,1)} collective-permute-done((bf16[128,1024]{1,0:T(8,128)(2,1)}, bf16[128,1024]{1,0:T(8,128)(2,1)}, u32[]{:S(2)}, u32[]{:S(2)}) %collective-permute-start.3) | collective-permute-done | bytes 262176 | tf_op jit(solution)/shard_map/ppermute | solution.py:220
  53.5 1.1 shard_map.142.refs_0_.refs_2_
  55.1 1.5 collective-permute-done.5.refs_2_
  57.2 1.6 %collective-permute-start.6 = (bf16[128,512]{1,0:T(8,128)(2,1)S(1)}, bf16[128,512]{1,0:T(8,128)(2,1)S(1)}, u32[]{:S(2)}, u32[]{:S(2)}) collective-permute-start(bf16[128,512]{1,0:T(8,128)(2,1)S(1)} %get-tuple-element.31.refs_2_), channel_id=1, source_target_pairs={{0,2},{1,3},{2,0},{3,1},{4,6},{5,7},{6,4},{7,5},{8,10},{9,11},{10,... | collective-permute-start | bytes 393224 | tf_op jit(solution)/shard_map/ppermute | solution.py:233
  59.4 1.6 %collective-permute-start.13 = (bf16[256,896]{1,0:T(8,128)(2,1)}, bf16[256,896]{1,0:T(8,128)(2,1)S(1)}, u32[]{:S(2)}, u32[]{:S(2)}) collective-permute-start(bf16[256,896]{1,0:T(8,128)(2,1)} %shard_map.153), channel_id=1, source_target_pairs={{0,4},{4,0},{8,12},{12,8},{16,20},{20,16},{24,28},{28,24},{1,5},{5... | collective-permute-start | bytes 1376264 | tf_op jit(solution)/shard_map/ppermute | solution.py:220
  61.0 1.8 %collective-permute-done.6.refs_1_ = bf16[128,512]{1,0:T(8,128)(2,1)S(1)} collective-permute-done((bf16[128,512]{1,0:T(8,128)(2,1)S(1)}, bf16[128,512]{1,0:T(8,128)(2,1)S(1)}, u32[]{:S(2)}, u32[]{:S(2)}) %collective-permute-start.6) | collective-permute-done | bytes 131104 | tf_op jit(solution)/shard_map/ppermute | solution.py:233
  65.2 1.7 %collective-permute-start.9 = (bf16[128,640]{1,0:T(8,128)(2,1)S(1)}, bf16[128,640]{1,0:T(8,128)(2,1)S(1)}, u32[]{:S(2)}, u32[]{:S(2)}) collective-permute-start(bf16[128,640]{1,0:T(8,128)(2,1)S(1)} %shard_map.146.refs_5_), channel_id=1, source_target_pairs={{0,4},{4,0},{8,12},{12,8},{16,20},{20,16},{24,28},{28,24},{1,5},{5... | collective-permute-start | bytes 491528 | tf_op jit(solution)/shard_map/ppermute | solution.py:220
  66.9 1.5 collective-permute-start.8
  68.3 1.3 collective-permute-done.7.refs_2_
  70.4 2.0 %copy-done.1 = bf16[512,3584]{1,0:T(8,128)(2,1)S(1)} copy-done((bf16[512,3584]{1,0:T(8,128)(2,1)S(1)}, bf16[512,3584]{1,0:T(8,128)(2,1)}, u32[]{:S(2)}) %copy-start.1) | copy-done | bytes 3670040
  72.5 2.0 %copy-done.2 = bf16[512,3584]{1,0:T(8,128)(2,1)S(1)} copy-done((bf16[512,3584]{1,0:T(8,128)(2,1)S(1)}, bf16[512,3584]{1,0:T(8,128)(2,1)}, u32[]{:S(2)}) %copy-start.2) | copy-done | bytes 3670040
  74.5 1.3 shard_map.148
  75.8 1.3 shard_map.149
  78.5 1.3 shard_map.154
  80.5 1.9 %shard_map.155 = (bf16[128,1920]{1,0:T(8,128)(2,1)S(1)}, bf16[128,1920]{1,0:T(8,128)(2,1)S(1)}) custom-call(s32[3]{0:T(128)S(1)} %pad_add_fusion.refs_0_, bf16[128,1792]{1,0:T(8,128)(2,1)S(1)} %get-tuple-element.37.refs_1_, bf16[128,1792]{1,0:T(8,128)(2,1)S(1)} %get-tuple-element.38.refs_2_, bf16[128,640]{1,0:T(8,128)(2,1)S(1)} %shard_map.151.refs_8_.refs_3_, ...), custom_call_target="tpu_custom_call" | custom-call | tf_op jit(solution)/shard_map/pallas_call | solution.py:249
  83.3 9.9 %collective-permute-done.15.refs_0_ = bf16[128,1920]{1,0:T(8,128)(2,1)S(1)} collective-permute-done((bf16[128,1920]{1,0:T(8,128)(2,1)S(1)}, bf16[128,1920]{1,0:T(8,128)(2,1)S(1)}, u32[]{:S(2)}, u32[]{:S(2)}) %collective-permute-start.15) | collective-permute-done | bytes 491552 | tf_op jit(solution)/shard_map/ppermute | solution.py:220
  93.3 2.4 %collective-permute-start.17 = (bf16[64,1920]{1,0:T(8,128)(2,1)S(1)}, bf16[64,1920]{1,0:T(8,128)(2,1)S(1)}, u32[]{:S(2)}, u32[]{:S(2)}) collective-permute-start(bf16[64,1920]{1,0:T(8,128)(2,1)S(1)} %get-tuple-element.45.refs_2_), channel_id=1, source_target_pairs={{0,16},{4,20},{8,24},{12,28},{16,0},{20,4},{24,8},{28,12},{1,17},{... | collective-permute-start | bytes 737288 | tf_op jit(solution)/shard_map/ppermute | solution.py:220
  95.9 2.1 %collective-permute-start.16 = (bf16[64,1920]{1,0:T(8,128)(2,1)S(1)}, bf16[64,1920]{1,0:T(8,128)(2,1)S(1)}, u32[]{:S(2)}, u32[]{:S(2)}) collective-permute-start(bf16[64,1920]{1,0:T(8,128)(2,1)S(1)} %get-tuple-element.46.refs_2_), channel_id=1, source_target_pairs={{0,16},{4,20},{8,24},{12,28},{16,0},{20,4},{24,8},{28,12},{1,17},{... | collective-permute-start | bytes 737288 | tf_op jit(solution)/shard_map/ppermute | solution.py:220
  98.0 14.1 %collective-permute-done.17.refs_0_ = bf16[64,1920]{1,0:T(8,128)(2,1)S(1)} collective-permute-done((bf16[64,1920]{1,0:T(8,128)(2,1)S(1)}, bf16[64,1920]{1,0:T(8,128)(2,1)S(1)}, u32[]{:S(2)}, u32[]{:S(2)}) %collective-permute-start.17) | collective-permute-done | bytes 245792 | tf_op jit(solution)/shard_map/ppermute | solution.py:220
  112.7 7.1 %collective-permute-done.16.refs_0_ = bf16[64,1920]{1,0:T(8,128)(2,1)S(1)} collective-permute-done((bf16[64,1920]{1,0:T(8,128)(2,1)S(1)}, bf16[64,1920]{1,0:T(8,128)(2,1)S(1)}, u32[]{:S(2)}, u32[]{:S(2)}) %collective-permute-start.16) | collective-permute-done | bytes 245792 | tf_op jit(solution)/shard_map/ppermute | solution.py:220
  120.5 1.7 %collective-permute-done.19.refs_1_ = bf16[64,896]{1,0:T(8,128)(2,1)S(1)} collective-permute-done((bf16[64,896]{1,0:T(8,128)(2,1)S(1)}, bf16[64,896]{1,0:T(8,128)(2,1)S(1)}, u32[]{:S(2)}, u32[]{:S(2)}) %collective-permute-start.19) | collective-permute-done | bytes 114720 | tf_op jit(solution)/shard_map/ppermute | solution.py:220
  122.2 2.2 %collective-permute-start.21 = (bf16[128,896]{1,0:T(8,128)(2,1)S(1)}, bf16[128,896]{1,0:T(8,128)(2,1)S(1)}, u32[]{:S(2)}, u32[]{:S(2)}) collective-permute-start(bf16[128,896]{1,0:T(8,128)(2,1)S(1)} %shard_map.160.refs_2_.refs_0_), channel_id=1, source_target_pairs={{0,8},{4,12},{8,0},{12,4},{16,24},{20,28},{24,16},{28,20},{1,9},{5... | collective-permute-start | bytes 688136 | tf_op jit(solution)/shard_map/ppermute | solution.py:220
  124.4 2.9 %collective-permute-done.18.refs_1_ = bf16[64,896]{1,0:T(8,128)(2,1)S(1)} collective-permute-done((bf16[64,896]{1,0:T(8,128)(2,1)S(1)}, bf16[64,896]{1,0:T(8,128)(2,1)S(1)}, u32[]{:S(2)}, u32[]{:S(2)}) %collective-permute-start.18) | collective-permute-done | bytes 114720 | tf_op jit(solution)/shard_map/ppermute | solution.py:220
  127.3 1.5 collective-permute-start.20
  128.8 2.4 %collective-permute-done.21.refs_1_ = bf16[128,896]{1,0:T(8,128)(2,1)S(1)} collective-permute-done((bf16[128,896]{1,0:T(8,128)(2,1)S(1)}, bf16[128,896]{1,0:T(8,128)(2,1)S(1)}, u32[]{:S(2)}, u32[]{:S(2)}) %collective-permute-start.21) | collective-permute-done | bytes 229408 | tf_op jit(solution)/shard_map/ppermute | solution.py:220
  131.3 1.2 collective-permute-start.23
  133.6 2.1 %collective-permute-start.22 = (bf16[256,896]{1,0:T(8,128)(2,1)S(1)}, bf16[256,896]{1,0:T(8,128)(2,1)S(1)}, u32[]{:S(2)}, u32[]{:S(2)}) collective-permute-start(bf16[256,896]{1,0:T(8,128)(2,1)S(1)} %shard_map.164.refs_1_.refs_4_), channel_id=1, source_target_pairs={{0,8},{4,12},{8,0},{12,4},{16,24},{20,28},{24,16},{28,20},{1,9},{5... | collective-permute-start | bytes 1376264 | tf_op jit(solution)/shard_map/ppermute | solution.py:220
  136.7 6.9 %collective-permute-done.23.refs_1_ = bf16[256,896]{1,0:T(8,128)(2,1)S(1)} collective-permute-done((bf16[256,896]{1,0:T(8,128)(2,1)S(1)}, bf16[256,896]{1,0:T(8,128)(2,1)S(1)}, u32[]{:S(2)}, u32[]{:S(2)}) %collective-permute-start.23) | collective-permute-done | bytes 458784 | tf_op jit(solution)/shard_map/ppermute | solution.py:220
  147.2 1.3 collective-permute-done.24
  148.6 1.3 collective-permute-start.25
  149.9 3.0 %collective-permute-done.25 = bf16[64,512]{1,0:T(8,128)(2,1)S(1)} collective-permute-done((bf16[64,512]{1,0:T(8,128)(2,1)S(1)}, bf16[64,512]{1,0:T(8,128)(2,1)S(1)}, u32[]{:S(2)}, u32[]{:S(2)}) %collective-permute-start.25) | collective-permute-done | bytes 65568 | tf_op jit(solution)/shard_map/ppermute | solution.py:233
  (85 shorter events, 19.9 us)
Async XLA Ops:
  0.0 16.2 %all-to-all-start = ((bf16[8,32,512]{2,1,0:T(8,128)(2,1)}), bf16[8,32,512]{2,1,0:T(8,128)(2,1)S(1)}, u32[]{:S(2)}, u32[]{:S(2)}) async-start(bf16[8,32,512]{2,1,0:T(8,128)(2,1)} %bitcast.8), calls=%async_computation | async-start | bytes 524288 | tf_op jit(solution)/shard_map/all_to_all | solution.py:825
  16.8 2.5 %copy-start.14 = (s32[32]{0:T(128)S(1)}, s32[32]{0:T(128)}, u32[]{:S(2)}) copy-start(s32[32]{0:T(128)} %param.22) | copy-start | bytes 388
  16.8 2.8 %copy-start.11 = (f32[4096]{0:T(1024)S(1)}, f32[4096]{0:T(1024)}, u32[]{:S(2)}) copy-start(f32[4096]{0:T(1024)} %param.15) | copy-start | bytes 49156
  16.8 2.8 %copy-start.13 = (s32[32]{0:T(128)S(1)}, s32[32]{0:T(128)}, u32[]{:S(2)}) copy-start(s32[32]{0:T(128)} %limits_ref.1) | copy-start | bytes 388
  16.8 36.7 %collective-permute-start.4 = (bf16[768,896]{1,0:T(8,128)(2,1)}, bf16[768,896]{1,0:T(8,128)(2,1)S(1)}, u32[]{:S(2)}, u32[]{:S(2)}) collective-permute-start(bf16[768,896]{1,0:T(8,128)(2,1)} %shard_map.141), channel_id=1, source_target_pairs={{0,4},{4,0},{8,12},{12,8},{16,20},{20,16},{24,28},{28,24},{1,5},{5... | collective-permute-start | bytes 4128776 | tf_op jit(solution)/shard_map/ppermute | solution.py:220
  18.2 22.5 %collective-permute-start.1 = (bf16[512,896]{1,0:T(8,128)(2,1)}, bf16[512,896]{1,0:T(8,128)(2,1)S(1)}, u32[]{:S(2)}, u32[]{:S(2)}) collective-permute-start(bf16[512,896]{1,0:T(8,128)(2,1)} %shard_map.138), channel_id=1, source_target_pairs={{0,8},{4,12},{8,0},{12,4},{16,24},{20,28},{24,16},{28,20},{1,9},{5... | collective-permute-start | bytes 2752520 | tf_op jit(solution)/shard_map/ppermute | solution.py:220
  19.6 3.4 %copy-start.3 = (bf16[4096,1024]{1,0:T(8,128)(2,1)S(1)}, bf16[4096,1024]{1,0:T(8,128)(2,1)}, u32[]{:S(2)}) copy-start(bf16[4096,1024]{1,0:T(8,128)(2,1)} %query_ref.1) | copy-start | bytes 25165828
  22.9 1.6 %copy-start.5 = (bf16[4096,256]{1,0:T(8,128)(2,1)S(1)}, bf16[4096,256]{1,0:T(8,128)(2,1)}, u32[]{:S(2)}) copy-start(bf16[4096,256]{1,0:T(8,128)(2,1)} %key_ref.1) | copy-start | bytes 6291460
  24.5 1.6 %copy-start.6 = (bf16[4096,256]{1,0:T(8,128)(2,1)S(1)}, bf16[4096,256]{1,0:T(8,128)(2,1)}, u32[]{:S(2)}) copy-start(bf16[4096,256]{1,0:T(8,128)(2,1)} %value_ref.1) | copy-start | bytes 6291460
  26.1 11.4 %copy-start.4 = (bf16[4096,512]{1,0:T(8,128)(2,1)S(1)}, bf16[4096,512]{1,0:T(8,128)(2,1)}, u32[]{:S(2)}) copy-start(bf16[4096,512]{1,0:T(8,128)(2,1)} %refs_1_.1) | copy-start | bytes 12582916
  26.1 11.4 %copy-start.7 = (bf16[256,512]{1,0:T(8,128)(2,1)S(1)}, bf16[256,512]{1,0:T(8,128)(2,1)}, u32[]{:S(2)}) copy-start(bf16[256,512]{1,0:T(8,128)(2,1)} %refs_2_.7) | copy-start | bytes 786436
  35.0 5.7 %collective-permute-start = (bf16[32,1024]{1,0:T(8,128)(2,1)S(1)}, bf16[32,1024]{1,0:T(8,128)(2,1)S(1)}, u32[]{:S(2)}, u32[]{:S(2)}) collective-permute-start(bf16[32,1024]{1,0:T(8,128)(2,1)S(1)} %shard_map.136.refs_3_.refs_0_), channel_id=1, source_target_pairs={{0,16},{4,20},{8,24},{12,28},{16,0},{20,4},{24,8},{28,12},{1,17},{... | collective-permute-start | bytes 196616 | tf_op jit(solution)/shard_map/ppermute | solution.py:220
  38.4 8.4 %copy-start.8 = (bf16[256,512]{1,0:T(8,128)(2,1)}, bf16[256,512]{1,0:T(8,128)(2,1)S(1)}, u32[]{:S(2)}) copy-start(bf16[256,512]{1,0:T(8,128)(2,1)S(1)} %get-tuple-element.33.refs_2_.refs_3_) | copy-start | bytes 786436
  40.7 5.4 %collective-permute-start.2 = (bf16[64,1024]{1,0:T(8,128)(2,1)S(1)}, bf16[64,1024]{1,0:T(8,128)(2,1)S(1)}, u32[]{:S(2)}, u32[]{:S(2)}) collective-permute-start(bf16[64,1024]{1,0:T(8,128)(2,1)S(1)} %shard_map.139.refs_0_.refs_2_), channel_id=1, source_target_pairs={{0,8},{4,12},{8,0},{12,4},{16,24},{20,28},{24,16},{28,20},{1,9},{5... | collective-permute-start | bytes 393224 | tf_op jit(solution)/shard_map/ppermute | solution.py:220
  46.8 6.7 %collective-permute-start.3 = (bf16[128,1024]{1,0:T(8,128)(2,1)}, bf16[128,1024]{1,0:T(8,128)(2,1)}, u32[]{:S(2)}, u32[]{:S(2)}) collective-permute-start(bf16[128,1024]{1,0:T(8,128)(2,1)} %shard_map.140.refs_0_.refs_2_), channel_id=1, source_target_pairs={{0,4},{4,0},{8,12},{12,8},{16,20},{20,16},{24,28},{28,24},{1,5},{5... | collective-permute-start | bytes 786440 | tf_op jit(solution)/shard_map/ppermute | solution.py:220
  48.7 31.8 %collective-permute-start.11 = (bf16[512,896]{1,0:T(8,128)(2,1)}, bf16[512,896]{1,0:T(8,128)(2,1)}, u32[]{:S(2)}, u32[]{:S(2)}) collective-permute-start(bf16[512,896]{1,0:T(8,128)(2,1)} %shard_map.152), channel_id=1, source_target_pairs={{0,8},{4,12},{8,0},{12,4},{16,24},{20,28},{24,16},{28,20},{1,9},{5... | collective-permute-start | bytes 2752520 | tf_op jit(solution)/shard_map/ppermute | solution.py:220
  54.6 9.0 %copy-start.12 = (f32[512]{0:T(512)S(1)}, f32[512]{0:T(512)}, u32[]{:S(2)}) copy-start(f32[512]{0:T(512)} %param.24) | copy-start | bytes 6148
  55.0 14.6 %copy-start.10 = (bf16[256,512]{1,0:T(8,128)(2,1)S(1)}, bf16[256,512]{1,0:T(8,128)(2,1)}, u32[]{:S(2)}) copy-start(bf16[256,512]{1,0:T(8,128)(2,1)} %copy-done.8) | copy-start | bytes 786436
  55.1 1.6 %collective-permute-start.5 = (bf16[256,512]{1,0:T(8,128)(2,1)S(1)}, bf16[256,512]{1,0:T(8,128)(2,1)S(1)}, u32[]{:S(2)}, u32[]{:S(2)}) collective-permute-start(bf16[256,512]{1,0:T(8,128)(2,1)S(1)} %shard_map.143.refs_1_.refs_3_), channel_id=1, source_target_pairs={{0,1},{1,0},{2,3},{3,2},{4,5},{5,4},{6,7},{7,6},{8,9},{9,8},{10,11... | collective-permute-start | bytes 786440 | tf_op jit(solution)/shard_map/ppermute | solution.py:233
  57.2 5.6 %collective-permute-start.6 = (bf16[128,512]{1,0:T(8,128)(2,1)S(1)}, bf16[128,512]{1,0:T(8,128)(2,1)S(1)}, u32[]{:S(2)}, u32[]{:S(2)}) collective-permute-start(bf16[128,512]{1,0:T(8,128)(2,1)S(1)} %get-tuple-element.31.refs_2_), channel_id=1, source_target_pairs={{0,2},{1,3},{2,0},{3,1},{4,6},{5,7},{6,4},{7,5},{8,10},{9,11},{10,... | collective-permute-start | bytes 393224 | tf_op jit(solution)/shard_map/ppermute | solution.py:233
  59.4 18.3 %collective-permute-start.13 = (bf16[256,896]{1,0:T(8,128)(2,1)}, bf16[256,896]{1,0:T(8,128)(2,1)S(1)}, u32[]{:S(2)}, u32[]{:S(2)}) collective-permute-start(bf16[256,896]{1,0:T(8,128)(2,1)} %shard_map.153), channel_id=1, source_target_pairs={{0,4},{4,0},{8,12},{12,8},{16,20},{20,16},{24,28},{28,24},{1,5},{5... | collective-permute-start | bytes 1376264 | tf_op jit(solution)/shard_map/ppermute | solution.py:220
  63.6 1.0 copy-start.9
  65.2 11.8 %collective-permute-start.9 = (bf16[128,640]{1,0:T(8,128)(2,1)S(1)}, bf16[128,640]{1,0:T(8,128)(2,1)S(1)}, u32[]{:S(2)}, u32[]{:S(2)}) collective-permute-start(bf16[128,640]{1,0:T(8,128)(2,1)S(1)} %shard_map.146.refs_5_), channel_id=1, source_target_pairs={{0,4},{4,0},{8,12},{12,8},{16,20},{20,16},{24,28},{28,24},{1,5},{5... | collective-permute-start | bytes 491528 | tf_op jit(solution)/shard_map/ppermute | solution.py:220
  66.9 10.4 %collective-permute-start.8 = (bf16[128,640]{1,0:T(8,128)(2,1)S(1)}, bf16[128,640]{1,0:T(8,128)(2,1)S(1)}, u32[]{:S(2)}, u32[]{:S(2)}) collective-permute-start(bf16[128,640]{1,0:T(8,128)(2,1)S(1)} %shard_map.146.refs_5_), channel_id=1, source_target_pairs={{0,8},{4,12},{8,0},{12,4},{16,24},{20,28},{24,16},{28,20},{1,9},{5... | collective-permute-start | bytes 491528 | tf_op jit(solution)/shard_map/ppermute | solution.py:220
  68.3 1.3 collective-permute-start.7
  70.4 2.0 %copy-start.1 = (bf16[512,3584]{1,0:T(8,128)(2,1)S(1)}, bf16[512,3584]{1,0:T(8,128)(2,1)}, u32[]{:S(2)}) copy-start(bf16[512,3584]{1,0:T(8,128)(2,1)} %refs_3_.3) | copy-start | bytes 11010052
  72.5 2.0 %copy-start.2 = (bf16[512,3584]{1,0:T(8,128)(2,1)S(1)}, bf16[512,3584]{1,0:T(8,128)(2,1)}, u32[]{:S(2)}) copy-start(bf16[512,3584]{1,0:T(8,128)(2,1)} %refs_2_.9) | copy-start | bytes 11010052
  77.1 1.5 collective-permute-start.12
  77.3 3.2 %collective-permute-start.10 = (bf16[128,640]{1,0:T(8,128)(2,1)S(1)}, bf16[128,640]{1,0:T(8,128)(2,1)S(1)}, u32[]{:S(2)}, u32[]{:S(2)}) collective-permute-start(bf16[128,640]{1,0:T(8,128)(2,1)S(1)} %shard_map.151.refs_8_.refs_3_), channel_id=1, source_target_pairs={{0,1},{1,0},{2,3},{3,2},{4,5},{5,4},{6,7},{7,6},{8,9},{9,8},{10,11... | collective-permute-start | bytes 491528 | tf_op jit(solution)/shard_map/ppermute | solution.py:233
  79.8 13.3 %collective-permute-start.15 = (bf16[128,1920]{1,0:T(8,128)(2,1)S(1)}, bf16[128,1920]{1,0:T(8,128)(2,1)S(1)}, u32[]{:S(2)}, u32[]{:S(2)}) collective-permute-start(bf16[128,1920]{1,0:T(8,128)(2,1)S(1)} %get-tuple-element.41.refs_8_), channel_id=1, source_target_pairs={{0,8},{4,12},{8,0},{12,4},{16,24},{20,28},{24,16},{28,20},{1,9},{5... | collective-permute-start | bytes 1474568 | tf_op jit(solution)/shard_map/ppermute | solution.py:220
  82.4 13.3 %collective-permute-start.14 = (bf16[128,1920]{1,0:T(8,128)(2,1)S(1)}, bf16[128,1920]{1,0:T(8,128)(2,1)S(1)}, u32[]{:S(2)}, u32[]{:S(2)}) collective-permute-start(bf16[128,1920]{1,0:T(8,128)(2,1)S(1)} %get-tuple-element.42.refs_2_), channel_id=1, source_target_pairs={{0,4},{4,0},{8,12},{12,8},{16,20},{20,16},{24,28},{28,24},{1,5},{5... | collective-permute-start | bytes 1474568 | tf_op jit(solution)/shard_map/ppermute | solution.py:220
  93.3 39.2 %copy-start = (bf16[3584,512]{1,0:T(8,128)(2,1)S(1)}, bf16[3584,512]{1,0:T(8,128)(2,1)}, u32[]{:S(2)}) copy-start(bf16[3584,512]{1,0:T(8,128)(2,1)} %refs_2_.13) | copy-start | bytes 11010052
  93.3 18.8 %collective-permute-start.17 = (bf16[64,1920]{1,0:T(8,128)(2,1)S(1)}, bf16[64,1920]{1,0:T(8,128)(2,1)S(1)}, u32[]{:S(2)}, u32[]{:S(2)}) collective-permute-start(bf16[64,1920]{1,0:T(8,128)(2,1)S(1)} %get-tuple-element.45.refs_2_), channel_id=1, source_target_pairs={{0,16},{4,20},{8,24},{12,28},{16,0},{20,4},{24,8},{28,12},{1,17},{... | collective-permute-start | bytes 737288 | tf_op jit(solution)/shard_map/ppermute | solution.py:220
  95.9 24.0 %collective-permute-start.16 = (bf16[64,1920]{1,0:T(8,128)(2,1)S(1)}, bf16[64,1920]{1,0:T(8,128)(2,1)S(1)}, u32[]{:S(2)}, u32[]{:S(2)}) collective-permute-start(bf16[64,1920]{1,0:T(8,128)(2,1)S(1)} %get-tuple-element.46.refs_2_), channel_id=1, source_target_pairs={{0,16},{4,20},{8,24},{12,28},{16,0},{20,4},{24,8},{28,12},{1,17},{... | collective-permute-start | bytes 737288 | tf_op jit(solution)/shard_map/ppermute | solution.py:220
  112.7 9.4 %collective-permute-start.19 = (bf16[64,896]{1,0:T(8,128)(2,1)S(1)}, bf16[64,896]{1,0:T(8,128)(2,1)S(1)}, u32[]{:S(2)}, u32[]{:S(2)}) collective-permute-start(bf16[64,896]{1,0:T(8,128)(2,1)S(1)} %get-tuple-element.49.refs_2_.refs_0_), channel_id=1, source_target_pairs={{0,16},{4,20},{8,24},{12,28},{16,0},{20,4},{24,8},{28,12},{1,17},{... | collective-permute-start | bytes 344072 | tf_op jit(solution)/shard_map/ppermute | solution.py:220
  120.5 6.9 %collective-permute-start.18 = (bf16[64,896]{1,0:T(8,128)(2,1)S(1)}, bf16[64,896]{1,0:T(8,128)(2,1)S(1)}, u32[]{:S(2)}, u32[]{:S(2)}) collective-permute-start(bf16[64,896]{1,0:T(8,128)(2,1)S(1)} %get-tuple-element.50.refs_2_.refs_0_), channel_id=1, source_target_pairs={{0,16},{4,20},{8,24},{12,28},{16,0},{20,4},{24,8},{28,12},{1,17},{... | collective-permute-start | bytes 344072 | tf_op jit(solution)/shard_map/ppermute | solution.py:220
  122.2 9.0 %collective-permute-start.21 = (bf16[128,896]{1,0:T(8,128)(2,1)S(1)}, bf16[128,896]{1,0:T(8,128)(2,1)S(1)}, u32[]{:S(2)}, u32[]{:S(2)}) collective-permute-start(bf16[128,896]{1,0:T(8,128)(2,1)S(1)} %shard_map.160.refs_2_.refs_0_), channel_id=1, source_target_pairs={{0,8},{4,12},{8,0},{12,4},{16,24},{20,28},{24,16},{28,20},{1,9},{5... | collective-permute-start | bytes 688136 | tf_op jit(solution)/shard_map/ppermute | solution.py:220
  127.3 6.2 %collective-permute-start.20 = (bf16[128,896]{1,0:T(8,128)(2,1)S(1)}, bf16[128,896]{1,0:T(8,128)(2,1)S(1)}, u32[]{:S(2)}, u32[]{:S(2)}) collective-permute-start(bf16[128,896]{1,0:T(8,128)(2,1)S(1)} %shard_map.161.refs_2_.refs_0_), channel_id=1, source_target_pairs={{0,4},{4,0},{8,12},{12,8},{16,20},{20,16},{24,28},{28,24},{1,5},{5... | collective-permute-start | bytes 688136 | tf_op jit(solution)/shard_map/ppermute | solution.py:220
  131.3 12.3 %collective-permute-start.23 = (bf16[256,896]{1,0:T(8,128)(2,1)S(1)}, bf16[256,896]{1,0:T(8,128)(2,1)S(1)}, u32[]{:S(2)}, u32[]{:S(2)}) collective-permute-start(bf16[256,896]{1,0:T(8,128)(2,1)S(1)} %shard_map.162.refs_1_.refs_3_), channel_id=1, source_target_pairs={{0,4},{4,0},{8,12},{12,8},{16,20},{20,16},{24,28},{28,24},{1,5},{5... | collective-permute-start | bytes 1376264 | tf_op jit(solution)/shard_map/ppermute | solution.py:220
  133.6 11.8 %collective-permute-start.22 = (bf16[256,896]{1,0:T(8,128)(2,1)S(1)}, bf16[256,896]{1,0:T(8,128)(2,1)S(1)}, u32[]{:S(2)}, u32[]{:S(2)}) collective-permute-start(bf16[256,896]{1,0:T(8,128)(2,1)S(1)} %shard_map.164.refs_1_.refs_4_), channel_id=1, source_target_pairs={{0,8},{4,12},{8,0},{12,4},{16,24},{20,28},{24,16},{28,20},{1,9},{5... | collective-permute-start | bytes 1376264 | tf_op jit(solution)/shard_map/ppermute | solution.py:220
  147.1 1.4 collective-permute-start.24
  148.6 4.3 %collective-permute-start.25 = (bf16[64,512]{1,0:T(8,128)(2,1)S(1)}, bf16[64,512]{1,0:T(8,128)(2,1)S(1)}, u32[]{:S(2)}, u32[]{:S(2)}) collective-permute-start(bf16[64,512]{1,0:T(8,128)(2,1)S(1)} %dynamic-slice_convert_fusion), channel_id=1, source_target_pairs={{0,2},{1,3},{2,0},{3,1},{4,6},{5,7},{6,4},{7,5},{8,10},{9,11},{10,... | collective-permute-start | bytes 196616 | tf_op jit(solution)/shard_map/ppermute | solution.py:233

commit v6 on v4

--- a/solution.py
+++ b/solution.py
@@ -660,7 +660,7 @@
 
 def areas_of(columns):
     tiles = columns // 128
-    return tiles // 4 * 128, tiles // 4 * 128
+    return tiles * 8 // 28 * 128, tiles * 6 // 28 * 128
 
 
 def plan(columns, bits):

time: 154 us -> 170 us (1.10)
  waiting for transfers between devices: 65.4 us -> 80.7 us
  local copies, waits for them, and re-layouts: 20.9 us -> 23.3 us
  Pallas kernels: 25.4 us -> 23.1 us
    ppermute x19, waiting for transfers between devices: 55 us -> 73 us  [exchange(): return lax.ppermute(value, 'req', [(i, i ^ 1 << bit) for i in range(size)])]
    pallas_call x26, Pallas kernels: 16.4 us -> 14.2 us  [run(): pl.pallas_call(kernel, out_shape=outs, in_specs=[*specs, *[pl.BlockSpec(m...]
    ppermute x7, waiting for transfers between devices: 9.5 us -> 7.61 us  [kv_exchange(): return lax.ppermute(value, 'kv', [(i, i ^ 1 << bit) for i in range(size)])]
    dynamic_slice x2 -> x3, local copies, waits for them, and re-layouts: 4.73 us -> 5.44 us  [shards(): lax.dynamic_slice_in_dim(v, first, area, 1)]
  transfers between devices with their start and end apart: 27 -> 27, of which waited for: 18 -> 17; matrix products, arithmetic and copies ran while one was open for 7% -> 7% of each run, Pallas kernels for 15% -> 12%
where the time goes in v6:
time: 170 us; the launch traced here: 168 us
  waiting for transfers between devices  80.7 us (47%)
  starting transfers between devices  38.4 us (23%)
  local copies, waits for them, and re-layouts  23.3 us (14%)
  Pallas kernels  23.1 us (14%)
  other arithmetic  2.28 us (1%)
    ppermute x19, waiting for transfers between devices, exchange(): return lax.ppermute(value, 'req', [(i, i ^ 1 << bit) for i in range(size)])  73 us
    ppermute x19, starting transfers between devices, exchange(): return lax.ppermute(value, 'req', [(i, i ^ 1 << bit) for i in range(size)])  28.6 us
    pallas_call x26, Pallas kernels, run(): pl.pallas_call(kernel, out_shape=outs, in_specs=[*specs, *[pl.BlockSpec(m...  14.2 us
    unnamed x30, local copies, waits for them, and re-layouts  13.1 us
    pallas_call x1, Pallas kernels, attention(): pl.pallas_call(body, out_shape=array((rows, heads * head_size), jnp.bfloa...  8.91 us
    ppermute x7, waiting for transfers between devices, kv_exchange(): return lax.ppermute(value, 'kv', [(i, i ^ 1 << bit) for i in range(size)])  7.61 us
    all_to_all x1, starting transfers between devices, shards(): lax.all_to_all(residual_in.reshape(req_size, local_rows, -1), 'req', spli...  7.25 us
    dynamic_slice x3, local copies, waits for them, and re-layouts, shards(): lax.dynamic_slice_in_dim(v, first, area, 1)  5.44 us
  transfers between devices with their start and end apart: 27, of which 17 were waited for; matrix products, arithmetic and copies ran while one was open for 7% of the time, Pallas kernels for 12%

profile of v6, /device:TPU:0, one launch (start us, length us, event | category | flops | bytes accessed | tf_op | source)
XLA Modules:
  0.0 168.2 jit_solution(8265679235632241426)
XLA Ops:
  0.0 7.3 %all-to-all-start = ((bf16[8,32,512]{2,1,0:T(8,128)(2,1)}), bf16[8,32,512]{2,1,0:T(8,128)(2,1)S(1)}, u32[]{:S(2)}, u32[]{:S(2)}) async-start(bf16[8,32,512]{2,1,0:T(8,128)(2,1)} %bitcast.8), calls=%async_computation | async-start | bytes 524288 | tf_op jit(solution)/shard_map/all_to_all | solution.py:774
  7.3 2.1 %constant_dynamic-slice_fusion.5.refs_0_.refs_3_ = bf16[512,768]{1,0:T(8,128)(2,1)} fusion(bf16[512,3584]{1,0:T(8,128)(2,1)} %refs_2_.5, s32[]{:T(128)S(6)} %select_n.27), kind=kLoop, calls=%fused_computation.15 | loop fusion | bytes 1572868 | tf_op jit(solution)/shard_map/dynamic_slice | solution.py:783
  9.3 2.1 %constant_dynamic-slice_fusion.3.refs_4_.refs_0_ = bf16[512,768]{1,0:T(8,128)(2,1)} fusion(bf16[512,3584]{1,0:T(8,128)(2,1)} %refs_3_.5, s32[]{:T(128)S(6)} %select_n.27), kind=kLoop, calls=%fused_computation.13 | loop fusion | bytes 1572868 | tf_op jit(solution)/shard_map/dynamic_slice | solution.py:783
  11.4 1.3 constant_dynamic-slice_fusion.4
  12.7 2.1 %fusion.2 = (bf16[256,1024]{1,0:T(8,128)(2,1)}, bf16[256,1024]{1,0:T(8,128)(2,1)S(1)}) fusion(bf16[512,3584]{1,0:T(8,128)(2,1)} %refs_3_.5, s32[]{:T(128)S(6)} %add.48, s32[]{:T(128)S(6)} %select_n.28), kind=kLoop, calls=%fused_computation.18 | loop fusion | bytes 2097160 | tf_op jit(solution)/shard_map/slice | solution.py:786
  14.8 1.3 pad_maximum_fusion.refs_0_
  16.8 1.9 %collective-permute-start.4 = (bf16[768,1024]{1,0:T(8,128)(2,1)}, bf16[768,1024]{1,0:T(8,128)(2,1)S(1)}, u32[]{:S(2)}, u32[]{:S(2)}) collective-permute-start(bf16[768,1024]{1,0:T(8,128)(2,1)} %shard_map.141), channel_id=1, source_target_pairs={{0,4},{4,0},{8,12},{12,8},{16,20},{20,16},{24,28},{28,24},{1,5},{5... | collective-permute-start | bytes 4718600 | tf_op jit(solution)/shard_map/ppermute | solution.py:220
  18.7 1.5 collective-permute-start.1
  20.4 3.4 %copy-done.3 = bf16[4096,1024]{1,0:T(8,128)(2,1)S(1)} copy-done((bf16[4096,1024]{1,0:T(8,128)(2,1)S(1)}, bf16[4096,1024]{1,0:T(8,128)(2,1)}, u32[]{:S(2)}) %copy-start.3) | copy-done | bytes 8388632
  23.8 1.6 copy-done.5
  25.4 1.6 copy-done.6
  27.0 8.9 %shard_map.136.refs_3_.refs_0_ = bf16[32,1024]{1,0:T(8,128)(2,1)S(1)} custom-call(bf16[8,32,512]{2,1,0:T(8,128)(2,1)S(1)} %all-to-all-done.tokens_ref, f32[1,4096]{1,0:T(1,128)S(1)} %bitcast.9, bf16[4096,1024]{1,0:T(8,128)(2,1)S(1)} %copy-done.3, bf16[4096,256]{1,0:T(8,128)(2,1)S(1)} %copy-done.5, bf16[4096,256]{1,0:T(8,128)(2,1)S(1)} %copy-done.6, ...), custom_call_target="tpu_custom_call" | custom-call | tf_op jit(solution)/shard_map/pallas_call | solution.py:190
  35.9 2.4 %collective-permute-start = (bf16[32,1024]{1,0:T(8,128)(2,1)S(1)}, bf16[32,1024]{1,0:T(8,128)(2,1)S(1)}, u32[]{:S(2)}, u32[]{:S(2)}) collective-permute-start(bf16[32,1024]{1,0:T(8,128)(2,1)S(1)} %shard_map.136.refs_3_.refs_0_), channel_id=1, source_target_pairs={{0,16},{4,20},{8,24},{12,28},{16,0},{20,4},{24,8},{28,12},{1,17},{... | collective-permute-start | bytes 196616 | tf_op jit(solution)/shard_map/ppermute | solution.py:220
  39.3 2.6 %collective-permute-done.refs_1_ = bf16[32,1024]{1,0:T(8,128)(2,1)S(1)} collective-permute-done((bf16[32,1024]{1,0:T(8,128)(2,1)S(1)}, bf16[32,1024]{1,0:T(8,128)(2,1)S(1)}, u32[]{:S(2)}, u32[]{:S(2)}) %collective-permute-start) | collective-permute-done | bytes 65568 | tf_op jit(solution)/shard_map/ppermute | solution.py:220
  41.9 5.0 %collective-permute-done.2.refs_1_ = bf16[64,1024]{1,0:T(8,128)(2,1)S(1)} collective-permute-done((bf16[64,1024]{1,0:T(8,128)(2,1)S(1)}, bf16[64,1024]{1,0:T(8,128)(2,1)S(1)}, u32[]{:S(2)}, u32[]{:S(2)}) %collective-permute-start.2) | collective-permute-done | bytes 131104 | tf_op jit(solution)/shard_map/ppermute | solution.py:220
  47.1 11.3 %collective-permute-done.3.refs_1_ = bf16[128,1024]{1,0:T(8,128)(2,1)S(1)} collective-permute-done((bf16[128,1024]{1,0:T(8,128)(2,1)S(1)}, bf16[128,1024]{1,0:T(8,128)(2,1)S(1)}, u32[]{:S(2)}, u32[]{:S(2)}) %collective-permute-start.3) | collective-permute-done | bytes 262176 | tf_op jit(solution)/shard_map/ppermute | solution.py:220
  59.5 1.7 %collective-permute-start.13 = (bf16[256,1024]{1,0:T(8,128)(2,1)}, bf16[256,1024]{1,0:T(8,128)(2,1)}, u32[]{:S(2)}, u32[]{:S(2)}) collective-permute-start(bf16[256,1024]{1,0:T(8,128)(2,1)} %shard_map.153), channel_id=1, source_target_pairs={{0,4},{4,0},{8,12},{12,8},{16,20},{20,16},{24,28},{28,24},{1,5},{5... | collective-permute-start | bytes 1572872 | tf_op jit(solution)/shard_map/ppermute | solution.py:220
  62.0 0.9 copy-done.9
  63.5 1.6 collective-permute-start.6
  65.7 1.5 collective-permute-start.11
  67.2 2.0 %collective-permute-done.6.refs_1_ = bf16[128,512]{1,0:T(8,128)(2,1)S(1)} collective-permute-done((bf16[128,512]{1,0:T(8,128)(2,1)S(1)}, bf16[128,512]{1,0:T(8,128)(2,1)S(1)}, u32[]{:S(2)}, u32[]{:S(2)}) %collective-permute-start.6) | collective-permute-done | bytes 131104 | tf_op jit(solution)/shard_map/ppermute | solution.py:233
  71.5 1.5 collective-permute-start.8
  74.5 2.0 %copy-done = bf16[512,3584]{1,0:T(8,128)(2,1)S(1)} copy-done((bf16[512,3584]{1,0:T(8,128)(2,1)S(1)}, bf16[512,3584]{1,0:T(8,128)(2,1)}, u32[]{:S(2)}) %copy-start) | copy-done | bytes 3670040
  76.6 2.0 %copy-done.1 = bf16[512,3584]{1,0:T(8,128)(2,1)S(1)} copy-done((bf16[512,3584]{1,0:T(8,128)(2,1)S(1)}, bf16[512,3584]{1,0:T(8,128)(2,1)}, u32[]{:S(2)}) %copy-start.1) | copy-done | bytes 3670040
  78.6 1.3 shard_map.148
  79.9 1.1 shard_map.149
  81.3 7.5 %collective-permute-done.8.refs_0_ = bf16[128,640]{1,0:T(8,128)(2,1)S(1)} collective-permute-done((bf16[128,640]{1,0:T(8,128)(2,1)S(1)}, bf16[128,640]{1,0:T(8,128)(2,1)S(1)}, u32[]{:S(2)}, u32[]{:S(2)}) %collective-permute-start.8) | collective-permute-done | bytes 163872 | tf_op jit(solution)/shard_map/ppermute | solution.py:220
  88.8 1.8 %shard_map.154 = (bf16[128,2176]{1,0:T(8,128)(2,1)S(1)}, bf16[128,2176]{1,0:T(8,128)(2,1)S(1)}) custom-call(s32[3]{0:T(128)S(1)} %pad_add_fusion.refs_0_, bf16[128,2048]{1,0:T(8,128)(2,1)S(1)} %get-tuple-element.36.refs_4_.refs_1_, bf16[128,2048]{1,0:T(8,128)(2,1)S(1)} %get-tuple-element.40.refs_2_, bf16[128,640]{1,0:T(8,128)(2,1)S(1)} %shard_map.150.refs_1_.refs_3_, ...), custom_call_target="tpu_custom_call" | custom-call | tf_op jit(solution)/shard_map/pallas_call | solution.py:249
  90.7 1.5 collective-permute-start.15
  92.2 1.4 collective-permute-done.10.refs_4_
  93.6 1.2 shard_map.155
  94.8 0.9 collective-permute-start.14
  95.7 8.7 %collective-permute-done.15.refs_0_ = bf16[128,2176]{1,0:T(8,128)(2,1)S(1)} collective-permute-done((bf16[128,2176]{1,0:T(8,128)(2,1)S(1)}, bf16[128,2176]{1,0:T(8,128)(2,1)S(1)}, u32[]{:S(2)}, u32[]{:S(2)}) %collective-permute-start.15) | collective-permute-done | bytes 557088 | tf_op jit(solution)/shard_map/ppermute | solution.py:220
  104.5 2.4 %collective-permute-start.17 = (bf16[64,2176]{1,0:T(8,128)(2,1)S(1)}, bf16[64,2176]{1,0:T(8,128)(2,1)S(1)}, u32[]{:S(2)}, u32[]{:S(2)}) collective-permute-start(bf16[64,2176]{1,0:T(8,128)(2,1)S(1)} %get-tuple-element.45.refs_2_), channel_id=1, source_target_pairs={{0,16},{4,20},{8,24},{12,28},{16,0},{20,4},{24,8},{28,12},{1,17},{... | collective-permute-start | bytes 835592 | tf_op jit(solution)/shard_map/ppermute | solution.py:220
  107.0 2.2 %collective-permute-start.16 = (bf16[64,1664]{1,0:T(8,128)(2,1)S(1)}, bf16[64,1664]{1,0:T(8,128)(2,1)S(1)}, u32[]{:S(2)}, u32[]{:S(2)}) collective-permute-start(bf16[64,1664]{1,0:T(8,128)(2,1)S(1)} %get-tuple-element.46.refs_2_), channel_id=1, source_target_pairs={{0,16},{4,20},{8,24},{12,28},{16,0},{20,4},{24,8},{28,12},{1,17},{... | collective-permute-start | bytes 638984 | tf_op jit(solution)/shard_map/ppermute | solution.py:220
  109.2 14.5 %collective-permute-done.17.refs_0_ = bf16[64,2176]{1,0:T(8,128)(2,1)S(1)} collective-permute-done((bf16[64,2176]{1,0:T(8,128)(2,1)S(1)}, bf16[64,2176]{1,0:T(8,128)(2,1)S(1)}, u32[]{:S(2)}, u32[]{:S(2)}) %collective-permute-start.17) | collective-permute-done | bytes 278560 | tf_op jit(solution)/shard_map/ppermute | solution.py:220
  124.4 6.7 %collective-permute-done.16.refs_0_ = bf16[64,1664]{1,0:T(8,128)(2,1)S(1)} collective-permute-done((bf16[64,1664]{1,0:T(8,128)(2,1)S(1)}, bf16[64,1664]{1,0:T(8,128)(2,1)S(1)}, u32[]{:S(2)}, u32[]{:S(2)}) %collective-permute-start.16) | collective-permute-done | bytes 213024 | tf_op jit(solution)/shard_map/ppermute | solution.py:220
  131.8 1.1 collective-permute-done.19.refs_1_
  133.4 3.4 %collective-permute-start.18 = (bf16[64,768]{1,0:T(8,128)(2,1)S(1)}, bf16[64,768]{1,0:T(8,128)(2,1)S(1)}, u32[]{:S(2)}, u32[]{:S(2)}) collective-permute-start(bf16[64,768]{1,0:T(8,128)(2,1)S(1)} %get-tuple-element.50.refs_2_.refs_0_), channel_id=1, source_target_pairs={{0,16},{4,20},{8,24},{12,28},{16,0},{20,4},{24,8},{28,12},{1,17},{... | collective-permute-start | bytes 294920 | tf_op jit(solution)/shard_map/ppermute | solution.py:220
  136.8 4.5 %collective-permute-done.18.refs_1_ = bf16[64,768]{1,0:T(8,128)(2,1)S(1)} collective-permute-done((bf16[64,768]{1,0:T(8,128)(2,1)S(1)}, bf16[64,768]{1,0:T(8,128)(2,1)S(1)}, u32[]{:S(2)}, u32[]{:S(2)}) %collective-permute-start.18) | collective-permute-done | bytes 98336 | tf_op jit(solution)/shard_map/ppermute | solution.py:220
  142.4 1.1 collective-permute-start.23
  143.5 5.7 %collective-permute-done.20.refs_1_ = bf16[128,768]{1,0:T(8,128)(2,1)S(1)} collective-permute-done((bf16[128,768]{1,0:T(8,128)(2,1)S(1)}, bf16[128,768]{1,0:T(8,128)(2,1)S(1)}, u32[]{:S(2)}, u32[]{:S(2)}) %collective-permute-start.20) | collective-permute-done | bytes 196640 | tf_op jit(solution)/shard_map/ppermute | solution.py:220
  149.2 4.2 %collective-permute-start.22 = (bf16[256,768]{1,0:T(8,128)(2,1)S(1)}, bf16[256,768]{1,0:T(8,128)(2,1)S(1)}, u32[]{:S(2)}, u32[]{:S(2)}) collective-permute-start(bf16[256,768]{1,0:T(8,128)(2,1)S(1)} %shard_map.163.refs_4_.refs_1_), channel_id=1, source_target_pairs={{0,8},{4,12},{8,0},{12,4},{16,24},{20,28},{24,16},{28,20},{1,9},{5... | collective-permute-start | bytes 1179656 | tf_op jit(solution)/shard_map/ppermute | solution.py:220
  153.4 5.1 %collective-permute-done.23.refs_2_ = bf16[256,1024]{1,0:T(8,128)(2,1)S(1)} collective-permute-done((bf16[256,1024]{1,0:T(8,128)(2,1)S(1)}, bf16[256,1024]{1,0:T(8,128)(2,1)S(1)}, u32[]{:S(2)}, u32[]{:S(2)}) %collective-permute-start.23) | collective-permute-done | bytes 524320 | tf_op jit(solution)/shard_map/ppermute | solution.py:220
  158.6 1.2 shard_map.164.refs_4_.refs_5_
  159.8 1.1 shard_map.165.refs_1_.refs_2_
  161.8 1.3 collective-permute-done.24
  164.6 2.9 %collective-permute-done.25 = bf16[64,512]{1,0:T(8,128)(2,1)S(1)} collective-permute-done((bf16[64,512]{1,0:T(8,128)(2,1)S(1)}, bf16[64,512]{1,0:T(8,128)(2,1)S(1)}, u32[]{:S(2)}, u32[]{:S(2)}) %collective-permute-start.25) | collective-permute-done | bytes 65568 | tf_op jit(solution)/shard_map/ppermute | solution.py:233
  (84 shorter events, 15.5 us)
Async XLA Ops:
  0.0 16.2 %all-to-all-start = ((bf16[8,32,512]{2,1,0:T(8,128)(2,1)}), bf16[8,32,512]{2,1,0:T(8,128)(2,1)S(1)}, u32[]{:S(2)}, u32[]{:S(2)}) async-start(bf16[8,32,512]{2,1,0:T(8,128)(2,1)} %bitcast.8), calls=%async_computation | async-start | bytes 524288 | tf_op jit(solution)/shard_map/all_to_all | solution.py:774
  16.1 4.1 %copy-start.14 = (s32[32]{0:T(128)S(1)}, s32[32]{0:T(128)}, u32[]{:S(2)}) copy-start(s32[32]{0:T(128)} %param.22) | copy-start | bytes 388
  16.1 4.3 %copy-start.11 = (f32[4096]{0:T(1024)S(1)}, f32[4096]{0:T(1024)}, u32[]{:S(2)}) copy-start(f32[4096]{0:T(1024)} %param.15) | copy-start | bytes 49156
  16.1 4.3 %copy-start.13 = (s32[32]{0:T(128)S(1)}, s32[32]{0:T(128)}, u32[]{:S(2)}) copy-start(s32[32]{0:T(128)} %limits_ref.1) | copy-start | bytes 388
  16.8 41.6 %collective-permute-start.4 = (bf16[768,1024]{1,0:T(8,128)(2,1)}, bf16[768,1024]{1,0:T(8,128)(2,1)S(1)}, u32[]{:S(2)}, u32[]{:S(2)}) collective-permute-start(bf16[768,1024]{1,0:T(8,128)(2,1)} %shard_map.141), channel_id=1, source_target_pairs={{0,4},{4,0},{8,12},{12,8},{16,20},{20,16},{24,28},{28,24},{1,5},{5... | collective-permute-start | bytes 4718600 | tf_op jit(solution)/shard_map/ppermute | solution.py:220
  18.7 23.1 %collective-permute-start.1 = (bf16[512,768]{1,0:T(8,128)(2,1)}, bf16[512,768]{1,0:T(8,128)(2,1)S(1)}, u32[]{:S(2)}, u32[]{:S(2)}) collective-permute-start(bf16[512,768]{1,0:T(8,128)(2,1)} %shard_map.138), channel_id=1, source_target_pairs={{0,8},{4,12},{8,0},{12,4},{16,24},{20,28},{24,16},{28,20},{1,9},{5... | collective-permute-start | bytes 2359304 | tf_op jit(solution)/shard_map/ppermute | solution.py:220
  20.4 3.4 %copy-start.3 = (bf16[4096,1024]{1,0:T(8,128)(2,1)S(1)}, bf16[4096,1024]{1,0:T(8,128)(2,1)}, u32[]{:S(2)}) copy-start(bf16[4096,1024]{1,0:T(8,128)(2,1)} %query_ref.1) | copy-start | bytes 25165828
  23.8 1.6 copy-start.5
  25.4 1.6 copy-start.6
  27.0 11.4 %copy-start.4 = (bf16[4096,512]{1,0:T(8,128)(2,1)S(1)}, bf16[4096,512]{1,0:T(8,128)(2,1)}, u32[]{:S(2)}) copy-start(bf16[4096,512]{1,0:T(8,128)(2,1)} %refs_1_.1) | copy-start | bytes 12582916
  27.0 11.4 %copy-start.7 = (bf16[256,512]{1,0:T(8,128)(2,1)S(1)}, bf16[256,512]{1,0:T(8,128)(2,1)}, u32[]{:S(2)}) copy-start(bf16[256,512]{1,0:T(8,128)(2,1)} %refs_2_.3) | copy-start | bytes 786436
  35.9 5.9 %collective-permute-start = (bf16[32,1024]{1,0:T(8,128)(2,1)S(1)}, bf16[32,1024]{1,0:T(8,128)(2,1)S(1)}, u32[]{:S(2)}, u32[]{:S(2)}) collective-permute-start(bf16[32,1024]{1,0:T(8,128)(2,1)S(1)} %shard_map.136.refs_3_.refs_0_), channel_id=1, source_target_pairs={{0,16},{4,20},{8,24},{12,28},{16,0},{20,4},{24,8},{28,12},{1,17},{... | collective-permute-start | bytes 196616 | tf_op jit(solution)/shard_map/ppermute | solution.py:220
  41.9 5.0 %collective-permute-start.2 = (bf16[64,1024]{1,0:T(8,128)(2,1)S(1)}, bf16[64,1024]{1,0:T(8,128)(2,1)S(1)}, u32[]{:S(2)}, u32[]{:S(2)}) collective-permute-start(bf16[64,1024]{1,0:T(8,128)(2,1)S(1)} %shard_map.139.refs_0_.refs_2_), channel_id=1, source_target_pairs={{0,8},{4,12},{8,0},{12,4},{16,24},{20,28},{24,16},{28,20},{1,9},{5... | collective-permute-start | bytes 393224 | tf_op jit(solution)/shard_map/ppermute | solution.py:220
  46.9 11.4 %collective-permute-start.3 = (bf16[128,1024]{1,0:T(8,128)(2,1)S(1)}, bf16[128,1024]{1,0:T(8,128)(2,1)S(1)}, u32[]{:S(2)}, u32[]{:S(2)}) collective-permute-start(bf16[128,1024]{1,0:T(8,128)(2,1)S(1)} %shard_map.140.refs_0_.refs_2_), channel_id=1, source_target_pairs={{0,4},{4,0},{8,12},{12,8},{16,20},{20,16},{24,28},{28,24},{1,5},{5... | collective-permute-start | bytes 786440 | tf_op jit(solution)/shard_map/ppermute | solution.py:220
  58.4 11.5 %copy-start.12 = (f32[512]{0:T(512)S(1)}, f32[512]{0:T(512)}, u32[]{:S(2)}) copy-start(f32[512]{0:T(512)} %param.24) | copy-start | bytes 6148
  58.8 2.4 %collective-permute-start.5 = (bf16[256,512]{1,0:T(8,128)(2,1)S(1)}, bf16[256,512]{1,0:T(8,128)(2,1)S(1)}, u32[]{:S(2)}, u32[]{:S(2)}) collective-permute-start(bf16[256,512]{1,0:T(8,128)(2,1)S(1)} %shard_map.143.refs_1_.refs_3_), channel_id=1, source_target_pairs={{0,1},{1,0},{2,3},{3,2},{4,5},{5,4},{6,7},{7,6},{8,9},{9,8},{10,11... | collective-permute-start | bytes 786440 | tf_op jit(solution)/shard_map/ppermute | solution.py:233
  59.5 29.3 %collective-permute-start.13 = (bf16[256,1024]{1,0:T(8,128)(2,1)}, bf16[256,1024]{1,0:T(8,128)(2,1)}, u32[]{:S(2)}, u32[]{:S(2)}) collective-permute-start(bf16[256,1024]{1,0:T(8,128)(2,1)} %shard_map.153), channel_id=1, source_target_pairs={{0,4},{4,0},{8,12},{12,8},{16,20},{20,16},{24,28},{28,24},{1,5},{5... | collective-permute-start | bytes 1572872 | tf_op jit(solution)/shard_map/ppermute | solution.py:220
  61.3 0.7 copy-start.8
  62.0 0.9 copy-start.9
  63.5 5.7 %collective-permute-start.6 = (bf16[128,512]{1,0:T(8,128)(2,1)S(1)}, bf16[128,512]{1,0:T(8,128)(2,1)S(1)}, u32[]{:S(2)}, u32[]{:S(2)}) collective-permute-start(bf16[128,512]{1,0:T(8,128)(2,1)S(1)} %get-tuple-element.31.refs_2_), channel_id=1, source_target_pairs={{0,2},{1,3},{2,0},{3,1},{4,6},{5,7},{6,4},{7,5},{8,10},{9,11},{10,... | collective-permute-start | bytes 393224 | tf_op jit(solution)/shard_map/ppermute | solution.py:233
  65.7 26.5 %collective-permute-start.11 = (bf16[512,768]{1,0:T(8,128)(2,1)}, bf16[512,768]{1,0:T(8,128)(2,1)S(1)}, u32[]{:S(2)}, u32[]{:S(2)}) collective-permute-start(bf16[512,768]{1,0:T(8,128)(2,1)} %shard_map.152), channel_id=1, source_target_pairs={{0,8},{4,12},{8,0},{12,4},{16,24},{20,28},{24,16},{28,20},{1,9},{5... | collective-permute-start | bytes 2359304 | tf_op jit(solution)/shard_map/ppermute | solution.py:220
  70.6 10.4 %collective-permute-start.9 = (bf16[128,640]{1,0:T(8,128)(2,1)S(1)}, bf16[128,640]{1,0:T(8,128)(2,1)S(1)}, u32[]{:S(2)}, u32[]{:S(2)}) collective-permute-start(bf16[128,640]{1,0:T(8,128)(2,1)S(1)} %shard_map.146.refs_5_), channel_id=1, source_target_pairs={{0,4},{4,0},{8,12},{12,8},{16,20},{20,16},{24,28},{28,24},{1,5},{5... | collective-permute-start | bytes 491528 | tf_op jit(solution)/shard_map/ppermute | solution.py:220
  71.5 1.5 collective-permute-start.7
  71.5 17.3 %collective-permute-start.8 = (bf16[128,640]{1,0:T(8,128)(2,1)S(1)}, bf16[128,640]{1,0:T(8,128)(2,1)S(1)}, u32[]{:S(2)}, u32[]{:S(2)}) collective-permute-start(bf16[128,640]{1,0:T(8,128)(2,1)S(1)} %shard_map.146.refs_5_), channel_id=1, source_target_pairs={{0,8},{4,12},{8,0},{12,4},{16,24},{20,28},{24,16},{28,20},{1,9},{5... | collective-permute-start | bytes 491528 | tf_op jit(solution)/shard_map/ppermute | solution.py:220
  73.7 0.8 copy-start.10
  74.5 2.0 %copy-start = (bf16[512,3584]{1,0:T(8,128)(2,1)S(1)}, bf16[512,3584]{1,0:T(8,128)(2,1)}, u32[]{:S(2)}) copy-start(bf16[512,3584]{1,0:T(8,128)(2,1)} %refs_2_.5) | copy-start | bytes 11010052
  76.6 2.0 %copy-start.1 = (bf16[512,3584]{1,0:T(8,128)(2,1)S(1)}, bf16[512,3584]{1,0:T(8,128)(2,1)}, u32[]{:S(2)}) copy-start(bf16[512,3584]{1,0:T(8,128)(2,1)} %refs_3_.5) | copy-start | bytes 11010052
  81.0 7.8 %collective-permute-start.12 = (bf16[128,640]{1,0:T(8,128)(2,1)S(1)}, bf16[128,640]{1,0:T(8,128)(2,1)S(1)}, u32[]{:S(2)}, u32[]{:S(2)}) collective-permute-start(bf16[128,640]{1,0:T(8,128)(2,1)S(1)} %shard_map.150.refs_1_.refs_3_), channel_id=1, source_target_pairs={{0,1},{1,0},{2,3},{3,2},{4,5},{5,4},{6,7},{7,6},{8,9},{9,8},{10,11... | collective-permute-start | bytes 491528 | tf_op jit(solution)/shard_map/ppermute | solution.py:233
  90.7 13.7 %collective-permute-start.15 = (bf16[128,2176]{1,0:T(8,128)(2,1)S(1)}, bf16[128,2176]{1,0:T(8,128)(2,1)S(1)}, u32[]{:S(2)}, u32[]{:S(2)}) collective-permute-start(bf16[128,2176]{1,0:T(8,128)(2,1)S(1)} %get-tuple-element.41.refs_8_), channel_id=1, source_target_pairs={{0,8},{4,12},{8,0},{12,4},{16,24},{20,28},{24,16},{28,20},{1,9},{5... | collective-permute-start | bytes 1671176 | tf_op jit(solution)/shard_map/ppermute | solution.py:220
  92.2 1.4 collective-permute-start.10
  94.8 12.1 %collective-permute-start.14 = (bf16[128,1664]{1,0:T(8,128)(2,1)S(1)}, bf16[128,1664]{1,0:T(8,128)(2,1)S(1)}, u32[]{:S(2)}, u32[]{:S(2)}) collective-permute-start(bf16[128,1664]{1,0:T(8,128)(2,1)S(1)} %get-tuple-element.42.refs_2_), channel_id=1, source_target_pairs={{0,4},{4,0},{8,12},{12,8},{16,20},{20,16},{24,28},{28,24},{1,5},{5... | collective-permute-start | bytes 1277960 | tf_op jit(solution)/shard_map/ppermute | solution.py:220
  104.4 54.2 %copy-start.2 = (bf16[3584,512]{1,0:T(8,128)(2,1)S(1)}, bf16[3584,512]{1,0:T(8,128)(2,1)}, u32[]{:S(2)}) copy-start(bf16[3584,512]{1,0:T(8,128)(2,1)} %refs_3_.7) | copy-start | bytes 11010052
  104.5 19.3 %collective-permute-start.17 = (bf16[64,2176]{1,0:T(8,128)(2,1)S(1)}, bf16[64,2176]{1,0:T(8,128)(2,1)S(1)}, u32[]{:S(2)}, u32[]{:S(2)}) collective-permute-start(bf16[64,2176]{1,0:T(8,128)(2,1)S(1)} %get-tuple-element.45.refs_2_), channel_id=1, source_target_pairs={{0,16},{4,20},{8,24},{12,28},{16,0},{20,4},{24,8},{28,12},{1,17},{... | collective-permute-start | bytes 835592 | tf_op jit(solution)/shard_map/ppermute | solution.py:220
  107.0 24.1 %collective-permute-start.16 = (bf16[64,1664]{1,0:T(8,128)(2,1)S(1)}, bf16[64,1664]{1,0:T(8,128)(2,1)S(1)}, u32[]{:S(2)}, u32[]{:S(2)}) collective-permute-start(bf16[64,1664]{1,0:T(8,128)(2,1)S(1)} %get-tuple-element.46.refs_2_), channel_id=1, source_target_pairs={{0,16},{4,20},{8,24},{12,28},{16,0},{20,4},{24,8},{28,12},{1,17},{... | collective-permute-start | bytes 638984 | tf_op jit(solution)/shard_map/ppermute | solution.py:220
  124.4 8.5 %collective-permute-start.19 = (bf16[64,1024]{1,0:T(8,128)(2,1)S(1)}, bf16[64,1024]{1,0:T(8,128)(2,1)S(1)}, u32[]{:S(2)}, u32[]{:S(2)}) collective-permute-start(bf16[64,1024]{1,0:T(8,128)(2,1)S(1)} %get-tuple-element.49.refs_2_.refs_0_), channel_id=1, source_target_pairs={{0,16},{4,20},{8,24},{12,28},{16,0},{20,4},{24,8},{28,12},{1,17},{... | collective-permute-start | bytes 393224 | tf_op jit(solution)/shard_map/ppermute | solution.py:220
  132.9 9.4 %collective-permute-start.21 = (bf16[128,1024]{1,0:T(8,128)(2,1)S(1)}, bf16[128,1024]{1,0:T(8,128)(2,1)S(1)}, u32[]{:S(2)}, u32[]{:S(2)}) collective-permute-start(bf16[128,1024]{1,0:T(8,128)(2,1)S(1)} %shard_map.160.refs_2_.refs_0_), channel_id=1, source_target_pairs={{0,8},{4,12},{8,0},{12,4},{16,24},{20,28},{24,16},{28,20},{1,9},{5... | collective-permute-start | bytes 786440 | tf_op jit(solution)/shard_map/ppermute | solution.py:220
  133.4 7.8 %collective-permute-start.18 = (bf16[64,768]{1,0:T(8,128)(2,1)S(1)}, bf16[64,768]{1,0:T(8,128)(2,1)S(1)}, u32[]{:S(2)}, u32[]{:S(2)}) collective-permute-start(bf16[64,768]{1,0:T(8,128)(2,1)S(1)} %get-tuple-element.50.refs_2_.refs_0_), channel_id=1, source_target_pairs={{0,16},{4,20},{8,24},{12,28},{16,0},{20,4},{24,8},{28,12},{1,17},{... | collective-permute-start | bytes 294920 | tf_op jit(solution)/shard_map/ppermute | solution.py:220
  141.3 7.9 %collective-permute-start.20 = (bf16[128,768]{1,0:T(8,128)(2,1)S(1)}, bf16[128,768]{1,0:T(8,128)(2,1)S(1)}, u32[]{:S(2)}, u32[]{:S(2)}) collective-permute-start(bf16[128,768]{1,0:T(8,128)(2,1)S(1)} %shard_map.161.refs_2_.refs_0_), channel_id=1, source_target_pairs={{0,4},{4,0},{8,12},{12,8},{16,20},{20,16},{24,28},{28,24},{1,5},{5... | collective-permute-start | bytes 589832 | tf_op jit(solution)/shard_map/ppermute | solution.py:220
  142.4 16.2 %collective-permute-start.23 = (bf16[256,1024]{1,0:T(8,128)(2,1)S(1)}, bf16[256,1024]{1,0:T(8,128)(2,1)S(1)}, u32[]{:S(2)}, u32[]{:S(2)}) collective-permute-start(bf16[256,1024]{1,0:T(8,128)(2,1)S(1)} %shard_map.162.refs_2_.refs_1_), channel_id=1, source_target_pairs={{0,4},{4,0},{8,12},{12,8},{16,20},{20,16},{24,28},{28,24},{1,5},{5... | collective-permute-start | bytes 1572872 | tf_op jit(solution)/shard_map/ppermute | solution.py:220
  149.2 10.6 %collective-permute-start.22 = (bf16[256,768]{1,0:T(8,128)(2,1)S(1)}, bf16[256,768]{1,0:T(8,128)(2,1)S(1)}, u32[]{:S(2)}, u32[]{:S(2)}) collective-permute-start(bf16[256,768]{1,0:T(8,128)(2,1)S(1)} %shard_map.163.refs_4_.refs_1_), channel_id=1, source_target_pairs={{0,8},{4,12},{8,0},{12,4},{16,24},{20,28},{24,16},{28,20},{1,9},{5... | collective-permute-start | bytes 1179656 | tf_op jit(solution)/shard_map/ppermute | solution.py:220
  161.7 1.4 collective-permute-start.24
  163.2 4.3 %collective-permute-start.25 = (bf16[64,512]{1,0:T(8,128)(2,1)S(1)}, bf16[64,512]{1,0:T(8,128)(2,1)S(1)}, u32[]{:S(2)}, u32[]{:S(2)}) collective-permute-start(bf16[64,512]{1,0:T(8,128)(2,1)S(1)} %dynamic-slice_convert_fusion), channel_id=1, source_target_pairs={{0,2},{1,3},{2,0},{3,1},{4,6},{5,7},{6,4},{7,5},{8,10},{9,11},{10,... | collective-permute-start | bytes 196616 | tf_op jit(solution)/shard_map/ppermute | solution.py:233
